TPU v7x, 256 devices: a whole 4x4x8 slice. The times are simulated.
256 devices in a mesh: gy: 8 (over z_hi, core), gx: 32 (over y, z_lo, x).
Axes of the slice: x: 4, y: 4, z: 8 (z_hi: 4, z_lo: 2; z = z_hi * 2 + z_lo), core: 2. Of those that a mesh axis runs over, the one named last changes fastest.
Arguments:
- nest_adjoint: float32 [50, 192, 4096], P(None, 'gy', 'gx'), may hold values from -6 to 6
- nest_kappa: float32 [2, 50, 192, 4096], P(None, None, 'gy', 'gx'), may hold values from 0.1 to 10
- nest_nu: float32 [50, 192, 4096], P(None, 'gy', 'gx'), may hold values from 0.02 to 0.24
- land_mask: int32 [192, 4096], P('gy', 'gx'), may hold values 0 or 1
- parent_adjoint: float32 [50, 384, 4096], P(None, 'gy', 'gx'), may hold values from -6 to 6
- parent_kappa: float32 [2, 50, 384, 4096], P(None, None, 'gy', 'gx'), may hold values from 0.1 to 10
- parent_traj: float32 [2, 50, 384, 4096], P(None, None, 'gy', 'gx'), may hold values from -6 to 6
- offset_row: int32 [1], replicated, may hold values from 193 to 240
- offset_col: int32 [1], replicated, may hold values from 2049 to 2176
Outputs:
- nest_result: float32 [50, 192, 4096], P(None, 'gy', 'gx')
- parent_result: float32 [50, 384, 4096], P(None, 'gy', 'gx')
- side_weights: float32 [2, 50, 2, 64], replicated
- side_gradients: float32 [2, 50, 2, 64], replicated
All inputs are finite; a program needn't handle non-finite values. No bound on the sum of `land_mask` on one device may be relied on, other than what follows from the above.
Results may differ from a plain program's by a relative error of at most 0.0001.
Values sent between devices are 32-bit elements; how exact they have to be, the bound alone decides.
No kernel may reach another device: no remote copies, remote signals or barrier semaphores. Data moves between devices by JAX's collectives and lax.ppermute only.
A program may use at most 128 MiB of HBM per device.

v0:
```python
import jax
import jax.numpy as jnp
from jax import lax
from jax.experimental import pallas as pl
from jax.experimental.pallas import tpu as pltpu
from jax.sharding import PartitionSpec as P

R = 3
K = 50
NR = 24
PR = 48
L = 128
GY = 8
GX = 32
SR = 64
ROW0 = 192
COL0 = 2048
SOUTH = 4
WEST = 16
SPAN = 1366
F32 = jnp.float32
VM = pl.BlockSpec(memory_space=pltpu.VMEM)
SM = pl.BlockSpec(memory_space=pltpu.SMEM)
PARAMS = pltpu.CompilerParams(vmem_limit_bytes=48 * 1024 * 1024)


def exact(left, right):
    return lax.dot_general(
        left, right, (((1,), (0,)), ((), ())), precision=lax.Precision.HIGHEST, preferred_element_type=F32
    )


def exact_t(left, right):
    return lax.dot_general(
        left, right, (((1,), (1,)), ((), ())), precision=lax.Precision.HIGHEST, preferred_element_type=F32
    )


def iota(shape, dim):
    return lax.broadcasted_iota(jnp.int32, shape, dim)


def wide(col, rows):
    return jnp.broadcast_to(col, (rows, L))


def side_lane(x, ox):
    west = ox - 1 - L * x
    east = ox + SPAN - L * x
    is_west = (west >= 0) & (west < L)
    is_east = (east >= 0) & (east < L)
    return is_west, is_east, jnp.where(is_west, west, east)


def ring_row(g, oy):
    row = jnp.where(g == SOUTH, oy - 1, oy + SR) - PR * g
    return (row >= 0) & (row < PR) & (g >= SOUTH) & (g < GY - 1), row


def pack_kernel(info, a, nu, mask, traj, v_top, v_bot, v_left, v_right, pay, buf):
    g, x, oy, ox = info[0], info[1], info[2], info[3]
    m = mask[...].astype(F32)
    lane = iota((NR, L), 1)
    acc_l = jnp.zeros((NR, L), F32)
    acc_r = jnp.zeros((NR, L), F32)
    for k in range(K):
        v = nu[k] * m * a[k]
        v_top[pl.ds(k, 1), :] = v[0:1]
        v_bot[pl.ds(k, 1), :] = v[NR - 1 : NR]
        acc_l = jnp.where(lane == k, pltpu.roll(v, k, 1) if k else v, acc_l)
        acc_r = jnp.where(lane == k, pltpu.roll(v, k + 1, 1), acc_r)
    v_left[...] = acc_l
    v_right[...] = acc_r

    pay[...] = jnp.zeros(pay.shape, F32)
    row_ok, row = ring_row(g, oy)

    @pl.when(row_ok)
    def _():
        for i, s in enumerate((1, 0)):
            for k in range(K):
                pay[pl.ds(K * i + k, 1), :] = jax.nn.sigmoid(traj[s, k, pl.ds(row, 1), :])

    is_west, is_east, spot = side_lane(x, ox)

    @pl.when((is_west | is_east) & (g >= SOUTH) & (g < GY - 1))
    def _():
        plane = iota((PR, L), 1)
        acc = jnp.zeros((PR, L), F32)
        for i, s in enumerate((1, 0)):
            for k in range(K):
                to = 64 * i + k
                acc = jnp.where(plane == to, pltpu.roll(traj[s, k], lax.rem(to - spot + L, L), 1), acc)
        used = (plane < K) | ((plane >= 64) & (plane < 64 + K))
        buf[...] = jnp.zeros(buf.shape, F32)
        start = PR * g - oy + SR
        weights = jnp.where(used, jax.nn.sigmoid(acc), 0.0)
        for r in range(PR):
            buf[pl.ds(start + r, 1), :] = weights[r : r + 1]
        pay[104:168, :] = buf[SR : 2 * SR, :]


def nest_kernel(
    info, a, nu, mask, kappa, r0, r1, r2, r3, r4, r5, r6, we, h_up, h_down, h_left, h_right,
    a_out, v_top, v_bot, v_left, v_right, grad, side,
    e_s, y_s, w_s, up_s, down_s, g_s,
):
    g, x, oy, ox = info[0], info[1], info[2], info[3]
    sig = ox - COL0
    t = lax.rem(x, 3)
    rows = 104
    own = r0[0:rows, :] + r1[0:rows, :] + r2[0:rows, :]
    nxt = r3[0:rows, :] + r4[0:rows, :] + r5[0:rows, :]
    nxt2 = r6[0:rows, :]
    wl = iota((rows, L), 1)
    back = L - sig
    shift = lax.rem(back + L, L)
    panel = jnp.where(wl < back, pltpu.roll(own, shift, 1), pltpu.roll(nxt, shift, 1))
    pi, pc = iota((L, L), 0), iota((L, L), 1)
    spread = ((3 * pi <= L * t + pc) & (L * t + pc < 3 * pi + 3)).astype(F32)
    c_all = x * L + wl
    w_s[...] = jnp.where((c_all > 0) & (c_all < GX * L - 1), exact(panel, spread), 0.0)

    er, el = iota((8, L), 0), iota((8, L), 1)
    left_at = jnp.where(t == 0, -1, jnp.where(t == 1, 42, 85)) + sig
    right_at = jnp.where(t == 0, 42, jnp.where(t == 1, 85, L)) + sig
    want = jnp.where(er == 0, left_at, jnp.where(er == 1, right_at, -1))
    ends = (
        exact_t((el == want).astype(F32), own)
        + exact_t((el + L == want).astype(F32), nxt)
        + exact_t((el + 2 * L == want).astype(F32), nxt2)
    )

    row24, lane24 = iota((NR, L), 0), iota((NR, L), 1)
    m_row = (((row24 == 0) & (g == 0)) | ((row24 == NR - 1) & (g == GY - 1))).astype(F32)
    m_lane = (((lane24 == 0) & (x == 0)) | ((lane24 == L - 1) & (x == GX - 1))).astype(F32)
    ends_l = jnp.concatenate([ends[0:1], jnp.zeros((1, 24), F32)], 1)
    ends_r = jnp.concatenate([ends[1:2], jnp.zeros((1, 24), F32)], 1)
    hl = h_left[...] * (1.0 - m_row * wide(ends_l, NR))
    hr = h_right[...] * (1.0 - m_row * wide(ends_r, NR))

    panel_we = we[...]
    qr, qj = iota((NR, SR), 0), iota((NR, SR), 1)
    base = 3 * (qj - 8 * g)
    w_we = exact(((base <= qr) & (qr < base + 3)).astype(F32), panel_we)
    flip = jnp.concatenate([panel_we, jnp.zeros((SR, L), F32)], 0).T
    edge = ((pc == 0) & (x == 0)) | ((pc == L - 1) & (x == GX - 1))
    up_s[...] = h_up[...] * (1.0 - exact(flip, (edge & (pi == 8 * g - 1)).astype(F32))[0:K])
    down_s[...] = h_down[...] * (1.0 - exact(flip, (edge & (pi == 8 * g + 8)).astype(F32))[0:K])

    m = mask[...].astype(F32)
    one = jnp.ones((NR, L), F32)
    zero = jnp.zeros((NR, L), F32)
    c_prev, e_prev, y_prev = zero, zero, zero
    top = g == 0
    is31 = (x == GX - 1).astype(jnp.int32)
    for k in range(K):
        w_row = w_s[pl.ds(k, 1), :]
        raw = a[k]
        g_s[pl.ds(k, 1), :] = w_row * jnp.where(top, raw[0:1], raw[NR - 1 : NR])
        now = raw * (one - (m_row * wide(w_row, NR) + m_lane * wide(w_we[:, k : k + 1], NR)))
        v = nu[k] * m * now
        above = jnp.where(row24 == 0, wide(up_s[pl.ds(k, 1), :], NR), pltpu.roll(v, 1, 0))
        below = jnp.where(row24 == NR - 1, wide(down_s[pl.ds(k, 1), :], NR), pltpu.roll(v, NR - 1, 0))
        left = jnp.where(lane24 == 0, wide(hl[:, k : k + 1], NR), pltpu.roll(v, 1, 1))
        right = jnp.where(lane24 == L - 1, wide(hr[:, k : k + 1], NR), pltpu.roll(v, L - 1, 1))
        b = m * (now + (above + below + left + right - 4.0 * v))
        c = kappa[1, k]
        r = 1.0 / (1.0 + c + c_prev * (1.0 - e_prev))
        e = c * r
        y = (b + c_prev * y_prev) * r
        e_s[k] = e
        y_s[k] = y
        c_prev, e_prev, y_prev = c, e, y
    sol = zero
    acc_l, acc_r = zero, zero
    for k in range(K - 1, -1, -1):
        sol = y_s[k] + e_s[k] * sol if k < K - 1 else y_s[k]
        y_s[k] = sol
        w_row = w_s[pl.ds(K + k, 1), :]
        g_s[pl.ds(K + k, 1), :] = w_row * jnp.where(top, sol[0:1], sol[NR - 1 : NR])
        now = sol * (one - (m_row * wide(w_row, NR) + m_lane * wide(w_we[:, 64 + k : 65 + k], NR)))
        a_out[k] = now
        v = nu[k] * m * now
        v_top[pl.ds(k, 1), :] = v[0:1]
        v_bot[pl.ds(k, 1), :] = v[NR - 1 : NR]
        acc_l = jnp.where(lane24 == k, pltpu.roll(v, k, 1) if k else v, acc_l)
        acc_r = jnp.where(lane24 == k, pltpu.roll(v, k + 1, 1), acc_r)
    v_left[...] = acc_l
    v_right[...] = acc_r
    for i in range(2 * K, rows):
        g_s[pl.ds(i, 1), :] = jnp.zeros((1, L), F32)
    gather = ((3 * pc <= L * t + pi) & (L * t + pi < 3 * pc + 3)).astype(F32)
    grad[...] = exact(g_s[...], gather)

    side[...] = jnp.zeros(side.shape, F32)

    @pl.when((x == 0) | (x == GX - 1))
    def _():
        acc = zero
        for k in range(K):
            acc = jnp.where(lane24 == k, pltpu.roll(a[k], lax.rem(k + is31, L), 1), acc)
            acc = jnp.where(lane24 == 64 + k, pltpu.roll(y_s[k], lax.rem(64 + k + is31, L), 1), acc)
        terms = w_we * acc
        sj, sr = iota((8, NR), 0), iota((8, NR), 1)
        side[0:8, :] = exact(((3 * sj <= sr) & (sr < 3 * sj + 3)).astype(F32), terms)
        side[8:16, :] = we[pl.ds(pl.multiple_of(8 * g, 8), 8), :]


def row_kernel(info, r0, r1, r2, r3, r4, r5, out):
    sig = info[3] - COL0
    own = r0[...] + r1[...] + r2[...]
    prev = r3[...] + r4[...] + r5[...]
    shift = lax.rem(sig, L)
    out[...] = jnp.where(iota(own.shape, 1) >= sig, pltpu.roll(own, shift, 1), pltpu.roll(prev, shift, 1))


def last_kernel(
    info, a, nu, mask, kappa, h_up, h_down, h_left, h_right, q, pkappa, g_own, g_fwd, sides,
    a_out, q_out, s_w, s_g,
    e_s, pe_s, panel_s, local_s,
):
    g, x, oy, ox = info[0], info[1], info[2], info[3]
    m = mask[...].astype(F32)
    row24, lane24 = iota((NR, L), 0), iota((NR, L), 1)
    hl, hr = h_left[...], h_right[...]
    zero = jnp.zeros((NR, L), F32)
    c_prev, e_prev, y_prev = zero, zero, zero
    for k in range(K):
        now = a[k]
        v = nu[k] * m * now
        above = jnp.where(row24 == 0, wide(h_up[pl.ds(k, 1), :], NR), pltpu.roll(v, 1, 0))
        below = jnp.where(row24 == NR - 1, wide(h_down[pl.ds(k, 1), :], NR), pltpu.roll(v, NR - 1, 0))
        left = jnp.where(lane24 == 0, wide(hl[:, k : k + 1], NR), pltpu.roll(v, 1, 1))
        right = jnp.where(lane24 == L - 1, wide(hr[:, k : k + 1], NR), pltpu.roll(v, L - 1, 1))
        b = m * (now + (above + below + left + right - 4.0 * v))
        c = kappa[0, k]
        r = 1.0 / (1.0 + c + c_prev * (1.0 - e_prev))
        e = c * r
        y = (b + c_prev * y_prev) * r
        e_s[k] = e
        a_out[k] = y
        c_prev, e_prev, y_prev = c, e, y
    sol = y_prev
    for k in range(K - 2, -1, -1):
        sol = a_out[k] + e_s[k] * sol
        a_out[k] = sol

    def panels(first):
        return jnp.concatenate([sides[i, 16 * e + first : 16 * e + first + 8, :] for e in (0, 1) for i in range(GY)], 0)

    grads = panels(0)
    flip_g = grads.T
    flip_w = panels(8).T
    for i, s in enumerate((1, 0)):
        for e in (0, 1):
            s_g[s, :, e, :] = flip_g[64 * i : 64 * i + K, SR * e : SR * e + SR]
            s_w[s, :, e, :] = flip_w[64 * i : 64 * i + K, SR * e : SR * e + SR]

    q_out[...] = q[...]
    row_ok, row = ring_row(g, oy)
    is_west, is_east, spot = side_lane(x, ox)
    side_ok = (is_west | is_east) & (g >= SOUTH) & (g < GY - 1)

    @pl.when(side_ok)
    def _():
        panel_s[...] = jnp.zeros(panel_s.shape, F32)
        panel_s[SR : 2 * SR, :] = jnp.where(is_west, grads[0:SR], grads[SR : 2 * SR])
        start = PR * g - oy + SR
        for r in range(PR):
            local_s[pl.ds(r, 1), :] = panel_s[pl.ds(start + r, 1), :]

    lane48 = iota((PR, L), 1)
    for i, s in enumerate((1, 0)):

        @pl.when(row_ok)
        def _():
            for k in range(K):
                at = pl.ds(K * i + k, 1)
                q_out[k, pl.ds(row, 1), :] = q_out[k, pl.ds(row, 1), :] + (g_own[at, :] + g_fwd[at, :])

        @pl.when(side_ok)
        def _():
            for k in range(K):
                at = 64 * i + k
                q_out[k] = q_out[k] + jnp.where(lane48 == spot, wide(local_s[:, at : at + 1], PR), 0.0)

        zero = jnp.zeros((PR, L), F32)
        c_prev, e_prev, y_prev = zero, zero, zero
        for k in range(K):
            c = pkappa[s, k]
            r = 1.0 / (1.0 + c + c_prev * (1.0 - e_prev))
            e = c * r
            y = (q_out[k] + c_prev * y_prev) * r
            pe_s[k] = e
            q_out[k] = y
            c_prev, e_prev, y_prev = c, e, y
        sol = y_prev
        for k in range(K - 2, -1, -1):
            sol = q_out[k] + pe_s[k] * sol
            q_out[k] = sol


def shape(*dims):
    return jax.ShapeDtypeStruct(dims, F32)


def at(g, x):
    return g * GX + x


def moved(value, pairs):
    return lax.ppermute(value, ("gy", "gx"), pairs)


def shifted(value, axis, count, step):
    pairs = [(i, i + step) for i in range(count) if 0 <= i + step < count]
    return lax.ppermute(value, axis, pairs)


def halos(v_top, v_bot, v_left, v_right):
    return (
        shifted(v_bot, "gy", GY, 1),
        shifted(v_top, "gy", GY, -1),
        shifted(v_right, "gx", GX, 1),
        shifted(v_left, "gx", GX, -1),
    )


def on_device(nest_adjoint, nest_kappa, nest_nu, land_mask, parent_adjoint, parent_kappa, parent_traj, offset_row, offset_col):
    g = lax.axis_index("gy")
    x = lax.axis_index("gx")
    info = jnp.stack([g.astype(jnp.int32), x.astype(jnp.int32), offset_row[0], offset_col[0]])
    v_top, v_bot, v_left, v_right, pay = pl.pallas_call(
        pack_kernel,
        out_shape=(shape(K, L), shape(K, L), shape(NR, L), shape(NR, L), shape(168, L)),
        in_specs=[SM, VM, VM, VM, VM],
        out_specs=(VM,) * 5,
        scratch_shapes=[pltpu.VMEM((256, L), F32)],
        compiler_params=PARAMS,
        name="pack",
    )(info, nest_adjoint, nest_nu, land_mask, parent_traj)

    ring = range(WEST, WEST + 12)
    north = moved(pay, [(at(6, p), at(5, p)) for p in ring])
    h_up, h_down, h_left, h_right = halos(v_top, v_bot, v_left, v_right)
    pay = pay + north
    parts = []
    for t in (0, 1, 2, -3, -2, -1, -4):
        pairs = []
        for p in ring:
            j = 3 * (p - WEST) + t
            if 0 <= j < GX:
                pairs += [(at(4, p), at(0, j)), (at(5, p), at(7, j))]
        parts.append(moved(pay, pairs))
    we = parts[0][104:168]
    for part in parts[1:6]:
        we = we + part[104:168]
    for pairs in ([(0, 7), (7, 0)], [(0, 2), (7, 5)], [(0, 1), (2, 3), (5, 4), (7, 6)]):
        we = we + moved(we, [(at(i, e), at(j, e)) for i, j in pairs for e in (0, GX - 1)])

    state, v_top, v_bot, v_left, v_right, grad, side = pl.pallas_call(
        nest_kernel,
        out_shape=(
            shape(K, NR, L), shape(K, L), shape(K, L), shape(NR, L), shape(NR, L), shape(104, L), shape(16, L)
        ),
        in_specs=[SM] + [VM] * 16,
        out_specs=(VM,) * 7,
        scratch_shapes=[
            pltpu.VMEM((K, NR, L), F32), pltpu.VMEM((K, NR, L), F32), pltpu.VMEM((104, L), F32),
            pltpu.VMEM((K, L), F32), pltpu.VMEM((K, L), F32), pltpu.VMEM((104, L), F32),
        ],
        compiler_params=PARAMS,
        name="nest",
    )(info, nest_adjoint, nest_nu, land_mask, nest_kappa, *parts, we, h_up, h_down, h_left, h_right)

    h_up, h_down, h_left, h_right = halos(v_top, v_bot, v_left, v_right)
    parts = []
    for t in (0, 1, 2, -3, -2, -1):
        pairs = []
        for p in ring:
            j = 3 * (p - WEST) + t
            if 0 <= j < GX:
                pairs += [(at(0, j), at(4, p)), (at(7, j), at(5, p))]
        parts.append(moved(grad, pairs))
    g_own = pl.pallas_call(
        row_kernel,
        out_shape=shape(104, L),
        in_specs=[SM] + [VM] * 6,
        out_specs=VM,
        compiler_params=PARAMS,
        name="row",
    )(info, *parts)
    g_fwd = moved(g_own, [(at(5, p), at(6, p)) for p in ring])
    wide_side = lax.all_to_all(jnp.broadcast_to(side[None], (GX, 16, L)), "gx", 0, 0)
    pair = jnp.concatenate([wide_side[0], wide_side[GX - 1]], 0)
    sides = lax.all_to_all(jnp.broadcast_to(pair[None], (GY, 32, L)), "gy", 0, 0)

    return pl.pallas_call(
        last_kernel,
        out_shape=(shape(K, NR, L), shape(K, PR, L), shape(2, K, 2, SR), shape(2, K, 2, SR)),
        in_specs=[SM] + [VM] * 13,
        out_specs=(VM,) * 4,
        scratch_shapes=[
            pltpu.VMEM((K, NR, L), F32), pltpu.VMEM((K, PR, L), F32), pltpu.VMEM((256, L), F32), pltpu.VMEM((PR, L), F32),
        ],
        compiler_params=PARAMS,
        name="last",
    )(
        info, state, nest_nu, land_mask, nest_kappa, h_up, h_down, h_left, h_right,
        parent_adjoint, parent_kappa, g_own, g_fwd, sides,
    )


def solution(mesh):
    in_specs = (
        P(None, "gy", "gx"),
        P(None, None, "gy", "gx"),
        P(None, "gy", "gx"),
        P("gy", "gx"),
        P(None, "gy", "gx"),
        P(None, None, "gy", "gx"),
        P(None, None, "gy", "gx"),
        P(),
        P(),
    )
    out_specs = (P(None, "gy", "gx"), P(None, "gy", "gx"), P(), P())
    return jax.shard_map(on_device, mesh=mesh, in_specs=in_specs, out_specs=out_specs, check_vma=False)
```

profile of v0, /device:TPU:144, one launch (start us, length us, event | category | flops | bytes accessed | tf_op | source)
XLA Modules:
  0.0 137.0 jit_solution(14112889510487305872)
XLA Ops:
  2.0 1.1 copy-done
  3.1 1.7 %copy-done.3 = f32[2,50,48,128]{3,2,1,0:T(8,128)S(1)} copy-done((f32[2,50,48,128]{3,2,1,0:T(8,128)S(1)}, f32[2,50,48,128]{3,2,1,0:T(8,128)}, u32[]{:S(2)}) %copy-start.3) | copy-done | bytes 2457624
  4.8 1.1 copy-done.4
  5.8 0.7 copy-done.8
  6.6 1.8 %pack.1 = (f32[50,128]{1,0:T(8,128)S(1)}, f32[50,128]{1,0:T(8,128)S(1)}, f32[24,128]{1,0:T(8,128)S(1)}, f32[24,128]{1,0:T(8,128)S(1)}, f32[168,128]{1,0:T(8,128)S(1)}) custom-call(s32[4]{0:T(128)S(1)} %pad_add_fusion.info, f32[50,24,128]{2,1,0:T(8,128)S(1)} %copy-done.4, f32[50,24,128]{2,1,0:T(8,128)S(1)} %copy-done, s32[24,128]{1,0:T(8,128)S(1)} %copy-done.8, ...), custom_call_target="tpu_custom_call" | custom-call | tf_op jit(solution)/shard_map/pack/pallas_call | solution.py:334
  8.3 0.7 collective-permute-start
  11.1 2.7 %collective-permute-start.3 = (f32[168,128]{1,0:T(8,128)S(1)}, f32[168,128]{1,0:T(8,128)S(1)}, u32[]{:S(2)}, u32[]{:S(2)}) collective-permute-start(f32[168,128]{1,0:T(8,128)S(1)} %add.27), channel_id=1, source_target_pairs={{144,2},{176,226},{145,5},{177,229},{146,8},{178,232},{147,11},{17... | collective-permute-start | bytes 258056 | tf_op jit(solution)/shard_map/ppermute | solution.py:313
  13.7 1.3 collective-permute-start.2
  15.1 1.3 collective-permute-start.1
  16.4 0.7 collective-permute-done.2.r1
  17.1 1.3 collective-permute-done.1.r0
  21.2 6.4 %collective-permute-start.11 = (f32[50,128]{1,0:T(8,128)S(1)}, f32[50,128]{1,0:T(8,128)S(1)}, u32[]{:S(2)}, u32[]{:S(2)}) collective-permute-start(f32[50,128]{1,0:T(8,128)S(1)} %get-tuple-element.17), channel_id=1, source_target_pairs={{0,32},{32,64},{64,96},{96,128},{128,160},{160,192},{192,224},{1,3... | collective-permute-start | bytes 76808 | tf_op jit(solution)/shard_map/ppermute | solution.py:318
  27.6 1.9 %collective-permute-start.12 = (f32[50,128]{1,0:T(8,128)S(1)}, f32[50,128]{1,0:T(8,128)S(1)}, u32[]{:S(2)}, u32[]{:S(2)}) collective-permute-start(f32[50,128]{1,0:T(8,128)S(1)} %get-tuple-element.18), channel_id=1, source_target_pairs={{32,0},{64,32},{96,64},{128,96},{160,128},{192,160},{224,192},{33,... | collective-permute-start | bytes 76808 | tf_op jit(solution)/shard_map/ppermute | solution.py:318
  29.5 4.9 %collective-permute-start.13 = (f32[24,128]{1,0:T(8,128)S(1)}, f32[24,128]{1,0:T(8,128)S(1)}, u32[]{:S(2)}, u32[]{:S(2)}) collective-permute-start(f32[24,128]{1,0:T(8,128)S(1)} %get-tuple-element.19), channel_id=1, source_target_pairs={{0,1},{1,2},{2,3},{3,4},{4,5},{5,6},{6,7},{7,8},{8,9},{9,10},{10,1... | collective-permute-start | bytes 36872 | tf_op jit(solution)/shard_map/ppermute | solution.py:318
  34.5 3.9 %collective-permute-start.14 = (f32[24,128]{1,0:T(8,128)S(1)}, f32[24,128]{1,0:T(8,128)S(1)}, u32[]{:S(2)}, u32[]{:S(2)}) collective-permute-start(f32[24,128]{1,0:T(8,128)S(1)} %get-tuple-element.20), channel_id=1, source_target_pairs={{1,0},{2,1},{3,2},{4,3},{5,4},{6,5},{7,6},{8,7},{9,8},{10,9},{11,1... | collective-permute-start | bytes 36872 | tf_op jit(solution)/shard_map/ppermute | solution.py:318
  38.4 6.3 %collective-permute-done.14.h_right = f32[24,128]{1,0:T(8,128)S(1)} collective-permute-done((f32[24,128]{1,0:T(8,128)S(1)}, f32[24,128]{1,0:T(8,128)S(1)}, u32[]{:S(2)}, u32[]{:S(2)}) %collective-permute-start.14) | collective-permute-done | bytes 12320 | tf_op jit(solution)/shard_map/ppermute | solution.py:318
  44.7 6.8 %nest.1 = (f32[50,24,128]{2,1,0:T(8,128)S(1)}, f32[50,128]{1,0:T(8,128)S(1)}, f32[50,128]{1,0:T(8,128)S(1)}, f32[24,128]{1,0:T(8,128)S(1)}, f32[24,128]{1,0:T(8,...) custom-call(s32[4]{0:T(128)S(1)} %pad_add_fusion.info, f32[50,24,128]{2,1,0:T(8,128)S(1)} %copy-done.4, ...), custom_call_target="tpu_custom_call" | custom-call | tf_op jit(solution)/shard_map/nest/pallas_call | solution.py:362
  51.5 0.8 copy-done.6
  52.4 23.1 %all_to_all.10 = f32[32,16,128]{2,1,0:T(8,128)S(1)} all-to-all(f32[32,16,128]{2,1,0:T(8,128)S(1)} %broadcast_in_dim.4), channel_id=1, replica_groups=mesh['gy'=8,'gx'=32] {'gx'}, dimensions={0} | all-to-all | bytes 524288 | tf_op jit(solution)/shard_map/all_to_all | solution.py:395
  75.5 0.7 broadcast_in_dim.5
  76.1 7.4 %all-to-all-start.1 = ((f32[8,32,128]{2,1,0:T(8,128)}), f32[8,32,128]{2,1,0:T(8,128)S(1)}, u32[]{:S(2)}, u32[]{:S(2)}) async-start(f32[8,32,128]{2,1,0:T(8,128)} %broadcast_in_dim.5), calls=%async_computation.1 | async-start | bytes 262144 | tf_op jit(solution)/shard_map/all_to_all | solution.py:397
  85.5 1.3 collective-permute-start.21
  86.8 1.3 collective-permute-start.20
  88.1 1.3 collective-permute-start.19
  89.4 11.2 %collective-permute-done.21.r2 = f32[104,128]{1,0:T(8,128)S(1)} collective-permute-done((f32[104,128]{1,0:T(8,128)S(1)}, f32[104,128]{1,0:T(8,128)S(1)}, u32[]{:S(2)}, u32[]{:S(2)}) %collective-permute-start.21) | collective-permute-done | bytes 53280 | tf_op jit(solution)/shard_map/ppermute | solution.py:313
  102.6 1.9 %collective-permute-start.15 = (f32[50,128]{1,0:T(8,128)S(1)}, f32[50,128]{1,0:T(8,128)S(1)}, u32[]{:S(2)}, u32[]{:S(2)}) collective-permute-start(f32[50,128]{1,0:T(8,128)S(1)} %get-tuple-element.22), channel_id=1, source_target_pairs={{0,32},{32,64},{64,96},{96,128},{128,160},{160,192},{192,224},{1,3... | collective-permute-start | bytes 76808 | tf_op jit(solution)/shard_map/ppermute | solution.py:318
  104.5 5.8 %collective-permute-start.16 = (f32[50,128]{1,0:T(8,128)S(1)}, f32[50,128]{1,0:T(8,128)S(1)}, u32[]{:S(2)}, u32[]{:S(2)}) collective-permute-start(f32[50,128]{1,0:T(8,128)S(1)} %get-tuple-element.23), channel_id=1, source_target_pairs={{32,0},{64,32},{96,64},{128,96},{160,128},{192,160},{224,192},{33,... | collective-permute-start | bytes 76808 | tf_op jit(solution)/shard_map/ppermute | solution.py:318
  110.3 13.8 %collective-permute-start.17 = (f32[24,128]{1,0:T(8,128)S(1)}, f32[24,128]{1,0:T(8,128)S(1)}, u32[]{:S(2)}, u32[]{:S(2)}) collective-permute-start(f32[24,128]{1,0:T(8,128)S(1)} %get-tuple-element.24), channel_id=1, source_target_pairs={{0,1},{1,2},{2,3},{3,4},{4,5},{5,6},{6,7},{7,8},{8,9},{9,10},{10,1... | collective-permute-start | bytes 36872 | tf_op jit(solution)/shard_map/ppermute | solution.py:318
  124.1 1.9 %collective-permute-start.18 = (f32[24,128]{1,0:T(8,128)S(1)}, f32[24,128]{1,0:T(8,128)S(1)}, u32[]{:S(2)}, u32[]{:S(2)}) collective-permute-start(f32[24,128]{1,0:T(8,128)S(1)} %get-tuple-element.25), channel_id=1, source_target_pairs={{1,0},{2,1},{3,2},{4,3},{5,4},{6,5},{7,6},{8,7},{9,8},{10,9},{11,1... | collective-permute-start | bytes 36872 | tf_op jit(solution)/shard_map/ppermute | solution.py:318
  126.0 3.6 %collective-permute-done.18.h_right = f32[24,128]{1,0:T(8,128)S(1)} collective-permute-done((f32[24,128]{1,0:T(8,128)S(1)}, f32[24,128]{1,0:T(8,128)S(1)}, u32[]{:S(2)}, u32[]{:S(2)}) %collective-permute-start.18) | collective-permute-done | bytes 12320 | tf_op jit(solution)/shard_map/ppermute | solution.py:318
  129.7 1.1 copy-done.7
  130.8 6.3 %last.1 = (f32[50,24,128]{2,1,0:T(8,128)}, f32[50,48,128]{2,1,0:T(8,128)}, f32[2,50,2,64]{3,2,1,0:T(2,128)}, f32[2,50,2,64]{3,2,1,0:T(2,128)}) custom-call(s32[4]{0:T(128)S(1)} %pad_add_fusion.info, f32[50,24,128]{2,1,0:T(8,128)S(1)} %copy-done.7, f32[50,24,128]{2,1,0:T(8,128)S(1)} %copy-done.1, s32[24,128]{1,0:T(8,128)S(1)} %copy-done.9, ...), custom_call_target="tpu_custom_call" | custom-call | tf_op jit(solution)/shard_map/last/pallas_call | solution.py:399
  (57 shorter events, 8.8 us)
Async XLA Ops:
  3.1 1.7 %copy-start.3 = (f32[2,50,48,128]{3,2,1,0:T(8,128)S(1)}, f32[2,50,48,128]{3,2,1,0:T(8,128)}, u32[]{:S(2)}) copy-start(f32[2,50,48,128]{3,2,1,0:T(8,128)} %traj.1) | copy-start | bytes 7372804
  6.6 38.1 %copy-start.2 = (f32[2,50,24,128]{3,2,1,0:T(8,128)S(1)}, f32[2,50,24,128]{3,2,1,0:T(8,128)}, u32[]{:S(2)}) copy-start(f32[2,50,24,128]{3,2,1,0:T(8,128)} %kappa.3) | copy-start | bytes 3686404
  8.3 0.7 collective-permute-start
  9.0 6.0 %collective-permute-start.6 = (f32[168,128]{1,0:T(8,128)S(1)}, f32[168,128]{1,0:T(8,128)S(1)}, u32[]{:S(2)}, u32[]{:S(2)}) collective-permute-start(f32[168,128]{1,0:T(8,128)S(1)} %add.27), channel_id=1, source_target_pairs={{145,2},{177,226},{146,5},{178,229},{147,8},{179,232},{148,11},{18... | collective-permute-start | bytes 258056 | tf_op jit(solution)/shard_map/ppermute | solution.py:313
  9.7 6.7 %collective-permute-start.5 = (f32[168,128]{1,0:T(8,128)S(1)}, f32[168,128]{1,0:T(8,128)S(1)}, u32[]{:S(2)}, u32[]{:S(2)}) collective-permute-start(f32[168,128]{1,0:T(8,128)S(1)} %add.27), channel_id=1, source_target_pairs={{145,1},{177,225},{146,4},{178,228},{147,7},{179,231},{148,10},{18... | collective-permute-start | bytes 258056 | tf_op jit(solution)/shard_map/ppermute | solution.py:313
  10.4 6.0 %collective-permute-start.4 = (f32[168,128]{1,0:T(8,128)S(1)}, f32[168,128]{1,0:T(8,128)S(1)}, u32[]{:S(2)}, u32[]{:S(2)}) collective-permute-start(f32[168,128]{1,0:T(8,128)S(1)} %add.27), channel_id=1, source_target_pairs={{145,0},{177,224},{146,3},{178,227},{147,6},{179,230},{148,9},{180... | collective-permute-start | bytes 258056 | tf_op jit(solution)/shard_map/ppermute | solution.py:313
  11.1 5.3 %collective-permute-start.3 = (f32[168,128]{1,0:T(8,128)S(1)}, f32[168,128]{1,0:T(8,128)S(1)}, u32[]{:S(2)}, u32[]{:S(2)}) collective-permute-start(f32[168,128]{1,0:T(8,128)S(1)} %add.27), channel_id=1, source_target_pairs={{144,2},{176,226},{145,5},{177,229},{146,8},{178,232},{147,11},{17... | collective-permute-start | bytes 258056 | tf_op jit(solution)/shard_map/ppermute | solution.py:313
  13.7 3.4 %collective-permute-start.2 = (f32[168,128]{1,0:T(8,128)S(1)}, f32[168,128]{1,0:T(8,128)S(1)}, u32[]{:S(2)}, u32[]{:S(2)}) collective-permute-start(f32[168,128]{1,0:T(8,128)S(1)} %add.27), channel_id=1, source_target_pairs={{144,1},{176,225},{145,4},{177,228},{146,7},{178,231},{147,10},{17... | collective-permute-start | bytes 258056 | tf_op jit(solution)/shard_map/ppermute | solution.py:313
  15.1 3.4 %collective-permute-start.1 = (f32[168,128]{1,0:T(8,128)S(1)}, f32[168,128]{1,0:T(8,128)S(1)}, u32[]{:S(2)}, u32[]{:S(2)}) collective-permute-start(f32[168,128]{1,0:T(8,128)S(1)} %add.27), channel_id=1, source_target_pairs={{144,0},{176,224},{145,3},{177,227},{146,6},{178,230},{147,9},{179... | collective-permute-start | bytes 258056 | tf_op jit(solution)/shard_map/ppermute | solution.py:313
  18.5 1.3 collective-permute-start.8
  19.1 25.6 %collective-permute-start.7 = (f32[168,128]{1,0:T(8,128)S(1)}, f32[168,128]{1,0:T(8,128)S(1)}, u32[]{:S(2)}, u32[]{:S(2)}) collective-permute-start(f32[168,128]{1,0:T(8,128)S(1)} %add.27), channel_id=1, source_target_pairs={{146,2},{178,226},{147,5},{179,229},{148,8},{180,232},{149,11},{18... | collective-permute-start | bytes 258056 | tf_op jit(solution)/shard_map/ppermute | solution.py:313
  19.8 0.7 collective-permute-start.9
  20.5 13.9 %collective-permute-start.10 = (f32[64,128]{1,0:T(8,128)S(1)}, f32[64,128]{1,0:T(8,128)S(1)}, u32[]{:S(2)}, u32[]{:S(2)}) collective-permute-start(f32[64,128]{1,0:T(8,128)S(1)} %add.34), channel_id=1, source_target_pairs={{0,32},{31,63},{64,96},{95,127},{160,128},{191,159},{224,192},{255... | collective-permute-start | bytes 98312 | tf_op jit(solution)/shard_map/ppermute | solution.py:313
  21.2 23.5 %collective-permute-start.11 = (f32[50,128]{1,0:T(8,128)S(1)}, f32[50,128]{1,0:T(8,128)S(1)}, u32[]{:S(2)}, u32[]{:S(2)}) collective-permute-start(f32[50,128]{1,0:T(8,128)S(1)} %get-tuple-element.17), channel_id=1, source_target_pairs={{0,32},{32,64},{64,96},{96,128},{128,160},{160,192},{192,224},{1,3... | collective-permute-start | bytes 76808 | tf_op jit(solution)/shard_map/ppermute | solution.py:318
  27.6 17.1 %collective-permute-start.12 = (f32[50,128]{1,0:T(8,128)S(1)}, f32[50,128]{1,0:T(8,128)S(1)}, u32[]{:S(2)}, u32[]{:S(2)}) collective-permute-start(f32[50,128]{1,0:T(8,128)S(1)} %get-tuple-element.18), channel_id=1, source_target_pairs={{32,0},{64,32},{96,64},{128,96},{160,128},{192,160},{224,192},{33,... | collective-permute-start | bytes 76808 | tf_op jit(solution)/shard_map/ppermute | solution.py:318
  29.5 8.9 %collective-permute-start.13 = (f32[24,128]{1,0:T(8,128)S(1)}, f32[24,128]{1,0:T(8,128)S(1)}, u32[]{:S(2)}, u32[]{:S(2)}) collective-permute-start(f32[24,128]{1,0:T(8,128)S(1)} %get-tuple-element.19), channel_id=1, source_target_pairs={{0,1},{1,2},{2,3},{3,4},{4,5},{5,6},{6,7},{7,8},{8,9},{9,10},{10,1... | collective-permute-start | bytes 36872 | tf_op jit(solution)/shard_map/ppermute | solution.py:318
  34.5 10.2 %collective-permute-start.14 = (f32[24,128]{1,0:T(8,128)S(1)}, f32[24,128]{1,0:T(8,128)S(1)}, u32[]{:S(2)}, u32[]{:S(2)}) collective-permute-start(f32[24,128]{1,0:T(8,128)S(1)} %get-tuple-element.20), channel_id=1, source_target_pairs={{1,0},{2,1},{3,2},{4,3},{5,4},{6,5},{7,6},{8,7},{9,8},{10,9},{11,1... | collective-permute-start | bytes 36872 | tf_op jit(solution)/shard_map/ppermute | solution.py:318
  44.7 85.0 %copy-start.5 = (f32[50,48,128]{2,1,0:T(8,128)S(1)}, f32[50,48,128]{2,1,0:T(8,128)}, u32[]{:S(2)}) copy-start(f32[50,48,128]{2,1,0:T(8,128)} %q.1) | copy-start | bytes 3686404
  52.3 77.3 %copy-start.1 = (f32[50,24,128]{2,1,0:T(8,128)S(1)}, f32[50,24,128]{2,1,0:T(8,128)}, u32[]{:S(2)}) copy-start(f32[50,24,128]{2,1,0:T(8,128)} %nu.5) | copy-start | bytes 1843204
  52.3 77.3 %copy-start.9 = (s32[24,128]{1,0:T(8,128)S(1)}, s32[24,128]{1,0:T(8,128)}, u32[]{:S(2)}) copy-start(s32[24,128]{1,0:T(8,128)} %mask.5) | copy-start | bytes 36868
  76.1 53.5 %all-to-all-start.1 = ((f32[8,32,128]{2,1,0:T(8,128)}), f32[8,32,128]{2,1,0:T(8,128)S(1)}, u32[]{:S(2)}, u32[]{:S(2)}) async-start(f32[8,32,128]{2,1,0:T(8,128)} %broadcast_in_dim.5), calls=%async_computation.1 | async-start | bytes 262144 | tf_op jit(solution)/shard_map/all_to_all | solution.py:397
  83.5 4.6 %collective-permute-start.24 = (f32[104,128]{1,0:T(8,128)S(1)}, f32[104,128]{1,0:T(8,128)S(1)}, u32[]{:S(2)}, u32[]{:S(2)}) collective-permute-start(f32[104,128]{1,0:T(8,128)S(1)} %get-tuple-element.26), channel_id=1, source_target_pairs={{2,145},{226,177},{5,146},{229,178},{8,147},{232,179},{11,148},{23... | collective-permute-start | bytes 159752 | tf_op jit(solution)/shard_map/ppermute | solution.py:313
  84.2 5.3 %collective-permute-start.23 = (f32[104,128]{1,0:T(8,128)S(1)}, f32[104,128]{1,0:T(8,128)S(1)}, u32[]{:S(2)}, u32[]{:S(2)}) collective-permute-start(f32[104,128]{1,0:T(8,128)S(1)} %get-tuple-element.26), channel_id=1, source_target_pairs={{1,145},{225,177},{4,146},{228,178},{7,147},{231,179},{10,148},{23... | collective-permute-start | bytes 159752 | tf_op jit(solution)/shard_map/ppermute | solution.py:313
  84.8 4.6 %collective-permute-start.22 = (f32[104,128]{1,0:T(8,128)S(1)}, f32[104,128]{1,0:T(8,128)S(1)}, u32[]{:S(2)}, u32[]{:S(2)}) collective-permute-start(f32[104,128]{1,0:T(8,128)S(1)} %get-tuple-element.26), channel_id=1, source_target_pairs={{0,145},{224,177},{3,146},{227,178},{6,147},{230,179},{9,148},{233... | collective-permute-start | bytes 159752 | tf_op jit(solution)/shard_map/ppermute | solution.py:313
  85.5 15.1 %collective-permute-start.21 = (f32[104,128]{1,0:T(8,128)S(1)}, f32[104,128]{1,0:T(8,128)S(1)}, u32[]{:S(2)}, u32[]{:S(2)}) collective-permute-start(f32[104,128]{1,0:T(8,128)S(1)} %get-tuple-element.26), channel_id=1, source_target_pairs={{2,144},{226,176},{5,145},{229,177},{8,146},{232,178},{11,147},{23... | collective-permute-start | bytes 159752 | tf_op jit(solution)/shard_map/ppermute | solution.py:313
  86.8 13.8 %collective-permute-start.20 = (f32[104,128]{1,0:T(8,128)S(1)}, f32[104,128]{1,0:T(8,128)S(1)}, u32[]{:S(2)}, u32[]{:S(2)}) collective-permute-start(f32[104,128]{1,0:T(8,128)S(1)} %get-tuple-element.26), channel_id=1, source_target_pairs={{1,144},{225,176},{4,145},{228,177},{7,146},{231,178},{10,147},{23... | collective-permute-start | bytes 159752 | tf_op jit(solution)/shard_map/ppermute | solution.py:313
  88.1 13.1 %collective-permute-start.19 = (f32[104,128]{1,0:T(8,128)S(1)}, f32[104,128]{1,0:T(8,128)S(1)}, u32[]{:S(2)}, u32[]{:S(2)}) collective-permute-start(f32[104,128]{1,0:T(8,128)S(1)} %get-tuple-element.26), channel_id=1, source_target_pairs={{0,144},{224,176},{3,145},{227,177},{6,146},{230,178},{9,147},{233... | collective-permute-start | bytes 159752 | tf_op jit(solution)/shard_map/ppermute | solution.py:313
  101.9 27.7 %collective-permute-start.25 = (f32[104,128]{1,0:T(8,128)S(1)}, f32[104,128]{1,0:T(8,128)S(1)}, u32[]{:S(2)}, u32[]{:S(2)}) collective-permute-start(f32[104,128]{1,0:T(8,128)S(1)} %row.1.g_own), channel_id=1, source_target_pairs={{176,208},{177,209},{178,210},{179,211},{180,212},{181,213},{182,2... | collective-permute-start | bytes 159752 | tf_op jit(solution)/shard_map/ppermute | solution.py:313
  102.6 27.1 %collective-permute-start.15 = (f32[50,128]{1,0:T(8,128)S(1)}, f32[50,128]{1,0:T(8,128)S(1)}, u32[]{:S(2)}, u32[]{:S(2)}) collective-permute-start(f32[50,128]{1,0:T(8,128)S(1)} %get-tuple-element.22), channel_id=1, source_target_pairs={{0,32},{32,64},{64,96},{96,128},{128,160},{160,192},{192,224},{1,3... | collective-permute-start | bytes 76808 | tf_op jit(solution)/shard_map/ppermute | solution.py:318
  104.5 25.1 %collective-permute-start.16 = (f32[50,128]{1,0:T(8,128)S(1)}, f32[50,128]{1,0:T(8,128)S(1)}, u32[]{:S(2)}, u32[]{:S(2)}) collective-permute-start(f32[50,128]{1,0:T(8,128)S(1)} %get-tuple-element.23), channel_id=1, source_target_pairs={{32,0},{64,32},{96,64},{128,96},{160,128},{192,160},{224,192},{33,... | collective-permute-start | bytes 76808 | tf_op jit(solution)/shard_map/ppermute | solution.py:318
  110.3 15.7 %collective-permute-start.17 = (f32[24,128]{1,0:T(8,128)S(1)}, f32[24,128]{1,0:T(8,128)S(1)}, u32[]{:S(2)}, u32[]{:S(2)}) collective-permute-start(f32[24,128]{1,0:T(8,128)S(1)} %get-tuple-element.24), channel_id=1, source_target_pairs={{0,1},{1,2},{2,3},{3,4},{4,5},{5,6},{6,7},{7,8},{8,9},{9,10},{10,1... | collective-permute-start | bytes 36872 | tf_op jit(solution)/shard_map/ppermute | solution.py:318
  124.1 5.6 %collective-permute-start.18 = (f32[24,128]{1,0:T(8,128)S(1)}, f32[24,128]{1,0:T(8,128)S(1)}, u32[]{:S(2)}, u32[]{:S(2)}) collective-permute-start(f32[24,128]{1,0:T(8,128)S(1)} %get-tuple-element.25), channel_id=1, source_target_pairs={{1,0},{2,1},{3,2},{4,3},{5,4},{6,5},{7,6},{8,7},{9,8},{10,9},{11,1... | collective-permute-start | bytes 36872 | tf_op jit(solution)/shard_map/ppermute | solution.py:318
  (5 other events, 4.8 us)
where the time goes:
time: 138 us; the launch traced here: 137 us
  starting transfers between devices  65 us (47%)
  waiting for transfers between devices  23.8 us (17%)
  blocking collectives  23.1 us (17%)
  Pallas kernels  15.5 us (11%)
  local copies, waits for them, and re-layouts  7.14 us (5%)
  between operations  2.37 us (2%)
    ppermute x8, starting transfers between devices, shifted(): return lax.ppermute(value, axis, pairs)  40.5 us
    all_to_all x1, blocking collectives, on_device(): lax.all_to_all(jnp.broadcast_to(side[None], (GX, 16, L)), 'gx', 0, 0)  23.1 us
    ppermute x18, starting transfers between devices, moved(): return lax.ppermute(value, ('gy', 'gx'), pairs)  17.1 us
    ppermute x18, waiting for transfers between devices, moved(): return lax.ppermute(value, ('gy', 'gx'), pairs)  13.9 us
    ppermute x8, waiting for transfers between devices, shifted(): return lax.ppermute(value, axis, pairs)  9.92 us
    all_to_all x1, starting transfers between devices, on_device(): lax.all_to_all(jnp.broadcast_to(pair[None], (GY, 32, L)), 'gy', 0, 0)  7.37 us
    pallas_call x1, Pallas kernels, on_device(): pl.pallas_call(nest_kernel, out_shape=(shape(K, NR, L), shape(K, L), shap...  6.79 us
    unnamed x20, local copies, waits for them, and re-layouts  6.45 us
  transfers between devices with their start and end apart: 27, of which 6 were waited for; matrix products, arithmetic and copies ran while one was open for 0% of the time, Pallas kernels for 0%

commit v1 on v0

v1 whole, which is shorter than its diff:
```python
import jax
import jax.numpy as jnp
from jax import lax
from jax.experimental import pallas as pl
from jax.experimental.pallas import tpu as pltpu
from jax.sharding import PartitionSpec as P

R = 3
K = 50
NR = 24
PR = 48
L = 128
GY = 8
GX = 32
SR = 64
ROW0 = 192
COL0 = 2048
SOUTH = 4
WEST = 16
SPAN = 1366
F32 = jnp.float32
VM = pl.BlockSpec(memory_space=pltpu.VMEM)
SM = pl.BlockSpec(memory_space=pltpu.SMEM)
HB = pl.BlockSpec(memory_space=pltpu.HBM)
ANY = pl.BlockSpec(memory_space=pl.ANY)
PARAMS = pltpu.CompilerParams(vmem_limit_bytes=24 * 1024 * 1024)
FULL = pltpu.CompilerParams(vmem_limit_bytes=60 * 1024 * 1024)


def exact(left, right):
    return lax.dot_general(
        left, right, (((1,), (0,)), ((), ())), precision=lax.Precision.HIGHEST, preferred_element_type=F32
    )


def exact_t(left, right):
    return lax.dot_general(
        left, right, (((1,), (1,)), ((), ())), precision=lax.Precision.HIGHEST, preferred_element_type=F32
    )


def iota(shape, dim):
    return lax.broadcasted_iota(jnp.int32, shape, dim)


def wide(col, rows):
    return jnp.broadcast_to(col, (rows, L))


def place(row, col):
    return lax.axis_index("gy"), lax.axis_index("gx"), row[0], col[0]


def side_lane(x, ox):
    west = ox - 1 - L * x
    east = ox + SPAN - L * x
    is_west = (west >= 0) & (west < L)
    is_east = (east >= 0) & (east < L)
    return is_west, is_east, jnp.where(is_west, west, east)


def ring_row(g, x, oy):
    row = jnp.where(g == SOUTH, oy - 1, oy + SR) - PR * g
    ok = (row >= 0) & (row < PR) & (g >= SOUTH) & (g < GY - 1) & (x >= WEST) & (x < WEST + 12)
    return ok, row


def threes(x, shape, dim):
    cell = L * lax.rem(x, 3) + iota(shape, dim)
    first = 3 * iota(shape, 1 - dim)
    return ((first <= cell) & (cell < first + 3)).astype(F32)


def row_sums(rows, x):
    col = x * L + iota(rows.shape, 1)
    return exact(jnp.where((col > 0) & (col < GX * L - 1), rows, 0.0), threes(x, (L, L), 0))


def panel_kernel(o_row, o_col, traj, pay, row_s, col_s, buf, sems):
    g, x, oy, ox = place(o_row, o_col)
    row_ok, row = ring_row(g, x, oy)
    is_west, is_east, spot = side_lane(x, ox)
    side_ok = (is_west | is_east) & (g >= SOUTH) & (g < GY - 1)
    tile = pl.multiple_of(8 * (row // 8), 8)

    def row_copy():
        return pltpu.make_async_copy(traj.at[:, :, pl.ds(tile, 8), :], row_s, sems.at[2])

    def col_copy(s):
        return pltpu.make_async_copy(traj.at[s], col_s.at[s], sems.at[s])

    @pl.when(side_ok)
    def _():
        col_copy(1).start()
        col_copy(0).start()

    @pl.when(row_ok)
    def _():
        row_copy().start()

    pay[...] = jnp.zeros(pay.shape, F32)
    @pl.when(row_ok)
    def _():
        row_copy().wait()
        for i, s in enumerate((1, 0)):
            for k in range(K):
                pay[pl.ds(K * i + k, 1), :] = jax.nn.sigmoid(row_s[s, k, pl.ds(row - tile, 1), :])

    @pl.when(side_ok)
    def _():
        plane = iota((PR, L), 1)
        acc = jnp.zeros((PR, L), F32)
        for i, s in enumerate((1, 0)):
            col_copy(s).wait()
            for k in range(K):
                to = 64 * i + k
                acc = jnp.where(plane == to, pltpu.roll(col_s[s, k], lax.rem(to - spot + L, L), 1), acc)
        used = (plane < K) | ((plane >= 64) & (plane < 64 + K))
        buf[...] = jnp.zeros(buf.shape, F32)
        start = PR * g - oy + SR
        weights = jnp.where(used, jax.nn.sigmoid(acc), 0.0)
        for r in range(PR):
            buf[pl.ds(start + r, 1), :] = weights[r : r + 1]
        pay[104:168, :] = buf[SR : 2 * SR, :]


def edge_kernel(a, nu, mask, pay, to_up, to_down, v_left, v_right):
    m = mask[...].astype(F32)
    lane = iota((NR, L), 1)
    acc_l = jnp.zeros((NR, L), F32)
    acc_r = jnp.zeros((NR, L), F32)
    for k in range(K):
        v = nu[k] * m * a[k]
        to_up[pl.ds(k, 1), :] = v[0:1]
        to_down[pl.ds(k, 1), :] = v[NR - 1 : NR]
        acc_l = jnp.where(lane == k, pltpu.roll(v, k, 1) if k else v, acc_l)
        acc_r = jnp.where(lane == k, pltpu.roll(v, k + 1, 1), acc_r)
    v_left[...] = acc_l
    v_right[...] = acc_r
    for to in (to_up, to_down):
        to[K:56, :] = jnp.zeros((56 - K, L), F32)
        to[56:224, :] = pay[...]


def mix_kernel(pay, down, up, swap, after_left, after_right, out):
    g = lax.axis_index("gy")
    own = pay[0:104, :]
    out[0:104, :] = jnp.where(g == 5, own + up[56:160, :], own)
    zero = jnp.zeros((SR, L), F32)
    above = jnp.where(g == 4, zero, down[160:224, :])
    below = jnp.where(g == 6, zero, up[160:224, :])
    out[104:168, :] = pay[104:168, :] + swap[104:168, :] + above + below


def base_kernel(q, pkappa, after, q_out, e_s):
    zero = jnp.zeros((PR, L), F32)
    src = q
    for step in (1, 0):
        c_prev, e_prev, y = zero, zero, zero
        for k in range(K):
            c = pkappa[step, k]
            r = 1.0 / (1.0 + c + c_prev * (1.0 - e_prev))
            e = c * r
            e_s[k] = e
            y = (src[k] + c_prev * y) * r
            q_out[k] = y
            c_prev, e_prev = c, e
        for k in range(K - 2, -1, -1):
            y = q_out[k] + e_s[k] * y
            q_out[k] = y
        src = q_out


def spread_kernel(side, v_left, v_right, down, up, out, one_s):
    x = lax.axis_index("gx")

    def packed(v):
        return v[0:12] + pltpu.roll(v[12:24], 64, 1)

    to_left, to_right = packed(v_left[...]), packed(v_right[...])
    one_s[0:K, :] = down[56 : 56 + K, :] + up[56 : 56 + K, :]
    one_s[K:62, :] = jnp.zeros((62 - K, L), F32)
    one_s[62:78, :] = side[...]
    one_s[78:80, :] = jnp.zeros((2, L), F32)
    every = one_s[...]
    for i in range(GX):
        out[i] = every

    @pl.when(x > 0)
    def _():
        out[jnp.maximum(x - 1, 0), K:62, :] = to_left

    @pl.when(x < GX - 1)
    def _():
        out[jnp.minimum(x + 1, GX - 1), K:62, :] = to_right


def turn_kernel(across, out):
    west, east = across[0, 62:78], across[GX - 1, 62:78]
    for i in range(GY):
        out[i, 0:16] = west
        out[i, 16:32] = east


def first_lane(t):
    return jnp.where(t == 0, 0, jnp.where(t == 1, 42, 85))


def nest_kernel(
    o_row, o_col, a, nu, mask, kappa, h_up, h_down, h_left, h_right, *rest,
):
    parts = rest[:7]
    a_out, to_up, to_down, v_left, v_right, side, e_s, y_s, w_s, up_s, down_s, g_s, we_s = rest[8:]
    g, x, oy, ox = place(o_row, o_col)
    sig = ox - COL0
    t = lax.rem(x, 3)
    rows = 104
    def third(i):
        got = jnp.where(t == 0, parts[i][0:rows, :], parts[i + 1][0:rows, :])
        return jnp.where(t == 2, parts[i + 2][0:rows, :], got)

    own, nxt, nxt2 = third(0), third(3), parts[6][0:rows, :]
    wl = iota((rows, L), 1)
    back = L - sig
    shift = lax.rem(back + L, L)
    panel = jnp.where(wl < back, pltpu.roll(own, shift, 1), pltpu.roll(nxt, shift, 1))
    pi, pc = iota((L, L), 0), iota((L, L), 1)
    spread = threes(x, (L, L), 1)
    c_all = x * L + wl
    inner = (c_all > 0) & (c_all < GX * L - 1) & ((g == 0) | (g == GY - 1))
    w_s[...] = jnp.where(inner, exact(panel, spread), 0.0)

    er, el = iota((8, L), 0), iota((8, L), 1)
    left_at = jnp.where(t == 0, -1, jnp.where(t == 1, 42, 85)) + sig
    right_at = jnp.where(t == 0, 42, jnp.where(t == 1, 85, L)) + sig
    want = jnp.where(er == 0, left_at, jnp.where(er == 1, right_at, -1))
    ends = (
        exact_t((el == want).astype(F32), own)
        + exact_t((el + L == want).astype(F32), nxt)
        + exact_t((el + 2 * L == want).astype(F32), nxt2)
    )

    row24, lane24 = iota((NR, L), 0), iota((NR, L), 1)
    m_row = (((row24 == 0) & (g == 0)) | ((row24 == NR - 1) & (g == GY - 1))).astype(F32)
    m_lane = (((lane24 == 0) & (x == 0)) | ((lane24 == L - 1) & (x == GX - 1))).astype(F32)
    ends_l = jnp.concatenate([ends[0:1], jnp.zeros((1, 24), F32)], 1)
    ends_r = jnp.concatenate([ends[1:2], jnp.zeros((1, 24), F32)], 1)
    hl = h_left[...] * (1.0 - m_row * wide(ends_l, NR))
    hr = h_right[...] * (1.0 - m_row * wide(ends_r, NR))

    panel_we = parts[0][rows:, :]
    for part in parts[1:]:
        panel_we = panel_we + part[rows:, :]
    we_s[...] = panel_we
    qr, qj = iota((NR, SR), 0), iota((NR, SR), 1)
    base = 3 * (qj - 8 * g)
    w_we = exact(((base <= qr) & (qr < base + 3)).astype(F32), panel_we)
    flip = jnp.concatenate([panel_we, jnp.zeros((SR, L), F32)], 0).T
    edge = ((pc == 0) & (x == 0)) | ((pc == L - 1) & (x == GX - 1))
    up_s[...] = h_up[0:K, :] * (1.0 - exact(flip, (edge & (pi == 8 * g - 1)).astype(F32))[0:K])
    down_s[...] = h_down[0:K, :] * (1.0 - exact(flip, (edge & (pi == 8 * g + 8)).astype(F32))[0:K])

    m = mask[...].astype(F32)
    one = jnp.ones((NR, L), F32)
    zero = jnp.zeros((NR, L), F32)
    c_prev, e_prev, y = zero, zero, zero
    top = g == 0
    is31 = (x == GX - 1).astype(jnp.int32)
    for k in range(K):
        w_row = w_s[pl.ds(k, 1), :]
        raw = a[k]
        g_s[pl.ds(k, 1), :] = jnp.where(top, raw[0:1], raw[NR - 1 : NR])
        now = raw * (one - (m_row * wide(w_row, NR) + m_lane * wide(w_we[:, k : k + 1], NR)))
        v = nu[k] * m * now
        above = jnp.where(row24 == 0, wide(up_s[pl.ds(k, 1), :], NR), pltpu.roll(v, 1, 0))
        below = jnp.where(row24 == NR - 1, wide(down_s[pl.ds(k, 1), :], NR), pltpu.roll(v, NR - 1, 0))
        left = jnp.where(lane24 == 0, wide(hl[:, k : k + 1], NR), pltpu.roll(v, 1, 1))
        right = jnp.where(lane24 == L - 1, wide(hr[:, k : k + 1], NR), pltpu.roll(v, L - 1, 1))
        b = m * (now + (above + below + left + right - 4.0 * v))
        c = kappa[1, k]
        r = 1.0 / (1.0 + c + c_prev * (1.0 - e_prev))
        e = c * r
        y = (b + c_prev * y) * r
        e_s[k] = e
        y_s[k] = y
        c_prev, e_prev = c, e
    sol = zero
    acc_l, acc_r = zero, zero
    for k in range(K - 1, -1, -1):
        sol = y_s[k] + e_s[k] * sol if k < K - 1 else y_s[k]
        y_s[k] = sol
        w_row = w_s[pl.ds(K + k, 1), :]
        g_s[pl.ds(56 + k, 1), :] = jnp.where(top, sol[0:1], sol[NR - 1 : NR])
        now = sol * (one - (m_row * wide(w_row, NR) + m_lane * wide(w_we[:, 64 + k : 65 + k], NR)))
        a_out[k] = now
        v = nu[k] * m * now
        to_up[pl.ds(k, 1), :] = v[0:1]
        to_down[pl.ds(k, 1), :] = v[NR - 1 : NR]
        acc_l = jnp.where(lane24 == k, pltpu.roll(v, k, 1) if k else v, acc_l)
        acc_r = jnp.where(lane24 == k, pltpu.roll(v, k + 1, 1), acc_r)
    v_left[...] = acc_l
    v_right[...] = acc_r
    for i in (*range(K, 56), *range(56 + K, 112)):
        g_s[pl.ds(i, 1), :] = jnp.zeros((1, L), F32)
    sums = row_sums(g_s[...], x)
    sums = pltpu.roll(sums, lax.rem(L - first_lane(t), L), 1)
    sums = sums[0:56] + pltpu.roll(sums[56:112], 64, 1)
    sums = jnp.where((g == 0) | (g == GY - 1), sums, 0.0)
    for to in (to_up, to_down):
        to[K:56, :] = jnp.zeros((56 - K, L), F32)
        to[56:112, :] = sums

    side[...] = jnp.zeros(side.shape, F32)

    @pl.when((x == 0) | (x == GX - 1))
    def _():
        acc = zero
        for k in range(K):
            acc = jnp.where(lane24 == k, pltpu.roll(a[k], lax.rem(k + is31, L), 1), acc)
            acc = jnp.where(lane24 == 64 + k, pltpu.roll(y_s[k], lax.rem(64 + k + is31, L), 1), acc)
        terms = w_we * acc
        sj, sr = iota((8, NR), 0), iota((8, NR), 1)
        side[0:8, :] = exact(((3 * sj <= sr) & (sr < 3 * sj + 3)).astype(F32), terms)
        side[8:16, :] = we_s[pl.ds(pl.multiple_of(8 * g, 8), 8), :]


def last_kernel(
    o_row, o_col, a, nu, mask, kappa, across, sides, down, up, third, pay, pkappa, q,
    a_out, q_out, s_w, s_g,
    e_s, panel_s, local_s, g_s, t_s, d_s, up_s, row_k, tile_s, col_k, q_s, pe_s, sems,
):
    g, x, oy, ox = place(o_row, o_col)
    row_ok, row = ring_row(g, x, oy)
    is_west, is_east, spot = side_lane(x, ox)
    side_ok = (is_west | is_east) & (g >= SOUTH) & (g < GY - 1)
    alone = row_ok & jnp.logical_not(side_ok)
    tile = pl.multiple_of(8 * (row // 8), 8)
    at = pl.ds(tile, 8)

    def row_copy():
        return pltpu.make_async_copy(pkappa.at[:, :, at, :], row_k, sems.at[0])

    def tile_copy():
        return pltpu.make_async_copy(q.at[:, at, :], tile_s, sems.at[1])

    def col_copy():
        return pltpu.make_async_copy(pkappa, col_k, sems.at[2])

    def whole_copy():
        return pltpu.make_async_copy(q, q_s, sems.at[3])

    @pl.when(side_ok)
    def _():
        col_copy().start()
        whole_copy().start()

    @pl.when(row_ok)
    def _():
        row_copy().start()

    @pl.when(alone)
    def _():
        tile_copy().start()

    m = mask[...].astype(F32)
    row24, lane24 = iota((NR, L), 0), iota((NR, L), 1)

    def unpacked(p):
        return jnp.concatenate([p, pltpu.roll(p, 64, 1)], 0)

    hl = jnp.where(x > 0, unpacked(across[jnp.maximum(x - 1, 0), K:62]), 0.0)
    hr = jnp.where(x < GX - 1, unpacked(across[jnp.minimum(x + 1, GX - 1), K:62]), 0.0)
    up_s[...] = third[...] + jnp.where((g == 4) | (g == 5), 0.0, down[0:K, :])
    zero = jnp.zeros((NR, L), F32)
    c_prev, e_prev, y = zero, zero, zero
    for k in range(K):
        now = a[k]
        v = nu[k] * m * now
        above = jnp.where(row24 == 0, wide(up_s[pl.ds(k, 1), :], NR), pltpu.roll(v, 1, 0))
        below = jnp.where(row24 == NR - 1, wide(up[pl.ds(k, 1), :], NR), pltpu.roll(v, NR - 1, 0))
        left = jnp.where(lane24 == 0, wide(hl[:, k : k + 1], NR), pltpu.roll(v, 1, 1))
        right = jnp.where(lane24 == L - 1, wide(hr[:, k : k + 1], NR), pltpu.roll(v, L - 1, 1))
        b = m * (now + (above + below + left + right - 4.0 * v))
        c = kappa[0, k]
        r = 1.0 / (1.0 + c + c_prev * (1.0 - e_prev))
        e = c * r
        y = (b + c_prev * y) * r
        e_s[k] = e
        a_out[k] = y
        c_prev, e_prev = c, e
    for k in range(K - 2, -1, -1):
        y = a_out[k] + e_s[k] * y
        a_out[k] = y

    def panels(first):
        return jnp.concatenate([sides[i, 16 * e + first : 16 * e + first + 8, :] for e in (0, 1) for i in range(GY)], 0)

    grads = panels(0)
    flip_g = grads.T
    flip_w = panels(8).T
    for i, s in enumerate((1, 0)):
        for e in (0, 1):
            s_g[s, :, e, :] = flip_g[64 * i : 64 * i + K, SR * e : SR * e + SR]
            s_w[s, :, e, :] = flip_w[64 * i : 64 * i + K, SR * e : SR * e + SR]

    def correct(coef, terms, zero, mid_s, fact_s):
        for step in (1, 0):
            c_prev, e_prev, y = zero, zero, zero
            for k in range(K):
                c = coef[step, k]
                r = 1.0 / (1.0 + c + c_prev * (1.0 - e_prev))
                e = c * r
                fact_s[k] = e
                term = terms(step, k)
                y = ((term if step else term + mid_s[k]) + c_prev * y) * r
                mid_s[k] = y
                c_prev, e_prev = c, e
            for k in range(K - 2, -1, -1):
                y = mid_s[k] + fact_s[k] * y
                mid_s[k] = y

    @pl.when(row_ok)
    def _():
        sig = ox - COL0
        turn = lax.rem(sig, L)
        low = iota((56, L), 1) < 64

        def come(base):
            first = jnp.zeros((56, L), F32)
            second = jnp.zeros((56, L), F32)
            for t in range(3):
                j = 3 * base + t
                got = jnp.where((j >= 0) & (j < GX), across[jnp.clip(j, 0, GX - 1), 0:56], 0.0)
                one = jnp.where(low, got, 0.0)
                two = jnp.where(low, pltpu.roll(got, 64, 1), 0.0)
                start = (0, 42, 85)[t]
                first = first + (pltpu.roll(one, start, 1) if t else one)
                second = second + (pltpu.roll(two, start, 1) if t else two)
            return first, second

        def on_parent(own, prev):
            return jnp.where(iota(own.shape, 1) >= sig, pltpu.roll(own, turn, 1), pltpu.roll(prev, turn, 1))

        own, prev = come(x - WEST), come(x - WEST - 1)
        g_s[0:56, :] = on_parent(own[0], prev[0]) * pay[0:56, :]
        g_s[K : 2 * K, :] = on_parent(own[1], prev[1])[0:K] * pay[K : 2 * K, :]
        here = iota((8, L), 0) == row - tile
        row_copy().wait()
        correct(
            row_k,
            lambda step, k: jnp.where(here, wide(g_s[pl.ds(k if step else K + k, 1), :], 8), 0.0),
            jnp.zeros((8, L), F32), t_s, pe_s.at[:, 0:8, :],
        )

    @pl.when(alone)
    def _():
        tile_copy().wait()
        t_s[...] = t_s[...] + tile_s[...]
        back = pltpu.make_async_copy(t_s, q_out.at[:, at, :], sems.at[1])
        back.start()
        back.wait()

    @pl.when(side_ok)
    def _():
        panel_s[...] = jnp.zeros(panel_s.shape, F32)
        panel_s[SR : 2 * SR, :] = jnp.where(is_west, grads[0:SR], grads[SR : 2 * SR])
        start = PR * g - oy + SR
        for r in range(PR):
            local_s[pl.ds(r, 1), :] = panel_s[pl.ds(start + r, 1), :]
        here = iota((PR, L), 1) == spot
        local = local_s[...]

        def terms(step, k):
            i = k if step else 64 + k
            return jnp.where(here, wide(local[:, i : i + 1], PR), 0.0)

        col_copy().wait()
        correct(col_k, terms, jnp.zeros((PR, L), F32), d_s, pe_s)
        whole_copy().wait()
        d_s[...] = d_s[...] + q_s[...]

        @pl.when(row_ok)
        def _():
            for k in range(K):
                d_s[k, at, :] = d_s[k, at, :] + t_s[k]

        back = pltpu.make_async_copy(d_s, q_out, sems.at[3])
        back.start()
        back.wait()


def shape(*dims):
    return jax.ShapeDtypeStruct(dims, F32)


def at(g, x):
    return g * GX + x


def moved(value, pairs):
    return lax.ppermute(value, ("gy", "gx"), pairs)


def shifted(value, axis, count, step):
    pairs = [(i, i + step) for i in range(count) if 0 <= i + step < count]
    return lax.ppermute(value, axis, pairs)


TURNS = (0, 1, 2, -3, -2, -1, -4)


def panel_routes():
    routes = []
    for t in TURNS:
        pairs = []
        for p in range(WEST, WEST + 12):
            j = 3 * (p - WEST) + t
            if 0 <= j < GX:
                pairs += [(at(4, p), at(0, j)), (at(5, p), at(7, j))]
        routes.append(pairs)
    for e, p in ((0, WEST), (GX - 1, WEST + 10), (GX - 1, WEST + 11)):
        for k in range(1, GY - 1):
            free = [
                (n, i)
                for i in (6, 5, 4)
                for n, pairs in enumerate(routes)
                if not any(a == at(i, p) or b == at(k, e) for a, b in pairs)
            ]
            n, i = free[0]
            routes[n].append((at(i, p), at(k, e)))
    return routes


def on_device(nest_adjoint, nest_kappa, nest_nu, land_mask, parent_adjoint, parent_kappa, parent_traj, offset_row, offset_col):
    here = (offset_row, offset_col)
    pay = pl.pallas_call(
        panel_kernel,
        out_shape=shape(168, L),
        in_specs=[SM, SM, HB],
        out_specs=VM,
        scratch_shapes=[
            pltpu.VMEM((2, K, 8, L), F32), pltpu.VMEM((2, K, PR, L), F32), pltpu.VMEM((256, L), F32),
            pltpu.SemaphoreType.DMA((3,)),
        ],
        compiler_params=FULL,
        name="panel",
    )(*here, parent_traj)
    to_up, to_down, v_left, v_right = pl.pallas_call(
        edge_kernel,
        out_shape=(shape(224, L), shape(224, L), shape(NR, L), shape(NR, L)),
        in_specs=[VM] * 4,
        out_specs=(VM,) * 4,
        compiler_params=PARAMS,
        name="edge",
    )(nest_adjoint, nest_nu, land_mask, pay)
    down = shifted(to_down, "gy", GY, 1)
    up = shifted(to_up, "gy", GY, -1)
    ring = range(WEST, WEST + 12)
    swap = moved(pay, [(at(i, p), at(10 - i, p)) for i in (4, 6) for p in ring])
    h_left = shifted(v_right, "gx", GX, 1)
    h_right = shifted(v_left, "gx", GX, -1)
    mixed = pl.pallas_call(
        mix_kernel,
        out_shape=shape(168, L),
        in_specs=[VM] * 4 + [ANY] * 2,
        out_specs=VM,
        compiler_params=PARAMS,
        name="mix",
    )(pay, down, up, swap, h_left, h_right)
    parts = [moved(mixed, pairs) for pairs in panel_routes()]
    nest, parent = shape(K, NR, L), shape(K, PR, L)
    base = pl.pallas_call(
        base_kernel,
        out_shape=parent,
        in_specs=[VM] * 2 + [ANY],
        out_specs=VM,
        scratch_shapes=[pltpu.VMEM((K, PR, L), F32)],
        compiler_params=PARAMS,
        cost_estimate=pl.CostEstimate(flops=10000000, bytes_accessed=12000000, transcendentals=0),
        name="base",
    )(parent_adjoint, parent_kappa, mixed)

    state, to_up, to_down, v_left, v_right, side = pl.pallas_call(
        nest_kernel,
        out_shape=(nest, shape(112, L), shape(112, L), shape(NR, L), shape(NR, L), shape(16, L)),
        in_specs=[SM] * 2 + [VM] * 15 + [ANY],
        out_specs=(VM,) * 6,
        scratch_shapes=[
            pltpu.VMEM((K, NR, L), F32), pltpu.VMEM((K, NR, L), F32), pltpu.VMEM((104, L), F32), pltpu.VMEM((K, L), F32),
            pltpu.VMEM((K, L), F32), pltpu.VMEM((112, L), F32), pltpu.VMEM((SR, L), F32),
        ],
        compiler_params=PARAMS,
        name="nest",
    )(*here, nest_adjoint, nest_nu, land_mask, nest_kappa, down, up, h_left, h_right, *parts, base)

    rows = ((0, 4), (7, 5), (1, 2), (2, 3), (5, 6), (6, 7))
    down = moved(to_down, [(at(i, j), at(k, j)) for i, k in rows for j in range(GX)])
    up = shifted(to_up, "gy", GY, -1)
    third = moved(to_down[0:K], [(at(i, j), at(i + 1, j)) for i in (0, 3, 4) for j in range(GX)])
    across = pl.pallas_call(
        spread_kernel,
        out_shape=shape(GX, 80, L),
        in_specs=[VM] * 5,
        out_specs=VM,
        scratch_shapes=[pltpu.VMEM((80, L), F32)],
        compiler_params=PARAMS,
        name="spread",
    )(side, v_left, v_right, down, up)
    across = lax.all_to_all(across, "gx", 0, 0)
    sides = pl.pallas_call(
        turn_kernel, out_shape=shape(GY, 32, L), in_specs=[VM], out_specs=VM, compiler_params=PARAMS, name="turn"
    )(across)
    sides = lax.all_to_all(sides, "gy", 0, 0)

    return pl.pallas_call(
        last_kernel,
        out_shape=(nest, parent, shape(2, K, 2, SR), shape(2, K, 2, SR)),
        in_specs=[SM] * 2 + [VM] * 10 + [HB] * 2,
        out_specs=(VM, HB, VM, VM),
        scratch_shapes=[
            pltpu.VMEM((K, NR, L), F32), pltpu.VMEM((256, L), F32), pltpu.VMEM((PR, L), F32), pltpu.VMEM((104, L), F32),
            pltpu.VMEM((K, 8, L), F32), pltpu.VMEM((K, PR, L), F32), pltpu.VMEM((K, L), F32),
            pltpu.VMEM((2, K, 8, L), F32), pltpu.VMEM((K, 8, L), F32), pltpu.VMEM((2, K, PR, L), F32),
            pltpu.VMEM((K, PR, L), F32), pltpu.VMEM((K, PR, L), F32), pltpu.SemaphoreType.DMA((4,)),
        ],
        input_output_aliases={13: 1},
        compiler_params=PARAMS,
        name="last",
    )(*here, state, nest_nu, land_mask, nest_kappa, across, sides, down, up, third, pay, parent_kappa, base)


def solution(mesh):
    in_specs = (
        P(None, "gy", "gx"),
        P(None, None, "gy", "gx"),
        P(None, "gy", "gx"),
        P("gy", "gx"),
        P(None, "gy", "gx"),
        P(None, None, "gy", "gx"),
        P(None, None, "gy", "gx"),
        P(),
        P(),
    )
    out_specs = (P(None, "gy", "gx"), P(None, "gy", "gx"), P(), P())
    return jax.shard_map(on_device, mesh=mesh, in_specs=in_specs, out_specs=out_specs, check_vma=False)
```

time: 138 us -> 114 us (0.83)
  the two profiles are of different devices: /device:TPU:144 before, /device:TPU:1 now
where the time goes in v1:
time: 114 us; the launch traced here: 113 us
  waiting for transfers between devices  35 us (31%)
  starting transfers between devices  33.4 us (29%)
  blocking collectives  20.7 us (18%)
  Pallas kernels  13 us (11%)
  local copies, waits for them, and re-layouts  8.29 us (7%)
  between operations  2.31 us (2%)
    ppermute x10, waiting for transfers between devices, moved(): return lax.ppermute(value, ('gy', 'gx'), pairs)  26.8 us
    all_to_all x1, blocking collectives, on_device(): across = lax.all_to_all(across, 'gx', 0, 0)  20.7 us
    ppermute x5, starting transfers between devices, shifted(): return lax.ppermute(value, axis, pairs)  14.5 us
    ppermute x10, starting transfers between devices, moved(): return lax.ppermute(value, ('gy', 'gx'), pairs)  11.9 us
    unnamed x28, local copies, waits for them, and re-layouts  8.29 us
    all_to_all x1, starting transfers between devices, on_device(): sides = lax.all_to_all(sides, 'gy', 0, 0)  6.98 us
    pallas_call x1, Pallas kernels, on_device(): pl.pallas_call(nest_kernel, out_shape=(nest, shape(112, L), shape(112, L)...  6.67 us
    all_to_all x1, waiting for transfers between devices, on_device(): sides = lax.all_to_all(sides, 'gy', 0, 0)  5.02 us
  transfers between devices with their start and end apart: 16, of which 5 were waited for; matrix products, arithmetic and copies ran while one was open for 0% of the time, Pallas kernels for 2%

profile of v1, /device:TPU:1, one launch (start us, length us, event | category | flops | bytes accessed | tf_op | source)
XLA Modules:
  0.0 112.7 jit_solution(13585023443495867680)
XLA Ops:
  2.1 0.7 panel.1.pay
  2.8 0.9 copy-done.7
  3.7 0.7 copy-done.12
  4.8 6.3 %collective-permute-start = (f32[224,128]{1,0:T(8,128)S(1)}, f32[224,128]{1,0:T(8,128)S(1)}, u32[]{:S(2)}, u32[]{:S(2)}) collective-permute-start(f32[224,128]{1,0:T(8,128)S(1)} %get-tuple-element.14), channel_id=1, source_target_pairs={{0,32},{32,64},{64,96},{96,128},{128,160},{160,192},{192,224},{1,3... | collective-permute-start | bytes 344072 | tf_op jit(solution)/shard_map/ppermute | solution.py:506
  11.1 1.9 %collective-permute-start.1 = (f32[224,128]{1,0:T(8,128)S(1)}, f32[224,128]{1,0:T(8,128)S(1)}, u32[]{:S(2)}, u32[]{:S(2)}) collective-permute-start(f32[224,128]{1,0:T(8,128)S(1)} %get-tuple-element.15), channel_id=1, source_target_pairs={{32,0},{64,32},{96,64},{128,96},{160,128},{192,160},{224,192},{33,... | collective-permute-start | bytes 344072 | tf_op jit(solution)/shard_map/ppermute | solution.py:506
  13.0 0.7 collective-permute-start.4
  13.7 3.1 %collective-permute-start.2 = (f32[24,128]{1,0:T(8,128)S(1)}, f32[24,128]{1,0:T(8,128)S(1)}, u32[]{:S(2)}, u32[]{:S(2)}) collective-permute-start(f32[24,128]{1,0:T(8,128)S(1)} %get-tuple-element.16), channel_id=1, source_target_pairs={{0,1},{1,2},{2,3},{3,4},{4,5},{5,6},{6,7},{7,8},{8,9},{9,10},{10,1... | collective-permute-start | bytes 36872 | tf_op jit(solution)/shard_map/ppermute | solution.py:506
  16.8 1.3 %collective-permute-start.3 = (f32[24,128]{1,0:T(8,128)S(1)}, f32[24,128]{1,0:T(8,128)S(1)}, u32[]{:S(2)}, u32[]{:S(2)}) collective-permute-start(f32[24,128]{1,0:T(8,128)S(1)} %get-tuple-element.17), channel_id=1, source_target_pairs={{1,0},{2,1},{3,2},{4,3},{5,4},{6,5},{7,6},{8,7},{9,8},{10,9},{11,1... | collective-permute-start | bytes 36872 | tf_op jit(solution)/shard_map/ppermute | solution.py:506
  18.1 3.1 %collective-permute-done.3.after_right.h_right = f32[24,128]{1,0:T(8,128)S(1)} collective-permute-done((f32[24,128]{1,0:T(8,128)S(1)}, f32[24,128]{1,0:T(8,128)S(1)}, u32[]{:S(2)}, u32[]{:S(2)}) %collective-permute-start.3) | collective-permute-done | bytes 12320 | tf_op jit(solution)/shard_map/ppermute | solution.py:506
  21.3 0.8 collective-permute-start.11
  22.1 0.7 collective-permute-start.10
  22.8 0.7 collective-permute-start.9
  23.5 0.7 collective-permute-start.8
  24.9 0.7 collective-permute-start.6
  25.5 1.3 %collective-permute-start.5 = (f32[168,128]{1,0:T(8,128)S(1)}, f32[168,128]{1,0:T(8,128)S(1)}, u32[]{:S(2)}, u32[]{:S(2)}) collective-permute-start(f32[168,128]{1,0:T(8,128)S(1)} %mix.1.after), channel_id=1, source_target_pairs={{144,0},{176,224},{145,3},{177,227},{146,6},{178,230},{147,9},{179... | collective-permute-start | bytes 258056 | tf_op jit(solution)/shard_map/ppermute | solution.py:501
  26.9 1.3 %copy-done.9 = f32[50,48,128]{2,1,0:T(8,128)S(1)} copy-done((f32[50,48,128]{2,1,0:T(8,128)S(1)}, f32[50,48,128]{2,1,0:T(8,128)}, u32[]{:S(2)}) %copy-start.9) | copy-done | bytes 1228824
  28.1 2.2 %base.1.rest_7_.q = f32[50,48,128]{2,1,0:T(8,128)} custom-call(f32[50,48,128]{2,1,0:T(8,128)S(1)} %copy-done.9, f32[2,50,48,128]{3,2,1,0:T(8,128)S(1)} %copy-done.1, f32[168,128]{1,0:T(8,128)S(1)} %mix.1.after), custom_call_target="tpu_custom_call" | custom-call | flops 10000000 | bytes 12000000 | tf_op jit(solution)/shard_map/base/pallas_call | solution.py:572
  30.3 23.8 %collective-permute-done.5.rest_0_ = f32[168,128]{1,0:T(8,128)S(1)} collective-permute-done((f32[168,128]{1,0:T(8,128)S(1)}, f32[168,128]{1,0:T(8,128)S(1)}, u32[]{:S(2)}, u32[]{:S(2)}) %collective-permute-start.5) | collective-permute-done | bytes 86048 | tf_op jit(solution)/shard_map/ppermute | solution.py:501
  54.1 1.3 %copy-done = f32[50,48,128]{2,1,0:T(8,128)S(1)} copy-done((f32[50,48,128]{2,1,0:T(8,128)S(1)}, f32[50,48,128]{2,1,0:T(8,128)}, u32[]{:S(2)}) %copy-start) | copy-done | bytes 1228824
  55.4 6.7 %nest.1 = (f32[50,24,128]{2,1,0:T(8,128)S(1)}, f32[112,128]{1,0:T(8,128)S(1)}, f32[112,128]{1,0:T(8,128)S(1)}, f32[24,128]{1,0:T(8,128)S(1)}, f32[24,128]{1,0:T(8,128)S(1)}, /*index=5*/f32[16,128]{1,0:T(8,128)S(1)}) custom-call(s32[1]{0:T(128)S(6)} %copy.15.o_row, s32[1]{0:T(128)S(6)} %copy.16.o_col, f32[50,24,128]{2,1,0:T(8,128)S(1)} %copy-done.6, ...), custom_call_target="tpu_custom_call" | custom-call | tf_op jit(solution)/shard_map/nest/pallas_call | solution.py:583
  62.1 1.9 %collective-permute-start.13 = (f32[112,128]{1,0:T(8,128)S(1)}, f32[112,128]{1,0:T(8,128)S(1)}, u32[]{:S(2)}, u32[]{:S(2)}) collective-permute-start(f32[112,128]{1,0:T(8,128)S(1)} %get-tuple-element.23), channel_id=1, source_target_pairs={{32,0},{64,32},{96,64},{128,96},{160,128},{192,160},{224,192},{33,... | collective-permute-start | bytes 172040 | tf_op jit(solution)/shard_map/ppermute | solution.py:506
  64.0 4.5 %collective-permute-start.12 = (f32[112,128]{1,0:T(8,128)S(1)}, f32[112,128]{1,0:T(8,128)S(1)}, u32[]{:S(2)}, u32[]{:S(2)}) collective-permute-start(f32[112,128]{1,0:T(8,128)S(1)} %get-tuple-element.22), channel_id=1, source_target_pairs={{0,128},{1,129},{2,130},{3,131},{4,132},{5,133},{6,134},{7,135},{8... | collective-permute-start | bytes 172040 | tf_op jit(solution)/shard_map/ppermute | solution.py:501
  68.5 1.2 %collective-permute-done.12.down = f32[112,128]{1,0:T(8,128)S(1)} collective-permute-done((f32[112,128]{1,0:T(8,128)S(1)}, f32[112,128]{1,0:T(8,128)S(1)}, u32[]{:S(2)}, u32[]{:S(2)}) %collective-permute-start.12) | collective-permute-done | bytes 57376 | tf_op jit(solution)/shard_map/ppermute | solution.py:501
  69.9 20.7 %all_to_all.10.across = f32[32,80,128]{2,1,0:T(8,128)S(1)} all-to-all(f32[32,80,128]{2,1,0:T(8,128)S(1)} %spread.1), channel_id=1, replica_groups=mesh['gy'=8,'gx'=32] {'gx'}, dimensions={0} | all-to-all | bytes 2621440 | tf_op jit(solution)/shard_map/all_to_all | solution.py:609
  91.3 7.0 %all-to-all-start.1 = ((f32[8,32,128]{2,1,0:T(8,128)}), f32[8,32,128]{2,1,0:T(8,128)S(1)}, u32[]{:S(2)}, u32[]{:S(2)}) async-start(f32[8,32,128]{2,1,0:T(8,128)} %turn.1), calls=%async_computation.1 | async-start | bytes 262144 | tf_op jit(solution)/shard_map/all_to_all | solution.py:613
  98.3 1.3 %collective-permute-start.14 = (f32[50,128]{1,0:T(8,128)S(1)}, f32[50,128]{1,0:T(8,128)S(1)}, u32[]{:S(2)}, u32[]{:S(2)}) collective-permute-start(f32[50,128]{1,0:T(8,128)S(1)} %slice.3), channel_id=1, source_target_pairs={{0,32},{1,33},{2,34},{3,35},{4,36},{5,37},{6,38},{7,39},{8,40},{9,... | collective-permute-start | bytes 76808 | tf_op jit(solution)/shard_map/ppermute | solution.py:501
  99.6 1.8 %collective-permute-done.14.third = f32[50,128]{1,0:T(8,128)S(1)} collective-permute-done((f32[50,128]{1,0:T(8,128)S(1)}, f32[50,128]{1,0:T(8,128)S(1)}, u32[]{:S(2)}, u32[]{:S(2)}) %collective-permute-start.14) | collective-permute-done | bytes 25632 | tf_op jit(solution)/shard_map/ppermute | solution.py:501
  101.3 5.0 %all-to-all-done.1.sides = f32[8,32,128]{2,1,0:T(8,128)S(1)} async-done(((f32[8,32,128]{2,1,0:T(8,128)}), f32[8,32,128]{2,1,0:T(8,128)S(1)}, u32[]{:S(2)}, u32[]{:S(2)}) %all-to-all-start.1) | async-done | bytes 131104 | tf_op jit(solution)/shard_map/all_to_all | solution.py:613
  106.4 1.7 %copy-done.2 = f32[2,50,48,128]{3,2,1,0:T(8,128)S(1)} copy-done((f32[2,50,48,128]{3,2,1,0:T(8,128)S(1)}, f32[2,50,48,128]{3,2,1,0:T(8,128)}, u32[]{:S(2)}) %copy-start.2) | copy-done | bytes 2457624
  108.1 1.3 %copy-done.5 = f32[2,50,24,128]{3,2,1,0:T(8,128)S(1)} copy-done((f32[2,50,24,128]{3,2,1,0:T(8,128)S(1)}, f32[2,50,24,128]{3,2,1,0:T(8,128)}, u32[]{:S(2)}) %copy-start.5) | copy-done | bytes 1228824
  109.4 1.1 copy-done.11
  110.4 2.3 %last.1 = (f32[50,24,128]{2,1,0:T(8,128)}, f32[50,48,128]{2,1,0:T(8,128)}, f32[2,50,2,64]{3,2,1,0:T(2,128)}, f32[2,50,2,64]{3,2,1,0:T(2,128)}) custom-call(s32[1]{0:T(128)S(6)} %copy.15.o_row, s32[1]{0:T(128)S(6)} %copy.16.o_col, f32[50,24,128]{2,1,0:T(8,128)S(1)} %copy-done.11, f32[50,24,128]{2,1,0:T(8,128)S(1)} %copy-done.3, ...), custom_call_target="tpu_custom_call", output_to_operand_aliasing={{1}: (13, {})} | custom-call | tf_op jit(solution)/shard_map/last/pallas_call | solution.py:615
  (38 shorter events, 1.9 us)
Async XLA Ops:
  0.6 2.1 %copy-start.3 = (f32[50,24,128]{2,1,0:T(8,128)S(1)}, f32[50,24,128]{2,1,0:T(8,128)}, u32[]{:S(2)}) copy-start(f32[50,24,128]{2,1,0:T(8,128)} %nu.5) | copy-start | bytes 1843204
  0.6 2.1 %copy-start.6 = (f32[50,24,128]{2,1,0:T(8,128)S(1)}, f32[50,24,128]{2,1,0:T(8,128)}, u32[]{:S(2)}) copy-start(f32[50,24,128]{2,1,0:T(8,128)} %a.3) | copy-start | bytes 1843204
  2.0 24.8 %copy-start.1 = (f32[2,50,48,128]{3,2,1,0:T(8,128)S(1)}, f32[2,50,48,128]{3,2,1,0:T(8,128)}, u32[]{:S(2)}) copy-start(f32[2,50,48,128]{3,2,1,0:T(8,128)} %pkappa.3) | copy-start | bytes 7372804
  2.8 0.9 copy-start.7
  3.7 0.7 copy-start.12
  4.8 16.5 %collective-permute-start = (f32[224,128]{1,0:T(8,128)S(1)}, f32[224,128]{1,0:T(8,128)S(1)}, u32[]{:S(2)}, u32[]{:S(2)}) collective-permute-start(f32[224,128]{1,0:T(8,128)S(1)} %get-tuple-element.14), channel_id=1, source_target_pairs={{0,32},{32,64},{64,96},{96,128},{128,160},{160,192},{192,224},{1,3... | collective-permute-start | bytes 344072 | tf_op jit(solution)/shard_map/ppermute | solution.py:506
  11.1 10.2 %collective-permute-start.1 = (f32[224,128]{1,0:T(8,128)S(1)}, f32[224,128]{1,0:T(8,128)S(1)}, u32[]{:S(2)}, u32[]{:S(2)}) collective-permute-start(f32[224,128]{1,0:T(8,128)S(1)} %get-tuple-element.15), channel_id=1, source_target_pairs={{32,0},{64,32},{96,64},{128,96},{160,128},{192,160},{224,192},{33,... | collective-permute-start | bytes 344072 | tf_op jit(solution)/shard_map/ppermute | solution.py:506
  13.0 8.2 %collective-permute-start.4 = (f32[168,128]{1,0:T(8,128)S(1)}, f32[168,128]{1,0:T(8,128)S(1)}, u32[]{:S(2)}, u32[]{:S(2)}) collective-permute-start(f32[168,128]{1,0:T(8,128)S(1)} %copy-done.7), channel_id=1, source_target_pairs={{144,208},{145,209},{146,210},{147,211},{148,212},{149,213},{150,2... | collective-permute-start | bytes 258056 | tf_op jit(solution)/shard_map/ppermute | solution.py:501
  13.7 4.4 %collective-permute-start.2 = (f32[24,128]{1,0:T(8,128)S(1)}, f32[24,128]{1,0:T(8,128)S(1)}, u32[]{:S(2)}, u32[]{:S(2)}) collective-permute-start(f32[24,128]{1,0:T(8,128)S(1)} %get-tuple-element.16), channel_id=1, source_target_pairs={{0,1},{1,2},{2,3},{3,4},{4,5},{5,6},{6,7},{7,8},{8,9},{9,10},{10,1... | collective-permute-start | bytes 36872 | tf_op jit(solution)/shard_map/ppermute | solution.py:506
  16.8 4.4 %collective-permute-start.3 = (f32[24,128]{1,0:T(8,128)S(1)}, f32[24,128]{1,0:T(8,128)S(1)}, u32[]{:S(2)}, u32[]{:S(2)}) collective-permute-start(f32[24,128]{1,0:T(8,128)S(1)} %get-tuple-element.17), channel_id=1, source_target_pairs={{1,0},{2,1},{3,2},{4,3},{5,4},{6,5},{7,6},{8,7},{9,8},{10,9},{11,1... | collective-permute-start | bytes 36872 | tf_op jit(solution)/shard_map/ppermute | solution.py:506
  21.3 32.8 %copy-start.13 = (s32[24,128]{1,0:T(8,128)S(1)}, s32[24,128]{1,0:T(8,128)}, u32[]{:S(2)}) copy-start(s32[24,128]{1,0:T(8,128)} %mask.5) | copy-start | bytes 36868
  21.3 32.8 %copy-start.4 = (f32[2,50,24,128]{3,2,1,0:T(8,128)S(1)}, f32[2,50,24,128]{3,2,1,0:T(8,128)}, u32[]{:S(2)}) copy-start(f32[2,50,24,128]{3,2,1,0:T(8,128)} %kappa.3) | copy-start | bytes 3686404
  21.3 3.5 %collective-permute-start.11 = (f32[168,128]{1,0:T(8,128)S(1)}, f32[168,128]{1,0:T(8,128)S(1)}, u32[]{:S(2)}, u32[]{:S(2)}) collective-permute-start(f32[168,128]{1,0:T(8,128)S(1)} %mix.1.after), channel_id=1, source_target_pairs={{146,2},{178,226},{147,5},{179,229},{148,8},{180,232},{149,11},{18... | collective-permute-start | bytes 258056 | tf_op jit(solution)/shard_map/ppermute | solution.py:501
  22.1 3.4 %collective-permute-start.10 = (f32[168,128]{1,0:T(8,128)S(1)}, f32[168,128]{1,0:T(8,128)S(1)}, u32[]{:S(2)}, u32[]{:S(2)}) collective-permute-start(f32[168,128]{1,0:T(8,128)S(1)} %mix.1.after), channel_id=1, source_target_pairs={{145,2},{177,226},{146,5},{178,229},{147,8},{179,232},{148,11},{18... | collective-permute-start | bytes 258056 | tf_op jit(solution)/shard_map/ppermute | solution.py:501
  22.8 7.5 %collective-permute-start.9 = (f32[168,128]{1,0:T(8,128)S(1)}, f32[168,128]{1,0:T(8,128)S(1)}, u32[]{:S(2)}, u32[]{:S(2)}) collective-permute-start(f32[168,128]{1,0:T(8,128)S(1)} %mix.1.after), channel_id=1, source_target_pairs={{145,1},{177,225},{146,4},{178,228},{147,7},{179,231},{148,10},{18... | collective-permute-start | bytes 258056 | tf_op jit(solution)/shard_map/ppermute | solution.py:501
  23.5 6.8 %collective-permute-start.8 = (f32[168,128]{1,0:T(8,128)S(1)}, f32[168,128]{1,0:T(8,128)S(1)}, u32[]{:S(2)}, u32[]{:S(2)}) collective-permute-start(f32[168,128]{1,0:T(8,128)S(1)} %mix.1.after), channel_id=1, source_target_pairs={{145,0},{177,224},{146,3},{178,227},{147,6},{179,230},{148,9},{180... | collective-permute-start | bytes 258056 | tf_op jit(solution)/shard_map/ppermute | solution.py:501
  24.2 6.1 %collective-permute-start.7 = (f32[168,128]{1,0:T(8,128)S(1)}, f32[168,128]{1,0:T(8,128)S(1)}, u32[]{:S(2)}, u32[]{:S(2)}) collective-permute-start(f32[168,128]{1,0:T(8,128)S(1)} %mix.1.after), channel_id=1, source_target_pairs={{144,2},{176,226},{145,5},{177,229},{146,8},{178,232},{147,11},{17... | collective-permute-start | bytes 258056 | tf_op jit(solution)/shard_map/ppermute | solution.py:501
  24.9 5.5 %collective-permute-start.6 = (f32[168,128]{1,0:T(8,128)S(1)}, f32[168,128]{1,0:T(8,128)S(1)}, u32[]{:S(2)}, u32[]{:S(2)}) collective-permute-start(f32[168,128]{1,0:T(8,128)S(1)} %mix.1.after), channel_id=1, source_target_pairs={{144,1},{176,225},{145,4},{177,228},{146,7},{178,231},{147,10},{17... | collective-permute-start | bytes 258056 | tf_op jit(solution)/shard_map/ppermute | solution.py:501
  25.5 28.6 %collective-permute-start.5 = (f32[168,128]{1,0:T(8,128)S(1)}, f32[168,128]{1,0:T(8,128)S(1)}, u32[]{:S(2)}, u32[]{:S(2)}) collective-permute-start(f32[168,128]{1,0:T(8,128)S(1)} %mix.1.after), channel_id=1, source_target_pairs={{144,0},{176,224},{145,3},{177,227},{146,6},{178,230},{147,9},{179... | collective-permute-start | bytes 258056 | tf_op jit(solution)/shard_map/ppermute | solution.py:501
  26.8 1.3 %copy-start.9 = (f32[50,48,128]{2,1,0:T(8,128)S(1)}, f32[50,48,128]{2,1,0:T(8,128)}, u32[]{:S(2)}) copy-start(f32[50,48,128]{2,1,0:T(8,128)} %q.1) | copy-start | bytes 3686404
  54.1 1.3 %copy-start = (f32[50,48,128]{2,1,0:T(8,128)S(1)}, f32[50,48,128]{2,1,0:T(8,128)}, u32[]{:S(2)}) copy-start(f32[50,48,128]{2,1,0:T(8,128)} %base.1.rest_7_.q) | copy-start | bytes 3686404
  62.1 28.6 %copy-start.10 = (f32[50,24,128]{2,1,0:T(8,128)}, f32[50,24,128]{2,1,0:T(8,128)S(1)}, u32[]{:S(2)}) copy-start(f32[50,24,128]{2,1,0:T(8,128)S(1)} %get-tuple-element.18.a) | copy-start | bytes 1843204
  62.1 6.5 %collective-permute-start.13 = (f32[112,128]{1,0:T(8,128)S(1)}, f32[112,128]{1,0:T(8,128)S(1)}, u32[]{:S(2)}, u32[]{:S(2)}) collective-permute-start(f32[112,128]{1,0:T(8,128)S(1)} %get-tuple-element.23), channel_id=1, source_target_pairs={{32,0},{64,32},{96,64},{128,96},{160,128},{192,160},{224,192},{33,... | collective-permute-start | bytes 172040 | tf_op jit(solution)/shard_map/ppermute | solution.py:506
  64.0 5.8 %collective-permute-start.12 = (f32[112,128]{1,0:T(8,128)S(1)}, f32[112,128]{1,0:T(8,128)S(1)}, u32[]{:S(2)}, u32[]{:S(2)}) collective-permute-start(f32[112,128]{1,0:T(8,128)S(1)} %get-tuple-element.22), channel_id=1, source_target_pairs={{0,128},{1,129},{2,130},{3,131},{4,132},{5,133},{6,134},{7,135},{8... | collective-permute-start | bytes 172040 | tf_op jit(solution)/shard_map/ppermute | solution.py:501
  90.6 15.8 %copy-start.8 = (f32[168,128]{1,0:T(8,128)S(1)}, f32[168,128]{1,0:T(8,128)}, u32[]{:S(2)}) copy-start(f32[168,128]{1,0:T(8,128)} %panel.1.pay) | copy-start | bytes 258052
  91.3 15.1 %all-to-all-start.1 = ((f32[8,32,128]{2,1,0:T(8,128)}), f32[8,32,128]{2,1,0:T(8,128)S(1)}, u32[]{:S(2)}, u32[]{:S(2)}) async-start(f32[8,32,128]{2,1,0:T(8,128)} %turn.1), calls=%async_computation.1 | async-start | bytes 262144 | tf_op jit(solution)/shard_map/all_to_all | solution.py:613
  98.3 3.1 %collective-permute-start.14 = (f32[50,128]{1,0:T(8,128)S(1)}, f32[50,128]{1,0:T(8,128)S(1)}, u32[]{:S(2)}, u32[]{:S(2)}) collective-permute-start(f32[50,128]{1,0:T(8,128)S(1)} %slice.3), channel_id=1, source_target_pairs={{0,32},{1,33},{2,34},{3,35},{4,36},{5,37},{6,38},{7,39},{8,40},{9,... | collective-permute-start | bytes 76808 | tf_op jit(solution)/shard_map/ppermute | solution.py:501
  106.4 1.7 %copy-start.2 = (f32[2,50,48,128]{3,2,1,0:T(8,128)S(1)}, f32[2,50,48,128]{3,2,1,0:T(8,128)}, u32[]{:S(2)}) copy-start(f32[2,50,48,128]{3,2,1,0:T(8,128)} %pkappa.3) | copy-start | bytes 7372804
  108.1 1.3 %copy-start.5 = (f32[2,50,24,128]{3,2,1,0:T(8,128)S(1)}, f32[2,50,24,128]{3,2,1,0:T(8,128)}, u32[]{:S(2)}) copy-start(f32[2,50,24,128]{3,2,1,0:T(8,128)} %kappa.3) | copy-start | bytes 3686404
  109.4 1.1 copy-start.11

commit v2 on v1

v2 whole, which is shorter than its diff:
```python
import jax
import jax.numpy as jnp
from jax import lax
from jax.experimental import pallas as pl
from jax.experimental.pallas import tpu as pltpu
from jax.sharding import PartitionSpec as P

R = 3
K = 50
NR = 24
PR = 48
L = 128
GY = 8
GX = 32
SR = 64
ROW0 = 192
COL0 = 2048
SOUTH = 4
WEST = 16
SPAN = 1366
F32 = jnp.float32
VM = pl.BlockSpec(memory_space=pltpu.VMEM)
SM = pl.BlockSpec(memory_space=pltpu.SMEM)
HB = pl.BlockSpec(memory_space=pltpu.HBM)
ANY = pl.BlockSpec(memory_space=pl.ANY)


def grant(mib):
    return pltpu.CompilerParams(vmem_limit_bytes=mib * 1024 * 1024)


TURNS = (0, 1, 2, -3, -2, -1, -4)
SEVENTH = ((WEST, 4), (WEST + 10, 2), (WEST + 11, 0))


def side_round(i, g):
    return jnp.where(g == GY - 1, SEVENTH[i][1], lax.rem((1, 3, 5)[i] + g, 7))


def exact(left, right):
    return lax.dot_general(
        left, right, (((1,), (0,)), ((), ())), precision=lax.Precision.HIGHEST, preferred_element_type=F32
    )


def exact_t(left, right):
    return lax.dot_general(
        left, right, (((1,), (1,)), ((), ())), precision=lax.Precision.HIGHEST, preferred_element_type=F32
    )


def iota(shape, dim):
    return lax.broadcasted_iota(jnp.int32, shape, dim)


def wide(col, rows):
    return jnp.broadcast_to(col, (rows, L))


def place(row, col):
    return lax.axis_index("gy"), lax.axis_index("gx"), row[0], col[0]


def side_lane(x, ox):
    west = ox - 1 - L * x
    east = ox + SPAN - L * x
    is_west = (west >= 0) & (west < L)
    is_east = (east >= 0) & (east < L)
    return is_west, is_east, jnp.where(is_west, west, east)


def ring_row(g, x, oy):
    row = jnp.where(g == SOUTH, oy - 1, oy + SR) - PR * g
    ok = (row >= 0) & (row < PR) & (g >= SOUTH) & (g < GY - 1) & (x >= WEST) & (x < WEST + 12)
    return ok, row


def threes(x, shape, dim):
    cell = L * lax.rem(x, 3) + iota(shape, dim)
    first = 3 * iota(shape, 1 - dim)
    return ((first <= cell) & (cell < first + 3)).astype(F32)


def row_sums(rows, x):
    col = x * L + iota(rows.shape, 1)
    return exact(jnp.where((col > 0) & (col < GX * L - 1), rows, 0.0), threes(x, (L, L), 0))


def edge_kernel(o_row, o_col, a, nu, mask, traj, to_up, to_down, v_left, v_right, pay, row_s, col_s, buf, sems):
    g, x, oy, ox = place(o_row, o_col)
    row_ok, row = ring_row(g, x, oy)
    is_west, is_east, spot = side_lane(x, ox)
    side_ok = (is_west | is_east) & (g >= SOUTH) & (g < GY - 1)
    tile = pl.multiple_of(8 * (row // 8), 8)

    def row_copy():
        return pltpu.make_async_copy(traj.at[:, :, pl.ds(tile, 8), :], row_s, sems.at[2])

    def col_copy(s):
        return pltpu.make_async_copy(traj.at[s], col_s.at[s], sems.at[s])

    @pl.when(side_ok)
    def _():
        col_copy(1).start()
        col_copy(0).start()

    @pl.when(row_ok)
    def _():
        row_copy().start()

    m = mask[...].astype(F32)
    lane = iota((NR, L), 1)
    acc_l = jnp.zeros((NR, L), F32)
    acc_r = jnp.zeros((NR, L), F32)
    for k in range(K):
        v = nu[k] * m * a[k]
        to_up[pl.ds(k, 1), :] = v[0:1]
        to_down[pl.ds(k, 1), :] = v[NR - 1 : NR]
        acc_l = jnp.where(lane == k, pltpu.roll(v, k, 1) if k else v, acc_l)
        acc_r = jnp.where(lane == k, pltpu.roll(v, k + 1, 1), acc_r)
    v_left[...] = acc_l
    v_right[...] = acc_r
    pay[...] = jnp.zeros(pay.shape, F32)

    @pl.when(row_ok)
    def _():
        row_copy().wait()
        for i, s in enumerate((1, 0)):
            for k in range(K):
                pay[pl.ds(K * i + k, 1), :] = jax.nn.sigmoid(row_s[s, k, pl.ds(row - tile, 1), :])

    @pl.when(side_ok)
    def _():
        plane = iota((PR, L), 1)
        acc = jnp.zeros((PR, L), F32)
        for i, s in enumerate((1, 0)):
            col_copy(s).wait()
            for k in range(K):
                to = 64 * i + k
                acc = jnp.where(plane == to, pltpu.roll(col_s[s, k], lax.rem(to - spot + L, L), 1), acc)
        used = (plane < K) | ((plane >= 64) & (plane < 64 + K))
        buf[...] = jnp.zeros(buf.shape, F32)
        start = PR * g - oy + SR
        weights = jnp.where(used, jax.nn.sigmoid(acc), 0.0)
        for r in range(PR):
            buf[pl.ds(start + r, 1), :] = weights[r : r + 1]
        pay[104:168, :] = buf[SR : 2 * SR, :]

    for to in (to_up, to_down):
        to[K:56, :] = jnp.zeros((56 - K, L), F32)
    to_down[56:120, :] = pay[104:168, :]


def mix_kernel(o_col, pay, down, skip, after_left, after_right, *outs):
    g, x = lax.axis_index("gy"), lax.axis_index("gx")
    sig = o_col[0] - COL0
    own = pay[0:104, :] + jnp.where(g == 5, skip[0:104, :], 0.0)
    sides = pay[104:168, :] + down[56:120, :] + skip[104:168, :]
    lane = iota((K, L), 1)
    spare = jnp.zeros((64 - K, L), F32)
    for i, (t, out) in enumerate(zip(TURNS, outs)):
        begin = (0, 42, 85)[t % 3] - 1 + L * (t // 3) + sig
        turn = lax.rem(4 * L - begin, L)
        cell = begin + lane
        one = jnp.where((lane < 48) & (cell >= 0) & (cell < L), pltpu.roll(own[0:K], turn, 1), 0.0)
        cell = cell - 64
        two = jnp.where(
            (lane >= 64) & (lane < 112) & (cell >= 0) & (cell < L), pltpu.roll(own[K : 2 * K], lax.rem(turn + 64, L), 1), 0.0
        )
        part = jnp.concatenate([one + two, spare], 0)
        extra = g == 6
        for p, n in SEVENTH:
            extra = extra | ((g == 5) & (x == p) & (n == i))
        out[...] = jnp.where(extra, sides, part)


def base_kernel(o_row, o_col, q, pkappa, after, q_out, row_k, col_c, col_r, e_s, r_s):
    g, x, oy, ox = place(o_row, o_col)
    zero = jnp.zeros((PR, L), F32)
    src = q
    for step in (1, 0):
        c_prev, e_prev, y = zero, zero, zero
        for k in range(K):
            c = pkappa[step, k]
            r = 1.0 / (1.0 + c + c_prev * (1.0 - e_prev))
            e = c * r
            e_s[k] = e
            r_s[step, k] = r
            y = (src[k] + c_prev * y) * r
            q_out[k] = y
            c_prev, e_prev = c, e
        for k in range(K - 2, -1, -1):
            y = q_out[k] + e_s[k] * y
            q_out[k] = y
        src = q_out
    row_ok, row = ring_row(g, x, oy)
    is_west, is_east, spot = side_lane(x, ox)

    @pl.when(row_ok)
    def _():
        row_k[...] = pkappa[:, :, pl.ds(pl.multiple_of(8 * (row // 8), 8), 8), :]

    @pl.when(is_west | is_east)
    def _():
        lane = iota((PR, L), 1)
        for values, out in ((pkappa, col_c), (r_s, col_r)):
            acc = zero
            for i, s in enumerate((1, 0)):
                for k in range(K):
                    to = 64 * i + k
                    acc = jnp.where(lane == to, pltpu.roll(values[s, k], lax.rem(to - spot + L, L), 1), acc)
            out[...] = acc


def spread_kernel(side, v_left, v_right, down, up, after, out, one_s):
    x = lax.axis_index("gx")

    def packed(v):
        return v[0:12] + pltpu.roll(v[12:24], 64, 1)

    to_left, to_right = packed(v_left[...]), packed(v_right[...])
    one_s[0:K, :] = down[56 : 56 + K, :] + up[56 : 56 + K, :]
    one_s[K:62, :] = jnp.zeros((62 - K, L), F32)
    one_s[62:78, :] = side[...]
    one_s[78:80, :] = jnp.zeros((2, L), F32)
    every = one_s[...]
    for i in range(GX):
        out[i] = every

    @pl.when(x > 0)
    def _():
        out[jnp.maximum(x - 1, 0), K:62, :] = to_left

    @pl.when(x < GX - 1)
    def _():
        out[jnp.minimum(x + 1, GX - 1), K:62, :] = to_right


def turn_kernel(across, out):
    west, east = across[0, 62:78], across[GX - 1, 62:78]
    for i in range(GY):
        out[i, 0:16] = west
        out[i, 16:32] = east


def first_lane(t):
    return jnp.where(t == 0, 0, jnp.where(t == 1, 42, 85))


def nest_kernel(
    o_row, o_col, a, nu, mask, kappa, h_up, h_down, h_left, h_right, *rest,
):
    parts = rest[:7]
    a_out, to_up, to_down, v_left, v_right, side, e_s, y_s, w_s, up_s, down_s, g_s, we_s, w24_s = rest[8:]
    g, x, oy, ox = place(o_row, o_col)
    t = lax.rem(x, 3)
    def pick(i):
        got = jnp.where(t == 0, parts[i][...], parts[i + 1][...])
        return jnp.where(t == 2, parts[i + 2][...], got)

    window = (pick(0) + pick(3) + jnp.where(t == 2, parts[6][...], 0.0))[0:56]
    wl = iota((56, L), 1)
    low = wl < 64
    panel = jnp.concatenate([jnp.where(low, window, 0.0), jnp.where(low, pltpu.roll(window, 64, 1), 0.0)], 0)
    shift = first_lane(t) - 1
    si, sc = iota((L, L), 0) + shift, L * t + iota((L, L), 1)
    spread = ((3 * si <= sc) & (sc < 3 * si + 3)).astype(F32)
    c_all = x * L + iota((112, L), 1)
    inner = (c_all > 0) & (c_all < GX * L - 1) & ((g == 0) | (g == GY - 1))
    w_s[...] = jnp.where(inner, exact(panel, spread), 0.0)

    er, el = iota((8, L), 0), iota((8, L), 1)
    want = jnp.where(er == 0, jnp.where(t == 0, 0, 1), jnp.where(er == 1, jnp.where(t == 0, 43, 44), -1))
    ends = exact_t((el == want).astype(F32), panel[0:56])

    row24, lane24 = iota((NR, L), 0), iota((NR, L), 1)
    m_row = (((row24 == 0) & (g == 0)) | ((row24 == NR - 1) & (g == GY - 1))).astype(F32)
    m_lane = (((lane24 == 0) & (x == 0)) | ((lane24 == L - 1) & (x == GX - 1))).astype(F32)
    ends_l = jnp.concatenate([ends[0:1], jnp.zeros((1, L - 56), F32)], 1)
    ends_r = jnp.concatenate([ends[1:2], jnp.zeros((1, L - 56), F32)], 1)
    hl = h_left[...] * (1.0 - m_row * wide(ends_l, NR))
    hr = h_right[...] * (1.0 - m_row * wide(ends_r, NR))

    panel_we = jnp.zeros((SR, L), F32)
    for i, part in enumerate(parts):
        come = ((x == 0) & (side_round(0, g) == i)) | (
            (x == GX - 1) & ((side_round(1, g) == i) | (side_round(2, g) == i))
        )
        panel_we = panel_we + jnp.where(come, part[...], 0.0)
    we_s[...] = panel_we
    mine = we_s[pl.ds(pl.multiple_of(8 * g, 8), 8), :]
    for i in range(8):
        w24_s[3 * i : 3 * i + 3, :] = jnp.broadcast_to(mine[i : i + 1], (3, L))
    w_we = w24_s[...]
    flip = jnp.concatenate([panel_we, jnp.zeros((SR, L), F32)], 0).T[0:56]
    spot = jnp.where(x == 0, 0, L - 1)
    lane56 = iota((56, L), 1)
    edge = (lane56 == spot) & ((x == 0) | (x == GX - 1))
    w_up = jnp.where(edge & (g > 0), pltpu.roll(flip, lax.rem(spot - (8 * g - 1) + L, L), 1), 0.0)
    w_down = jnp.where(edge & (g < GY - 1), pltpu.roll(flip, lax.rem(spot - (8 * g + 8) + L, L), 1), 0.0)
    up_s[...] = h_up[0:K, :] * (1.0 - w_up[0:K])
    down_s[...] = h_down[0:K, :] * (1.0 - w_down[0:K])

    m = mask[...].astype(F32)
    one = jnp.ones((NR, L), F32)
    zero = jnp.zeros((NR, L), F32)
    c_prev, e_prev, y = zero, zero, zero
    top = g == 0
    is31 = (x == GX - 1).astype(jnp.int32)
    for k in range(K):
        w_row = w_s[pl.ds(k, 1), :]
        raw = a[k]
        g_s[pl.ds(k, 1), :] = jnp.where(top, raw[0:1], raw[NR - 1 : NR])
        now = raw * (one - (m_row * wide(w_row, NR) + m_lane * wide(w_we[:, k : k + 1], NR)))
        v = nu[k] * m * now
        above = jnp.where(row24 == 0, wide(up_s[pl.ds(k, 1), :], NR), pltpu.roll(v, 1, 0))
        below = jnp.where(row24 == NR - 1, wide(down_s[pl.ds(k, 1), :], NR), pltpu.roll(v, NR - 1, 0))
        left = jnp.where(lane24 == 0, wide(hl[:, k : k + 1], NR), pltpu.roll(v, 1, 1))
        right = jnp.where(lane24 == L - 1, wide(hr[:, k : k + 1], NR), pltpu.roll(v, L - 1, 1))
        b = m * (now + (above + below + left + right - 4.0 * v))
        c = kappa[1, k]
        r = 1.0 / (1.0 + c + c_prev * (1.0 - e_prev))
        e = c * r
        y = (b + c_prev * y) * r
        e_s[k] = e
        y_s[k] = y
        c_prev, e_prev = c, e
    sol = zero
    acc_l, acc_r = zero, zero
    for k in range(K - 1, -1, -1):
        sol = y_s[k] + e_s[k] * sol if k < K - 1 else y_s[k]
        y_s[k] = sol
        w_row = w_s[pl.ds(56 + k, 1), :]
        g_s[pl.ds(56 + k, 1), :] = jnp.where(top, sol[0:1], sol[NR - 1 : NR])
        now = sol * (one - (m_row * wide(w_row, NR) + m_lane * wide(w_we[:, 64 + k : 65 + k], NR)))
        a_out[k] = now
        v = nu[k] * m * now
        to_up[pl.ds(k, 1), :] = v[0:1]
        to_down[pl.ds(k, 1), :] = v[NR - 1 : NR]
        acc_l = jnp.where(lane24 == k, pltpu.roll(v, k, 1) if k else v, acc_l)
        acc_r = jnp.where(lane24 == k, pltpu.roll(v, k + 1, 1), acc_r)
    v_left[...] = acc_l
    v_right[...] = acc_r
    for i in (*range(K, 56), *range(56 + K, 112)):
        g_s[pl.ds(i, 1), :] = jnp.zeros((1, L), F32)
    sums = row_sums(g_s[...], x)
    sums = pltpu.roll(sums, lax.rem(L - first_lane(t), L), 1)
    sums = sums[0:56] + pltpu.roll(sums[56:112], 64, 1)
    sums = jnp.where((g == 0) | (g == GY - 1), sums, 0.0)
    for to in (to_up, to_down):
        to[K:56, :] = jnp.zeros((56 - K, L), F32)
        to[56:112, :] = sums

    side[...] = jnp.zeros(side.shape, F32)

    @pl.when((x == 0) | (x == GX - 1))
    def _():
        acc = zero
        for k in range(K):
            acc = jnp.where(lane24 == k, pltpu.roll(a[k], lax.rem(k + is31, L), 1), acc)
            acc = jnp.where(lane24 == 64 + k, pltpu.roll(y_s[k], lax.rem(64 + k + is31, L), 1), acc)
        w24_s[...] = w_we * acc
        side[0:8, :] = w24_s[pl.ds(0, 8, 3), :] + w24_s[pl.ds(1, 8, 3), :] + w24_s[pl.ds(2, 8, 3), :]
        side[8:16, :] = mine


def inner_kernel(
    o_row, o_col, a, nu, mask, kappa, across, down, up, third, pay, row_k, q,
    a_out, q_out,
    e_s, g_s, t_s, up_s, tile_s, fact_s, sem,
):
    g, x, oy, ox = place(o_row, o_col)
    row_ok, row = ring_row(g, x, oy)
    tile = pl.multiple_of(8 * (row // 8), 8)
    at = pl.ds(tile, 8)

    def tile_copy():
        return pltpu.make_async_copy(q.at[:, at, :], tile_s, sem)

    @pl.when(row_ok)
    def _():
        tile_copy().start()

    m = mask[...].astype(F32)
    row24, lane24 = iota((NR, L), 0), iota((NR, L), 1)

    def unpacked(p):
        return jnp.concatenate([p, pltpu.roll(p, 64, 1)], 0)

    hl = jnp.where(x > 0, unpacked(across[jnp.maximum(x - 1, 0), K:62]), 0.0)
    hr = jnp.where(x < GX - 1, unpacked(across[jnp.minimum(x + 1, GX - 1), K:62]), 0.0)
    up_s[...] = third[...] + jnp.where((g == 4) | (g == 5), 0.0, down[0:K, :])
    zero = jnp.zeros((NR, L), F32)
    c_prev, e_prev, y = zero, zero, zero
    for k in range(K):
        now = a[k]
        v = nu[k] * m * now
        above = jnp.where(row24 == 0, wide(up_s[pl.ds(k, 1), :], NR), pltpu.roll(v, 1, 0))
        below = jnp.where(row24 == NR - 1, wide(up[pl.ds(k, 1), :], NR), pltpu.roll(v, NR - 1, 0))
        left = jnp.where(lane24 == 0, wide(hl[:, k : k + 1], NR), pltpu.roll(v, 1, 1))
        right = jnp.where(lane24 == L - 1, wide(hr[:, k : k + 1], NR), pltpu.roll(v, L - 1, 1))
        b = m * (now + (above + below + left + right - 4.0 * v))
        c = kappa[0, k]
        r = 1.0 / (1.0 + c + c_prev * (1.0 - e_prev))
        e = c * r
        y = (b + c_prev * y) * r
        e_s[k] = e
        a_out[k] = y
        c_prev, e_prev = c, e
    for k in range(K - 2, -1, -1):
        y = a_out[k] + e_s[k] * y
        a_out[k] = y

    @pl.when(row_ok)
    def _():
        sig = ox - COL0
        turn = lax.rem(sig, L)
        low = iota((56, L), 1) < 64

        def come(base):
            first = jnp.zeros((56, L), F32)
            second = jnp.zeros((56, L), F32)
            for t in range(3):
                j = 3 * base + t
                got = jnp.where((j >= 0) & (j < GX), across[jnp.clip(j, 0, GX - 1), 0:56], 0.0)
                one = jnp.where(low, got, 0.0)
                two = jnp.where(low, pltpu.roll(got, 64, 1), 0.0)
                start = (0, 42, 85)[t]
                first = first + (pltpu.roll(one, start, 1) if t else one)
                second = second + (pltpu.roll(two, start, 1) if t else two)
            return first, second

        def on_parent(own, prev):
            return jnp.where(iota(own.shape, 1) >= sig, pltpu.roll(own, turn, 1), pltpu.roll(prev, turn, 1))

        own, prev = come(x - WEST), come(x - WEST - 1)
        g_s[0:56, :] = on_parent(own[0], prev[0]) * pay[0:56, :]
        g_s[K : 2 * K, :] = on_parent(own[1], prev[1])[0:K] * pay[K : 2 * K, :]
        here = iota((8, L), 0) == row - tile
        zero = jnp.zeros((8, L), F32)
        for step in (1, 0):
            c_prev, e_prev, y = zero, zero, zero
            for k in range(K):
                c = row_k[step, k]
                r = 1.0 / (1.0 + c + c_prev * (1.0 - e_prev))
                e = c * r
                fact_s[k] = e
                term = jnp.where(here, wide(g_s[pl.ds(k if step else K + k, 1), :], 8), 0.0)
                y = ((term if step else term + t_s[k]) + c_prev * y) * r
                t_s[k] = y
                c_prev, e_prev = c, e
            for k in range(K - 2, -1, -1):
                y = t_s[k] + fact_s[k] * y
                t_s[k] = y
        tile_copy().wait()
        t_s[...] = t_s[...] + tile_s[...]
        back = pltpu.make_async_copy(t_s, q_out.at[:, at, :], sem)
        back.start()
        back.wait()


def outer_kernel(o_row, o_col, sides, col_c, col_r, q, q_out, s_w, s_g, panel_s, local_s, d_s, q_s, sems):
    g, x, oy, ox = place(o_row, o_col)
    is_west, is_east, spot = side_lane(x, ox)
    side_ok = (is_west | is_east) & (g >= SOUTH) & (g < GY - 1)

    def whole_copy():
        return pltpu.make_async_copy(q, q_s, sems.at[0])

    @pl.when(side_ok)
    def _():
        whole_copy().start()

    def panels(first):
        return jnp.concatenate([sides[i, 16 * e + first : 16 * e + first + 8, :] for e in (0, 1) for i in range(GY)], 0)

    grads = panels(0)
    flip_g = grads.T
    flip_w = panels(8).T
    for i, s in enumerate((1, 0)):
        for e in (0, 1):
            s_g[s, :, e, :] = flip_g[64 * i : 64 * i + K, SR * e : SR * e + SR]
            s_w[s, :, e, :] = flip_w[64 * i : 64 * i + K, SR * e : SR * e + SR]

    @pl.when(side_ok)
    def _():
        panel_s[...] = jnp.zeros(panel_s.shape, F32)
        panel_s[SR : 2 * SR, :] = jnp.where(is_west, grads[0:SR], grads[SR : 2 * SR])
        start = PR * g - oy + SR
        for r in range(PR):
            local_s[pl.ds(r, 1), :] = panel_s[pl.ds(start + r, 1), :]
        here = iota((PR, L), 1) == spot
        lane = iota((PR, L), 1)
        cs, rs = col_c[...], col_r[...]
        above = jnp.where((lane == 0) | (lane == 64), 0.0, pltpu.roll(cs, 1, 1)) * rs
        below = cs * rs
        own = local_s[...] * rs

        def column(values, i):
            return wide(values[:, i : i + 1], PR)

        zero = jnp.zeros((PR, L), F32)
        for step, first in ((1, 0), (0, 64)):
            y = zero
            for k in range(K):
                term = column(own, first + k)
                if step == 0:
                    term = term + d_s[k] * column(rs, first + k)
                y = term + column(above, first + k) * y
                d_s[k] = y
            if step == 1:
                for k in range(K - 2, -1, -1):
                    y = d_s[k] + column(below, first + k) * y
                    d_s[k] = y
        whole_copy().wait()
        d_s[K - 1] = jnp.where(here, y, 0.0) + q_s[K - 1]
        copies = []
        for k in range(K - 2, -1, -1):
            y = d_s[k] + column(below, 64 + k) * y
            d_s[k] = jnp.where(here, y, 0.0) + q_s[k]
            if k % 10 == 0:
                part = pl.ds(k, 10)
                copies.append(pltpu.make_async_copy(d_s.at[part], q_out.at[part], sems.at[1 + k // 10]))
                copies[-1].start()
        for copy in copies:
            copy.wait()


def shape(*dims):
    return jax.ShapeDtypeStruct(dims, F32)


def at(g, x):
    return g * GX + x


def moved(value, pairs):
    return lax.ppermute(value, ("gy", "gx"), pairs)


def shifted(value, axis, count, step):
    pairs = [(i, i + step) for i in range(count) if 0 <= i + step < count]
    return lax.ppermute(value, axis, pairs)


def panel_routes():
    routes = []
    for t in TURNS:
        pairs = []
        for p in range(WEST, WEST + 12):
            j = 3 * (p - WEST) + t
            if 0 <= j < GX:
                pairs += [(at(4, p), at(0, j)), (at(5, p), at(7, j))]
        routes.append(pairs)
    for p, e, first in ((WEST, 0, 1), (WEST + 10, GX - 1, 3), (WEST + 11, GX - 1, 5)):
        for k in range(GY - 1):
            routes[(first + k) % 7].append((at(6, p), at(k, e)))
    for p, n in SEVENTH:
        routes[n].append((at(5, p), at(7, 0 if p == WEST else GX - 1)))
    return routes


def on_device(nest_adjoint, nest_kappa, nest_nu, land_mask, parent_adjoint, parent_kappa, parent_traj, offset_row, offset_col):
    here = (offset_row, offset_col)
    to_up, to_down, v_left, v_right, pay = pl.pallas_call(
        edge_kernel,
        out_shape=(shape(56, L), shape(120, L), shape(NR, L), shape(NR, L), shape(168, L)),
        in_specs=[SM] * 2 + [VM] * 3 + [HB],
        out_specs=(VM,) * 5,
        scratch_shapes=[
            pltpu.VMEM((2, K, 8, L), F32), pltpu.VMEM((2, K, PR, L), F32), pltpu.VMEM((256, L), F32),
            pltpu.SemaphoreType.DMA((3,)),
        ],
        compiler_params=grant(60),
        name="edge",
    )(*here, nest_adjoint, nest_nu, land_mask, parent_traj)
    down = shifted(to_down, "gy", GY, 1)
    up = shifted(to_up, "gy", GY, -1)
    ring = range(WEST, WEST + 12)
    skip = moved(
        pay, [(at(6, p), at(5, p)) for p in ring] + [(at(4, p), at(6, p)) for p in (WEST, WEST + 10, WEST + 11)]
    )
    h_left = shifted(v_right, "gx", GX, 1)
    h_right = shifted(v_left, "gx", GX, -1)
    mixed = pl.pallas_call(
        mix_kernel,
        out_shape=(shape(SR, L),) * 7,
        in_specs=[SM] + [VM] * 3 + [ANY] * 2,
        out_specs=(VM,) * 7,
        compiler_params=grant(4),
        name="mix",
    )(offset_col, pay, down, skip, h_left, h_right)
    parts = [moved(message, pairs) for message, pairs in zip(mixed, panel_routes())]
    nest, parent = shape(K, NR, L), shape(K, PR, L)
    base, row_k, col_c, col_r = pl.pallas_call(
        base_kernel,
        out_shape=(parent, shape(2, K, 8, L), shape(PR, L), shape(PR, L)),
        in_specs=[SM] * 2 + [VM] * 2 + [ANY],
        out_specs=(VM,) * 4,
        scratch_shapes=[pltpu.VMEM((K, PR, L), F32), pltpu.VMEM((2, K, PR, L), F32)],
        compiler_params=grant(16),
        cost_estimate=pl.CostEstimate(flops=10000000, bytes_accessed=12000000, transcendentals=0),
        name="base",
    )(*here, parent_adjoint, parent_kappa, mixed[6])

    state, to_up, to_down, v_left, v_right, side = pl.pallas_call(
        nest_kernel,
        out_shape=(nest, shape(112, L), shape(112, L), shape(NR, L), shape(NR, L), shape(16, L)),
        in_specs=[SM] * 2 + [VM] * 15 + [ANY],
        out_specs=(VM,) * 6,
        scratch_shapes=[
            pltpu.VMEM((K, NR, L), F32), pltpu.VMEM((K, NR, L), F32), pltpu.VMEM((112, L), F32), pltpu.VMEM((K, L), F32),
            pltpu.VMEM((K, L), F32), pltpu.VMEM((112, L), F32), pltpu.VMEM((SR, L), F32),
            pltpu.VMEM((NR, L), F32),
        ],
        compiler_params=grant(12),
        name="nest",
    )(*here, nest_adjoint, nest_nu, land_mask, nest_kappa, down, up, h_left, h_right, *parts, col_c)

    rows = ((0, 4), (7, 5), (1, 2), (2, 3), (5, 6), (6, 7))
    down = moved(to_down, [(at(i, j), at(k, j)) for i, k in rows for j in range(GX)])
    up = shifted(to_up, "gy", GY, -1)
    third = moved(to_down[0:K], [(at(i, j), at(i + 1, j)) for i in (0, 3, 4) for j in range(GX)])
    across = pl.pallas_call(
        spread_kernel,
        out_shape=shape(GX, 80, L),
        in_specs=[VM] * 5 + [ANY],
        out_specs=VM,
        scratch_shapes=[pltpu.VMEM((80, L), F32)],
        compiler_params=grant(4),
        name="spread",
    )(side, v_left, v_right, down, up, third)
    across = lax.all_to_all(across, "gx", 0, 0)
    sides = pl.pallas_call(
        turn_kernel, out_shape=shape(GY, 32, L), in_specs=[VM], out_specs=VM, compiler_params=grant(4), name="turn"
    )(across)
    sides = lax.all_to_all(sides, "gy", 0, 0)

    state, base = pl.pallas_call(
        inner_kernel,
        out_shape=(nest, parent),
        in_specs=[SM] * 2 + [VM] * 10 + [HB],
        out_specs=(VM, HB),
        scratch_shapes=[
            pltpu.VMEM((K, NR, L), F32), pltpu.VMEM((104, L), F32), pltpu.VMEM((K, 8, L), F32), pltpu.VMEM((K, L), F32),
            pltpu.VMEM((K, 8, L), F32), pltpu.VMEM((K, 8, L), F32), pltpu.SemaphoreType.DMA,
        ],
        input_output_aliases={12: 1},
        compiler_params=grant(14),
        name="inner",
    )(*here, state, nest_nu, land_mask, nest_kappa, across, down, up, third, pay, row_k, base)
    base, side_weights, side_gradients = pl.pallas_call(
        outer_kernel,
        out_shape=(parent, shape(2, K, 2, SR), shape(2, K, 2, SR)),
        in_specs=[SM] * 2 + [VM] * 3 + [HB],
        out_specs=(HB, VM, VM),
        scratch_shapes=[
            pltpu.VMEM((256, L), F32), pltpu.VMEM((PR, L), F32), pltpu.VMEM((K, PR, L), F32), pltpu.VMEM((K, PR, L), F32),
            pltpu.SemaphoreType.DMA((6,)),
        ],
        input_output_aliases={5: 0},
        compiler_params=grant(12),
        name="outer",
    )(*here, sides, col_c, col_r, base)
    return state, base, side_weights, side_gradients


def solution(mesh):
    in_specs = (
        P(None, "gy", "gx"),
        P(None, None, "gy", "gx"),
        P(None, "gy", "gx"),
        P("gy", "gx"),
        P(None, "gy", "gx"),
        P(None, None, "gy", "gx"),
        P(None, None, "gy", "gx"),
        P(),
        P(),
    )
    out_specs = (P(None, "gy", "gx"), P(None, "gy", "gx"), P(), P())
    return jax.shard_map(on_device, mesh=mesh, in_specs=in_specs, out_specs=out_specs, check_vma=False)
```

time: 114 us -> 108 us (0.947)
  waiting for transfers between devices: 35 us -> 23.6 us
  blocking collectives: 20.7 us -> 25 us
  Pallas kernels: 13 us -> 16.1 us
  local copies, waits for them, and re-layouts: 8.29 us -> 5.44 us
  starting transfers between devices: 33.4 us -> 34.9 us
    ppermute x10, waiting for transfers between devices: 26.8 us -> 13.7 us  [moved(): return lax.ppermute(value, ('gy', 'gx'), pairs)]
    all_to_all x1, blocking collectives: 20.7 us -> 25 us  [on_device(): across = lax.all_to_all(across, 'gx', 0, 0)]
    unnamed x28, local copies, waits for them, and re-layouts: 8.29 us -> 5.43 us
    ppermute x5, waiting for transfers between devices: 3.14 us -> 5.75 us  [shifted(): return lax.ppermute(value, axis, pairs)]
    pallas_call x5, Pallas kernels: 5.53 us -> 7.77 us  [the longest x1 2.45 us: on_device(): pl.pallas_call(edge_kernel, out_shape=(shape(56, L), shape(120, L), shape...]
  transfers between devices with their start and end apart: 16 -> 16, of which waited for: 5 -> 5; matrix products, arithmetic and copies ran while one was open for 0% -> 0% of each run, Pallas kernels for 2% -> 4%
where the time goes in v2:
time: 108 us; the launch traced here: 107 us
  starting transfers between devices  34.9 us (32%)
  blocking collectives  25 us (23%)
  waiting for transfers between devices  23.6 us (22%)
  Pallas kernels  16.1 us (15%)
  local copies, waits for them, and re-layouts  5.44 us (5%)
  between operations  2.24 us (2%)
    all_to_all x1, blocking collectives, on_device(): across = lax.all_to_all(across, 'gx', 0, 0)  25 us
    ppermute x5, starting transfers between devices, shifted(): return lax.ppermute(value, axis, pairs)  15.1 us
    ppermute x10, waiting for transfers between devices, moved(): return lax.ppermute(value, ('gy', 'gx'), pairs)  13.7 us
    ppermute x10, starting transfers between devices, moved(): return lax.ppermute(value, ('gy', 'gx'), pairs)  12.5 us
    pallas_call x1, Pallas kernels, on_device(): pl.pallas_call(nest_kernel, out_shape=(nest, shape(112, L), shape(112, L)...  7.57 us
    all_to_all x1, starting transfers between devices, on_device(): sides = lax.all_to_all(sides, 'gy', 0, 0)  7.32 us
    ppermute x5, waiting for transfers between devices, shifted(): return lax.ppermute(value, axis, pairs)  5.75 us
    unnamed x28, local copies, waits for them, and re-layouts  5.43 us
  transfers between devices with their start and end apart: 16, of which 5 were waited for; matrix products, arithmetic and copies ran while one was open for 0% of the time, Pallas kernels for 4%

profile of v2, /device:TPU:1, one launch (start us, length us, event | category | flops | bytes accessed | tf_op | source)
XLA Modules:
  0.0 107.3 jit_solution(9927340897976141699)
XLA Ops:
  1.9 2.4 %edge.1 = (f32[56,128]{1,0:T(8,128)}, f32[120,128]{1,0:T(8,128)}, f32[24,128]{1,0:T(8,128)}, f32[24,128]{1,0:T(8,128)}, f32[168,128]{1,0:T(8,128)}) custom-call(s32[1]{0:T(128)S(6)} %copy.17.o_row, s32[1]{0:T(128)S(6)} %copy.18.o_col, f32[50,24,128]{2,1,0:T(8,128)} %a.3, f32[50,24,128]{2,1,0:T(8,128)} %nu.5, s32[24,128]{1,0:T(8,128)} %mask.5, ...), custom_call_target="tpu_custom_call" | custom-call | tf_op jit(solution)/shard_map/edge/pallas_call | solution.py:565
  4.4 0.7 collective-permute-start.4
  5.1 6.3 %collective-permute-start = (f32[120,128]{1,0:T(8,128)}, f32[120,128]{1,0:T(8,128)S(1)}, u32[]{:S(2)}, u32[]{:S(2)}) collective-permute-start(f32[120,128]{1,0:T(8,128)} %get-tuple-element.31), channel_id=1, source_target_pairs={{0,32},{32,64},{64,96},{96,128},{128,160},{160,192},{192,224},{1,3... | collective-permute-start | bytes 184328 | tf_op jit(solution)/shard_map/ppermute | solution.py:543
  11.4 3.1 %collective-permute-start.2 = (f32[24,128]{1,0:T(8,128)}, f32[24,128]{1,0:T(8,128)S(1)}, u32[]{:S(2)}, u32[]{:S(2)}) collective-permute-start(f32[24,128]{1,0:T(8,128)} %get-tuple-element.33), channel_id=1, source_target_pairs={{0,1},{1,2},{2,3},{3,4},{4,5},{5,6},{6,7},{7,8},{8,9},{9,10},{10,1... | collective-permute-start | bytes 36872 | tf_op jit(solution)/shard_map/ppermute | solution.py:543
  14.5 1.3 %collective-permute-start.3 = (f32[24,128]{1,0:T(8,128)}, f32[24,128]{1,0:T(8,128)S(1)}, u32[]{:S(2)}, u32[]{:S(2)}) collective-permute-start(f32[24,128]{1,0:T(8,128)} %get-tuple-element.34), channel_id=1, source_target_pairs={{1,0},{2,1},{3,2},{4,3},{5,4},{6,5},{7,6},{8,7},{9,8},{10,9},{11,1... | collective-permute-start | bytes 36872 | tf_op jit(solution)/shard_map/ppermute | solution.py:543
  15.8 3.3 %collective-permute-done.3.after_right.h_right = f32[24,128]{1,0:T(8,128)S(1)} collective-permute-done((f32[24,128]{1,0:T(8,128)}, f32[24,128]{1,0:T(8,128)S(1)}, u32[]{:S(2)}, u32[]{:S(2)}) %collective-permute-start.3) | collective-permute-done | bytes 12320 | tf_op jit(solution)/shard_map/ppermute | solution.py:543
  19.1 0.9 copy-done.9
  20.2 0.7 collective-permute-start.5
  20.9 0.7 collective-permute-start.6
  21.6 1.9 %collective-permute-start.1 = (f32[56,128]{1,0:T(8,128)}, f32[56,128]{1,0:T(8,128)S(1)}, u32[]{:S(2)}, u32[]{:S(2)}) collective-permute-start(f32[56,128]{1,0:T(8,128)} %get-tuple-element.32), channel_id=1, source_target_pairs={{32,0},{64,32},{96,64},{128,96},{160,128},{192,160},{224,192},{33,... | collective-permute-start | bytes 86024 | tf_op jit(solution)/shard_map/ppermute | solution.py:543
  23.5 1.3 %collective-permute-start.7 = (f32[64,128]{1,0:T(8,128)S(1)}, f32[64,128]{1,0:T(8,128)S(1)}, u32[]{:S(2)}, u32[]{:S(2)}) collective-permute-start(f32[64,128]{1,0:T(8,128)S(1)} %get-tuple-element.38), channel_id=1, source_target_pairs={{144,2},{176,226},{145,5},{177,229},{146,8},{178,232},{147,11},{17... | collective-permute-start | bytes 98312 | tf_op jit(solution)/shard_map/ppermute | solution.py:538
  24.8 0.7 collective-permute-start.8
  25.5 2.4 %collective-permute-done.1.h_down = f32[56,128]{1,0:T(8,128)S(1)} collective-permute-done((f32[56,128]{1,0:T(8,128)}, f32[56,128]{1,0:T(8,128)S(1)}, u32[]{:S(2)}, u32[]{:S(2)}) %collective-permute-start.1) | collective-permute-done | bytes 28704 | tf_op jit(solution)/shard_map/ppermute | solution.py:543
  28.5 0.7 collective-permute-start.10
  29.2 0.8 collective-permute-start.11
  30.1 1.7 %copy-done.3 = f32[2,50,48,128]{3,2,1,0:T(8,128)S(1)} copy-done((f32[2,50,48,128]{3,2,1,0:T(8,128)S(1)}, f32[2,50,48,128]{3,2,1,0:T(8,128)}, u32[]{:S(2)}) %copy-start.3) | copy-done | bytes 2457624
  31.8 2.1 %base.1 = (f32[50,48,128]{2,1,0:T(8,128)}, f32[2,50,8,128]{3,2,1,0:T(8,128)S(1)}, f32[48,128]{1,0:T(8,128)S(1)}, f32[48,128]{1,0:T(8,128)S(1)}) custom-call(s32[1]{0:T(128)S(6)} %copy.17.o_row, s32[1]{0:T(128)S(6)} %copy.18.o_col, f32[50,48,128]{2,1,0:T(8,128)S(1)} %copy-done.4, f32[2,50,48,128]{3,2,1,0:T(8,128)S(1)} %copy-done.3, ...), custom_call_target="tpu_custom_call" | custom-call | flops 10000000 | bytes 12000000 | tf_op jit(solution)/shard_map/base/pallas_call | solution.py:595
  33.9 8.7 %collective-permute-done.7.rest_2_ = f32[64,128]{1,0:T(8,128)S(1)} collective-permute-done((f32[64,128]{1,0:T(8,128)S(1)}, f32[64,128]{1,0:T(8,128)S(1)}, u32[]{:S(2)}, u32[]{:S(2)}) %collective-permute-start.7) | collective-permute-done | bytes 32800 | tf_op jit(solution)/shard_map/ppermute | solution.py:538
  42.6 7.6 %nest.1 = (f32[50,24,128]{2,1,0:T(8,128)S(1)}, f32[112,128]{1,0:T(8,128)S(1)}, f32[112,128]{1,0:T(8,128)S(1)}, f32[24,128]{1,0:T(8,128)S(1)}, f32[24,128]{1,0:T(8,128)S(1)}, /*index=5*/f32[16,128]{1,0:T(8,128)S(1)}) custom-call(s32[1]{0:T(128)S(6)} %copy.17.o_row, s32[1]{0:T(128)S(6)} %copy.18.o_col, f32[50,24,128]{2,1,0:T(8,128)S(1)} %copy-done.2, ...), custom_call_target="tpu_custom_call" | custom-call | tf_op jit(solution)/shard_map/nest/pallas_call | solution.py:606
  50.2 2.5 %collective-permute-start.13 = (f32[112,128]{1,0:T(8,128)S(1)}, f32[112,128]{1,0:T(8,128)S(1)}, u32[]{:S(2)}, u32[]{:S(2)}) collective-permute-start(f32[112,128]{1,0:T(8,128)S(1)} %get-tuple-element.49), channel_id=1, source_target_pairs={{32,0},{64,32},{96,64},{128,96},{160,128},{192,160},{224,192},{33,... | collective-permute-start | bytes 172040 | tf_op jit(solution)/shard_map/ppermute | solution.py:543
  52.8 5.1 %collective-permute-start.12 = (f32[112,128]{1,0:T(8,128)S(1)}, f32[112,128]{1,0:T(8,128)S(1)}, u32[]{:S(2)}, u32[]{:S(2)}) collective-permute-start(f32[112,128]{1,0:T(8,128)S(1)} %get-tuple-element.48), channel_id=1, source_target_pairs={{0,128},{1,129},{2,130},{3,131},{4,132},{5,133},{6,134},{7,135},{8... | collective-permute-start | bytes 172040 | tf_op jit(solution)/shard_map/ppermute | solution.py:538
  57.9 1.3 %collective-permute-start.14 = (f32[50,128]{1,0:T(8,128)S(1)}, f32[50,128]{1,0:T(8,128)S(1)}, u32[]{:S(2)}, u32[]{:S(2)}) collective-permute-start(f32[50,128]{1,0:T(8,128)S(1)} %slice.3), channel_id=1, source_target_pairs={{0,32},{1,33},{2,34},{3,35},{4,36},{5,37},{6,38},{7,39},{8,40},{9,... | collective-permute-start | bytes 76808 | tf_op jit(solution)/shard_map/ppermute | solution.py:538
  59.2 5.0 %collective-permute-done.14.after.third = f32[50,128]{1,0:T(8,128)S(1)} collective-permute-done((f32[50,128]{1,0:T(8,128)S(1)}, f32[50,128]{1,0:T(8,128)S(1)}, u32[]{:S(2)}, u32[]{:S(2)}) %collective-permute-start.14) | collective-permute-done | bytes 25632 | tf_op jit(solution)/shard_map/ppermute | solution.py:538
  64.4 25.0 %all_to_all.10.across = f32[32,80,128]{2,1,0:T(8,128)S(1)} all-to-all(f32[32,80,128]{2,1,0:T(8,128)S(1)} %spread.1), channel_id=1, replica_groups=mesh['gy'=8,'gx'=32] {'gx'}, dimensions={0} | all-to-all | bytes 2621440 | tf_op jit(solution)/shard_map/all_to_all | solution.py:633
  89.3 0.7 turn.1
  90.0 7.3 %all-to-all-start.1 = ((f32[8,32,128]{2,1,0:T(8,128)}), f32[8,32,128]{2,1,0:T(8,128)S(1)}, u32[]{:S(2)}, u32[]{:S(2)}) async-start(f32[8,32,128]{2,1,0:T(8,128)} %turn.1), calls=%async_computation.1 | async-start | bytes 262144 | tf_op jit(solution)/shard_map/all_to_all | solution.py:637
  97.3 1.1 copy-done.6
  98.4 1.0 copy-done.8
  99.4 1.9 %inner.1 = (f32[50,24,128]{2,1,0:T(8,128)}, f32[50,48,128]{2,1,0:T(8,128)}) custom-call(s32[1]{0:T(128)S(6)} %copy.17.o_row, s32[1]{0:T(128)S(6)} %copy.18.o_col, f32[50,24,128]{2,1,0:T(8,128)S(1)} %copy-done.6, f32[50,24,128]{2,1,0:T(8,128)S(1)} %copy-done, s32[24,128]{1,0:T(8,128)S(1)} %copy-done.11, ...), custom_call_target="tpu_custom_call", output_to_operand_aliasing={{1}: (12, {})} | custom-call | tf_op jit(solution)/shard_map/inner/pallas_call | solution.py:639
  101.3 4.1 %all-to-all-done.1.sides = f32[8,32,128]{2,1,0:T(8,128)S(1)} async-done(((f32[8,32,128]{2,1,0:T(8,128)}), f32[8,32,128]{2,1,0:T(8,128)S(1)}, u32[]{:S(2)}, u32[]{:S(2)}) %all-to-all-start.1) | async-done | bytes 131104 | tf_op jit(solution)/shard_map/all_to_all | solution.py:637
  105.4 0.7 copy-done.13
  106.2 1.1 %outer.1 = (f32[50,48,128]{2,1,0:T(8,128)}, f32[2,50,2,64]{3,2,1,0:T(2,128)}, f32[2,50,2,64]{3,2,1,0:T(2,128)}) custom-call(s32[1]{0:T(128)S(6)} %copy.17.o_row, s32[1]{0:T(128)S(6)} %copy.18.o_col, f32[8,32,128]{2,1,0:T(8,128)S(1)} %all-to-all-done.1.sides, f32[48,128]{1,0:T(8,128)S(1)} %get-tuple-element.43.rest_7_.col_c, ...), custom_call_target="tpu_custom_call", output_to_operand_aliasing={{0}: (5, {})} | custom-call | tf_op jit(solution)/shard_map/outer/pallas_call | solution.py:652
  (38 shorter events, 1.0 us)
Async XLA Ops:
  1.9 28.1 %copy-start.4 = (f32[50,48,128]{2,1,0:T(8,128)S(1)}, f32[50,48,128]{2,1,0:T(8,128)}, u32[]{:S(2)}) copy-start(f32[50,48,128]{2,1,0:T(8,128)} %q.1) | copy-start | bytes 3686404
  4.4 14.8 %collective-permute-start.4 = (f32[168,128]{1,0:T(8,128)}, f32[168,128]{1,0:T(8,128)S(1)}, u32[]{:S(2)}, u32[]{:S(2)}) collective-permute-start(f32[168,128]{1,0:T(8,128)} %get-tuple-element.35.pay), channel_id=1, source_target_pairs={{208,176},{209,177},{210,178},{211,179},{212,180},{213,181},{214,1... | collective-permute-start | bytes 258056 | tf_op jit(solution)/shard_map/ppermute | solution.py:538
  5.1 14.1 %collective-permute-start = (f32[120,128]{1,0:T(8,128)}, f32[120,128]{1,0:T(8,128)S(1)}, u32[]{:S(2)}, u32[]{:S(2)}) collective-permute-start(f32[120,128]{1,0:T(8,128)} %get-tuple-element.31), channel_id=1, source_target_pairs={{0,32},{32,64},{64,96},{96,128},{128,160},{160,192},{192,224},{1,3... | collective-permute-start | bytes 184328 | tf_op jit(solution)/shard_map/ppermute | solution.py:543
  11.4 4.4 %collective-permute-start.2 = (f32[24,128]{1,0:T(8,128)}, f32[24,128]{1,0:T(8,128)S(1)}, u32[]{:S(2)}, u32[]{:S(2)}) collective-permute-start(f32[24,128]{1,0:T(8,128)} %get-tuple-element.33), channel_id=1, source_target_pairs={{0,1},{1,2},{2,3},{3,4},{4,5},{5,6},{6,7},{7,8},{8,9},{9,10},{10,1... | collective-permute-start | bytes 36872 | tf_op jit(solution)/shard_map/ppermute | solution.py:543
  14.5 4.6 %collective-permute-start.3 = (f32[24,128]{1,0:T(8,128)}, f32[24,128]{1,0:T(8,128)S(1)}, u32[]{:S(2)}, u32[]{:S(2)}) collective-permute-start(f32[24,128]{1,0:T(8,128)} %get-tuple-element.34), channel_id=1, source_target_pairs={{1,0},{2,1},{3,2},{4,3},{5,4},{6,5},{7,6},{8,7},{9,8},{10,9},{11,1... | collective-permute-start | bytes 36872 | tf_op jit(solution)/shard_map/ppermute | solution.py:543
  19.1 0.9 copy-start.9
  20.2 8.3 %collective-permute-start.5 = (f32[64,128]{1,0:T(8,128)S(1)}, f32[64,128]{1,0:T(8,128)S(1)}, u32[]{:S(2)}, u32[]{:S(2)}) collective-permute-start(f32[64,128]{1,0:T(8,128)S(1)} %get-tuple-element.36), channel_id=1, source_target_pairs={{144,0},{176,224},{145,3},{177,227},{146,6},{178,230},{147,9},{179... | collective-permute-start | bytes 98312 | tf_op jit(solution)/shard_map/ppermute | solution.py:538
  20.9 8.3 %collective-permute-start.6 = (f32[64,128]{1,0:T(8,128)S(1)}, f32[64,128]{1,0:T(8,128)S(1)}, u32[]{:S(2)}, u32[]{:S(2)}) collective-permute-start(f32[64,128]{1,0:T(8,128)S(1)} %get-tuple-element.37), channel_id=1, source_target_pairs={{144,1},{176,225},{145,4},{177,228},{146,7},{178,231},{147,10},{17... | collective-permute-start | bytes 98312 | tf_op jit(solution)/shard_map/ppermute | solution.py:538
  21.6 6.3 %collective-permute-start.1 = (f32[56,128]{1,0:T(8,128)}, f32[56,128]{1,0:T(8,128)S(1)}, u32[]{:S(2)}, u32[]{:S(2)}) collective-permute-start(f32[56,128]{1,0:T(8,128)} %get-tuple-element.32), channel_id=1, source_target_pairs={{32,0},{64,32},{96,64},{128,96},{160,128},{192,160},{224,192},{33,... | collective-permute-start | bytes 86024 | tf_op jit(solution)/shard_map/ppermute | solution.py:543
  23.5 19.1 %collective-permute-start.7 = (f32[64,128]{1,0:T(8,128)S(1)}, f32[64,128]{1,0:T(8,128)S(1)}, u32[]{:S(2)}, u32[]{:S(2)}) collective-permute-start(f32[64,128]{1,0:T(8,128)S(1)} %get-tuple-element.38), channel_id=1, source_target_pairs={{144,2},{176,226},{145,5},{177,229},{146,8},{178,232},{147,11},{17... | collective-permute-start | bytes 98312 | tf_op jit(solution)/shard_map/ppermute | solution.py:538
  24.8 17.8 %collective-permute-start.8 = (f32[64,128]{1,0:T(8,128)S(1)}, f32[64,128]{1,0:T(8,128)S(1)}, u32[]{:S(2)}, u32[]{:S(2)}) collective-permute-start(f32[64,128]{1,0:T(8,128)S(1)} %get-tuple-element.39), channel_id=1, source_target_pairs={{145,0},{177,224},{146,3},{178,227},{147,6},{179,230},{148,9},{180... | collective-permute-start | bytes 98312 | tf_op jit(solution)/shard_map/ppermute | solution.py:538
  27.9 14.7 %collective-permute-start.9 = (f32[64,128]{1,0:T(8,128)S(1)}, f32[64,128]{1,0:T(8,128)S(1)}, u32[]{:S(2)}, u32[]{:S(2)}) collective-permute-start(f32[64,128]{1,0:T(8,128)S(1)} %get-tuple-element.40), channel_id=1, source_target_pairs={{145,1},{177,225},{146,4},{178,228},{147,7},{179,231},{148,10},{18... | collective-permute-start | bytes 98312 | tf_op jit(solution)/shard_map/ppermute | solution.py:538
  28.5 14.1 %collective-permute-start.10 = (f32[64,128]{1,0:T(8,128)S(1)}, f32[64,128]{1,0:T(8,128)S(1)}, u32[]{:S(2)}, u32[]{:S(2)}) collective-permute-start(f32[64,128]{1,0:T(8,128)S(1)} %get-tuple-element.41), channel_id=1, source_target_pairs={{145,2},{177,226},{146,5},{178,229},{147,8},{179,232},{148,11},{18... | collective-permute-start | bytes 98312 | tf_op jit(solution)/shard_map/ppermute | solution.py:538
  29.2 13.4 %copy-start = (f32[50,24,128]{2,1,0:T(8,128)S(1)}, f32[50,24,128]{2,1,0:T(8,128)}, u32[]{:S(2)}) copy-start(f32[50,24,128]{2,1,0:T(8,128)} %nu.5) | copy-start | bytes 1843204
  29.2 13.4 %copy-start.1 = (f32[2,50,24,128]{3,2,1,0:T(8,128)S(1)}, f32[2,50,24,128]{3,2,1,0:T(8,128)}, u32[]{:S(2)}) copy-start(f32[2,50,24,128]{3,2,1,0:T(8,128)} %kappa.3) | copy-start | bytes 3686404
  29.2 13.4 %copy-start.2 = (f32[50,24,128]{2,1,0:T(8,128)S(1)}, f32[50,24,128]{2,1,0:T(8,128)}, u32[]{:S(2)}) copy-start(f32[50,24,128]{2,1,0:T(8,128)} %a.3) | copy-start | bytes 1843204
  29.2 13.3 %collective-permute-start.11 = (f32[64,128]{1,0:T(8,128)S(1)}, f32[64,128]{1,0:T(8,128)S(1)}, u32[]{:S(2)}, u32[]{:S(2)}) collective-permute-start(f32[64,128]{1,0:T(8,128)S(1)} %get-tuple-element.42.after), channel_id=1, source_target_pairs={{146,2},{178,226},{147,5},{179,229},{148,8},{180,232},{149,11},{18... | collective-permute-start | bytes 98312 | tf_op jit(solution)/shard_map/ppermute | solution.py:538
  30.1 1.7 %copy-start.3 = (f32[2,50,48,128]{3,2,1,0:T(8,128)S(1)}, f32[2,50,48,128]{3,2,1,0:T(8,128)}, u32[]{:S(2)}) copy-start(f32[2,50,48,128]{3,2,1,0:T(8,128)} %pkappa.1) | copy-start | bytes 7372804
  31.7 10.9 %copy-start.11 = (s32[24,128]{1,0:T(8,128)S(1)}, s32[24,128]{1,0:T(8,128)}, u32[]{:S(2)}) copy-start(s32[24,128]{1,0:T(8,128)} %mask.5) | copy-start | bytes 36868
  33.9 16.3 %copy-start.7 = (f32[2,50,8,128]{3,2,1,0:T(8,128)}, f32[2,50,8,128]{3,2,1,0:T(8,128)S(1)}, u32[]{:S(2)}) copy-start(f32[2,50,8,128]{3,2,1,0:T(8,128)S(1)} %get-tuple-element.50.row_k) | copy-start | bytes 1228804
  33.9 16.3 %copy-start.12 = (f32[48,128]{1,0:T(8,128)}, f32[48,128]{1,0:T(8,128)S(1)}, u32[]{:S(2)}) copy-start(f32[48,128]{1,0:T(8,128)S(1)} %get-tuple-element.53.col_r) | copy-start | bytes 73732
  50.2 39.1 %copy-start.5 = (f32[50,24,128]{2,1,0:T(8,128)}, f32[50,24,128]{2,1,0:T(8,128)S(1)}, u32[]{:S(2)}) copy-start(f32[50,24,128]{2,1,0:T(8,128)S(1)} %get-tuple-element.44.a) | copy-start | bytes 1843204
  50.2 14.0 %collective-permute-start.13 = (f32[112,128]{1,0:T(8,128)S(1)}, f32[112,128]{1,0:T(8,128)S(1)}, u32[]{:S(2)}, u32[]{:S(2)}) collective-permute-start(f32[112,128]{1,0:T(8,128)S(1)} %get-tuple-element.49), channel_id=1, source_target_pairs={{32,0},{64,32},{96,64},{128,96},{160,128},{192,160},{224,192},{33,... | collective-permute-start | bytes 172040 | tf_op jit(solution)/shard_map/ppermute | solution.py:543
  52.8 11.5 %collective-permute-start.12 = (f32[112,128]{1,0:T(8,128)S(1)}, f32[112,128]{1,0:T(8,128)S(1)}, u32[]{:S(2)}, u32[]{:S(2)}) collective-permute-start(f32[112,128]{1,0:T(8,128)S(1)} %get-tuple-element.48), channel_id=1, source_target_pairs={{0,128},{1,129},{2,130},{3,131},{4,132},{5,133},{6,134},{7,135},{8... | collective-permute-start | bytes 172040 | tf_op jit(solution)/shard_map/ppermute | solution.py:538
  57.9 6.3 %collective-permute-start.14 = (f32[50,128]{1,0:T(8,128)S(1)}, f32[50,128]{1,0:T(8,128)S(1)}, u32[]{:S(2)}, u32[]{:S(2)}) collective-permute-start(f32[50,128]{1,0:T(8,128)S(1)} %slice.3), channel_id=1, source_target_pairs={{0,32},{1,33},{2,34},{3,35},{4,36},{5,37},{6,38},{7,39},{8,40},{9,... | collective-permute-start | bytes 76808 | tf_op jit(solution)/shard_map/ppermute | solution.py:538
  89.3 8.0 %copy-start.10 = (f32[168,128]{1,0:T(8,128)S(1)}, f32[168,128]{1,0:T(8,128)}, u32[]{:S(2)}) copy-start(f32[168,128]{1,0:T(8,128)} %get-tuple-element.35.pay) | copy-start | bytes 258052
  90.0 15.4 %all-to-all-start.1 = ((f32[8,32,128]{2,1,0:T(8,128)}), f32[8,32,128]{2,1,0:T(8,128)S(1)}, u32[]{:S(2)}, u32[]{:S(2)}) async-start(f32[8,32,128]{2,1,0:T(8,128)} %turn.1), calls=%async_computation.1 | async-start | bytes 262144 | tf_op jit(solution)/shard_map/all_to_all | solution.py:637
  97.3 1.1 %copy-start.6 = (f32[50,24,128]{2,1,0:T(8,128)S(1)}, f32[50,24,128]{2,1,0:T(8,128)}, u32[]{:S(2)}) copy-start(f32[50,24,128]{2,1,0:T(8,128)} %copy-done.5) | copy-start | bytes 1843204
  98.4 1.0 copy-start.8
  105.4 0.7 copy-start.13

commit v3 on v2

--- a/solution.py
+++ b/solution.py
@@ -59,6 +59,14 @@
 
 def place(row, col):
     return lax.axis_index("gy"), lax.axis_index("gx"), row[0], col[0]
+
+
+def to_first(values, i):
+    return pltpu.roll(values, L - i, 1) if i else values
+
+
+def to_last(values, i):
+    return pltpu.roll(values, L - 1 - i, 1) if i < L - 1 else values
 
 
 def side_lane(x, ox):
@@ -301,22 +309,34 @@
     up_s[...] = h_up[0:K, :] * (1.0 - w_up[0:K])
     down_s[...] = h_down[0:K, :] * (1.0 - w_down[0:K])
 
+    w_edge = jnp.where(x == 0, w_we, pltpu.roll(w_we, L - 1, 1))
     m = mask[...].astype(F32)
     one = jnp.ones((NR, L), F32)
     zero = jnp.zeros((NR, L), F32)
     c_prev, e_prev, y = zero, zero, zero
     top = g == 0
+    side_ok = (x == 0) | (x == GX - 1)
+
+    @pl.when(side_ok)
+    def _():
+        for k in range(K):
+            y_s[k] = a[k] * (one - m_lane * to_first(w_edge, k))
+
+    @pl.when(jnp.logical_not(side_ok))
+    def _():
+        y_s[...] = a[...]
+
     is31 = (x == GX - 1).astype(jnp.int32)
     for k in range(K):
         w_row = w_s[pl.ds(k, 1), :]
-        raw = a[k]
+        raw = y_s[k]
         g_s[pl.ds(k, 1), :] = jnp.where(top, raw[0:1], raw[NR - 1 : NR])
-        now = raw * (one - (m_row * wide(w_row, NR) + m_lane * wide(w_we[:, k : k + 1], NR)))
+        now = raw * (one - m_row * wide(w_row, NR))
         v = nu[k] * m * now
         above = jnp.where(row24 == 0, wide(up_s[pl.ds(k, 1), :], NR), pltpu.roll(v, 1, 0))
         below = jnp.where(row24 == NR - 1, wide(down_s[pl.ds(k, 1), :], NR), pltpu.roll(v, NR - 1, 0))
-        left = jnp.where(lane24 == 0, wide(hl[:, k : k + 1], NR), pltpu.roll(v, 1, 1))
-        right = jnp.where(lane24 == L - 1, wide(hr[:, k : k + 1], NR), pltpu.roll(v, L - 1, 1))
+        left = jnp.where(lane24 == 0, to_first(hl, k), pltpu.roll(v, 1, 1))
+        right = jnp.where(lane24 == L - 1, to_last(hr, k), pltpu.roll(v, L - 1, 1))
         b = m * (now + (above + below + left + right - 4.0 * v))
         c = kappa[1, k]
         r = 1.0 / (1.0 + c + c_prev * (1.0 - e_prev))
@@ -330,11 +350,18 @@
     for k in range(K - 1, -1, -1):
         sol = y_s[k] + e_s[k] * sol if k < K - 1 else y_s[k]
         y_s[k] = sol
-        w_row = w_s[pl.ds(56 + k, 1), :]
+    for k in range(K):
+        sol = y_s[k]
         g_s[pl.ds(56 + k, 1), :] = jnp.where(top, sol[0:1], sol[NR - 1 : NR])
-        now = sol * (one - (m_row * wide(w_row, NR) + m_lane * wide(w_we[:, 64 + k : 65 + k], NR)))
-        a_out[k] = now
-        v = nu[k] * m * now
+        a_out[k] = sol * (one - m_row * wide(w_s[pl.ds(56 + k, 1), :], NR))
+
+    @pl.when(side_ok)
+    def _():
+        for k in range(K):
+            a_out[k] = a_out[k] * (one - m_lane * to_first(w_edge, 64 + k))
+
+    for k in range(K):
+        v = nu[k] * m * a_out[k]
         to_up[pl.ds(k, 1), :] = v[0:1]
         to_down[pl.ds(k, 1), :] = v[NR - 1 : NR]
         acc_l = jnp.where(lane24 == k, pltpu.roll(v, k, 1) if k else v, acc_l)
@@ -397,8 +424,8 @@
         v = nu[k] * m * now
         above = jnp.where(row24 == 0, wide(up_s[pl.ds(k, 1), :], NR), pltpu.roll(v, 1, 0))
         below = jnp.where(row24 == NR - 1, wide(up[pl.ds(k, 1), :], NR), pltpu.roll(v, NR - 1, 0))
-        left = jnp.where(lane24 == 0, wide(hl[:, k : k + 1], NR), pltpu.roll(v, 1, 1))
-        right = jnp.where(lane24 == L - 1, wide(hr[:, k : k + 1], NR), pltpu.roll(v, L - 1, 1))
+        left = jnp.where(lane24 == 0, to_first(hl, k), pltpu.roll(v, 1, 1))
+        right = jnp.where(lane24 == L - 1, to_last(hr, k), pltpu.roll(v, L - 1, 1))
         b = m * (now + (above + below + left + right - 4.0 * v))
         c = kappa[0, k]
         r = 1.0 / (1.0 + c + c_prev * (1.0 - e_prev))
@@ -491,13 +518,15 @@
             local_s[pl.ds(r, 1), :] = panel_s[pl.ds(start + r, 1), :]
         here = iota((PR, L), 1) == spot
         lane = iota((PR, L), 1)
+        own = local_s[...]
         cs, rs = col_c[...], col_r[...]
         above = jnp.where((lane == 0) | (lane == 64), 0.0, pltpu.roll(cs, 1, 1)) * rs
         below = cs * rs
-        own = local_s[...] * rs
+        own = own * rs
+        own, above, below, rs = (pltpu.roll(v, spot, 1) for v in (own, above, below, rs))
 
         def column(values, i):
-            return wide(values[:, i : i + 1], PR)
+            return to_first(values, i)
 
         zero = jnp.zeros((PR, L), F32)
         for step, first in ((1, 0), (0, 64)):

time: 108 us -> 102 us (0.944)
  Pallas kernels: 16.1 us -> 10.7 us
    pallas_call x1, Pallas kernels: 7.57 us -> 2.4 us  [on_device(): pl.pallas_call(nest_kernel, out_shape=(nest, shape(112, L), shape(112, L)...]
where the time goes in v3:
time: 102 us
  starting transfers between devices  34.6 us (34%)
  blocking collectives  24.9 us (24%)
  waiting for transfers between devices  23.8 us (23%)
  Pallas kernels  10.7 us (10%)
  local copies, waits for them, and re-layouts  5.44 us (5%)
  between operations  2.23 us (2%)
    all_to_all x1, blocking collectives, on_device(): across = lax.all_to_all(across, 'gx', 0, 0)  24.9 us
    ppermute x5, starting transfers between devices, shifted(): return lax.ppermute(value, axis, pairs)  15.1 us
    ppermute x10, waiting for transfers between devices, moved(): return lax.ppermute(value, ('gy', 'gx'), pairs)  13.7 us
    ppermute x10, starting transfers between devices, moved(): return lax.ppermute(value, ('gy', 'gx'), pairs)  12.5 us
    all_to_all x1, starting transfers between devices, on_device(): sides = lax.all_to_all(sides, 'gy', 0, 0)  7.02 us
    ppermute x5, waiting for transfers between devices, shifted(): return lax.ppermute(value, axis, pairs)  5.75 us
    unnamed x28, local copies, waits for them, and re-layouts  5.43 us
    all_to_all x1, waiting for transfers between devices, on_device(): sides = lax.all_to_all(sides, 'gy', 0, 0)  4.3 us
  transfers between devices with their start and end apart: 16, of which 5 were waited for; matrix products, arithmetic and copies ran while one was open for 0% of the time, Pallas kernels for 4%

profile of v3, /device:TPU:1, one launch (start us, length us, event | category | flops | bytes accessed | tf_op | source)
XLA Modules:
  0.0 101.7 jit_solution(3583010971065964821)
XLA Ops:
  1.9 2.4 %edge.1 = (f32[56,128]{1,0:T(8,128)}, f32[120,128]{1,0:T(8,128)}, f32[24,128]{1,0:T(8,128)}, f32[24,128]{1,0:T(8,128)}, f32[168,128]{1,0:T(8,128)}) custom-call(s32[1]{0:T(128)S(6)} %copy.17.o_row, s32[1]{0:T(128)S(6)} %copy.18.o_col, f32[50,24,128]{2,1,0:T(8,128)} %a.3, f32[50,24,128]{2,1,0:T(8,128)} %nu.5, s32[24,128]{1,0:T(8,128)} %mask.5, ...), custom_call_target="tpu_custom_call" | custom-call | tf_op jit(solution)/shard_map/edge/pallas_call | solution.py:594
  4.4 0.7 collective-permute-start.4
  5.1 6.3 %collective-permute-start = (f32[120,128]{1,0:T(8,128)}, f32[120,128]{1,0:T(8,128)S(1)}, u32[]{:S(2)}, u32[]{:S(2)}) collective-permute-start(f32[120,128]{1,0:T(8,128)} %get-tuple-element.31), channel_id=1, source_target_pairs={{0,32},{32,64},{64,96},{96,128},{128,160},{160,192},{192,224},{1,3... | collective-permute-start | bytes 184328 | tf_op jit(solution)/shard_map/ppermute | solution.py:572
  11.4 3.1 %collective-permute-start.2 = (f32[24,128]{1,0:T(8,128)}, f32[24,128]{1,0:T(8,128)S(1)}, u32[]{:S(2)}, u32[]{:S(2)}) collective-permute-start(f32[24,128]{1,0:T(8,128)} %get-tuple-element.33), channel_id=1, source_target_pairs={{0,1},{1,2},{2,3},{3,4},{4,5},{5,6},{6,7},{7,8},{8,9},{9,10},{10,1... | collective-permute-start | bytes 36872 | tf_op jit(solution)/shard_map/ppermute | solution.py:572
  14.5 1.3 %collective-permute-start.3 = (f32[24,128]{1,0:T(8,128)}, f32[24,128]{1,0:T(8,128)S(1)}, u32[]{:S(2)}, u32[]{:S(2)}) collective-permute-start(f32[24,128]{1,0:T(8,128)} %get-tuple-element.34), channel_id=1, source_target_pairs={{1,0},{2,1},{3,2},{4,3},{5,4},{6,5},{7,6},{8,7},{9,8},{10,9},{11,1... | collective-permute-start | bytes 36872 | tf_op jit(solution)/shard_map/ppermute | solution.py:572
  15.8 3.3 %collective-permute-done.3.after_right.h_right = f32[24,128]{1,0:T(8,128)S(1)} collective-permute-done((f32[24,128]{1,0:T(8,128)}, f32[24,128]{1,0:T(8,128)S(1)}, u32[]{:S(2)}, u32[]{:S(2)}) %collective-permute-start.3) | collective-permute-done | bytes 12320 | tf_op jit(solution)/shard_map/ppermute | solution.py:572
  19.1 0.9 copy-done.9
  20.2 0.7 collective-permute-start.5
  20.9 0.7 collective-permute-start.6
  21.6 1.9 %collective-permute-start.1 = (f32[56,128]{1,0:T(8,128)}, f32[56,128]{1,0:T(8,128)S(1)}, u32[]{:S(2)}, u32[]{:S(2)}) collective-permute-start(f32[56,128]{1,0:T(8,128)} %get-tuple-element.32), channel_id=1, source_target_pairs={{32,0},{64,32},{96,64},{128,96},{160,128},{192,160},{224,192},{33,... | collective-permute-start | bytes 86024 | tf_op jit(solution)/shard_map/ppermute | solution.py:572
  23.5 1.3 %collective-permute-start.7 = (f32[64,128]{1,0:T(8,128)S(1)}, f32[64,128]{1,0:T(8,128)S(1)}, u32[]{:S(2)}, u32[]{:S(2)}) collective-permute-start(f32[64,128]{1,0:T(8,128)S(1)} %get-tuple-element.38), channel_id=1, source_target_pairs={{144,2},{176,226},{145,5},{177,229},{146,8},{178,232},{147,11},{17... | collective-permute-start | bytes 98312 | tf_op jit(solution)/shard_map/ppermute | solution.py:567
  24.8 0.7 collective-permute-start.8
  25.5 2.4 %collective-permute-done.1.h_down = f32[56,128]{1,0:T(8,128)S(1)} collective-permute-done((f32[56,128]{1,0:T(8,128)}, f32[56,128]{1,0:T(8,128)S(1)}, u32[]{:S(2)}, u32[]{:S(2)}) %collective-permute-start.1) | collective-permute-done | bytes 28704 | tf_op jit(solution)/shard_map/ppermute | solution.py:572
  28.5 0.7 collective-permute-start.10
  29.2 0.8 collective-permute-start.11
  30.1 1.7 %copy-done.3 = f32[2,50,48,128]{3,2,1,0:T(8,128)S(1)} copy-done((f32[2,50,48,128]{3,2,1,0:T(8,128)S(1)}, f32[2,50,48,128]{3,2,1,0:T(8,128)}, u32[]{:S(2)}) %copy-start.3) | copy-done | bytes 2457624
  31.8 2.1 %base.1 = (f32[50,48,128]{2,1,0:T(8,128)}, f32[2,50,8,128]{3,2,1,0:T(8,128)S(1)}, f32[48,128]{1,0:T(8,128)S(1)}, f32[48,128]{1,0:T(8,128)S(1)}) custom-call(s32[1]{0:T(128)S(6)} %copy.17.o_row, s32[1]{0:T(128)S(6)} %copy.18.o_col, f32[50,48,128]{2,1,0:T(8,128)S(1)} %copy-done.4, f32[2,50,48,128]{3,2,1,0:T(8,128)S(1)} %copy-done.3, ...), custom_call_target="tpu_custom_call" | custom-call | flops 10000000 | bytes 12000000 | tf_op jit(solution)/shard_map/base/pallas_call | solution.py:624
  33.9 8.7 %collective-permute-done.7.rest_2_ = f32[64,128]{1,0:T(8,128)S(1)} collective-permute-done((f32[64,128]{1,0:T(8,128)S(1)}, f32[64,128]{1,0:T(8,128)S(1)}, u32[]{:S(2)}, u32[]{:S(2)}) %collective-permute-start.7) | collective-permute-done | bytes 32800 | tf_op jit(solution)/shard_map/ppermute | solution.py:567
  42.6 2.4 %nest.1 = (f32[50,24,128]{2,1,0:T(8,128)S(1)}, f32[112,128]{1,0:T(8,128)S(1)}, f32[112,128]{1,0:T(8,128)S(1)}, f32[24,128]{1,0:T(8,128)S(1)}, f32[24,128]{1,0:T(8,128)S(1)}, /*index=5*/f32[16,128]{1,0:T(8,128)S(1)}) custom-call(s32[1]{0:T(128)S(6)} %copy.17.o_row, s32[1]{0:T(128)S(6)} %copy.18.o_col, f32[50,24,128]{2,1,0:T(8,128)S(1)} %copy-done.2, ...), custom_call_target="tpu_custom_call" | custom-call | tf_op jit(solution)/shard_map/nest/pallas_call | solution.py:635
  45.1 2.5 %collective-permute-start.13 = (f32[112,128]{1,0:T(8,128)S(1)}, f32[112,128]{1,0:T(8,128)S(1)}, u32[]{:S(2)}, u32[]{:S(2)}) collective-permute-start(f32[112,128]{1,0:T(8,128)S(1)} %get-tuple-element.49), channel_id=1, source_target_pairs={{32,0},{64,32},{96,64},{128,96},{160,128},{192,160},{224,192},{33,... | collective-permute-start | bytes 172040 | tf_op jit(solution)/shard_map/ppermute | solution.py:572
  47.6 5.1 %collective-permute-start.12 = (f32[112,128]{1,0:T(8,128)S(1)}, f32[112,128]{1,0:T(8,128)S(1)}, u32[]{:S(2)}, u32[]{:S(2)}) collective-permute-start(f32[112,128]{1,0:T(8,128)S(1)} %get-tuple-element.48), channel_id=1, source_target_pairs={{0,128},{1,129},{2,130},{3,131},{4,132},{5,133},{6,134},{7,135},{8... | collective-permute-start | bytes 172040 | tf_op jit(solution)/shard_map/ppermute | solution.py:567
  52.7 1.3 %collective-permute-start.14 = (f32[50,128]{1,0:T(8,128)S(1)}, f32[50,128]{1,0:T(8,128)S(1)}, u32[]{:S(2)}, u32[]{:S(2)}) collective-permute-start(f32[50,128]{1,0:T(8,128)S(1)} %slice.3), channel_id=1, source_target_pairs={{0,32},{1,33},{2,34},{3,35},{4,36},{5,37},{6,38},{7,39},{8,40},{9,... | collective-permute-start | bytes 76808 | tf_op jit(solution)/shard_map/ppermute | solution.py:567
  54.0 5.0 %collective-permute-done.14.after.third = f32[50,128]{1,0:T(8,128)S(1)} collective-permute-done((f32[50,128]{1,0:T(8,128)S(1)}, f32[50,128]{1,0:T(8,128)S(1)}, u32[]{:S(2)}, u32[]{:S(2)}) %collective-permute-start.14) | collective-permute-done | bytes 25632 | tf_op jit(solution)/shard_map/ppermute | solution.py:567
  59.2 24.9 %all_to_all.10.across = f32[32,80,128]{2,1,0:T(8,128)S(1)} all-to-all(f32[32,80,128]{2,1,0:T(8,128)S(1)} %spread.1), channel_id=1, replica_groups=mesh['gy'=8,'gx'=32] {'gx'}, dimensions={0} | all-to-all | bytes 2621440 | tf_op jit(solution)/shard_map/all_to_all | solution.py:662
  84.1 0.7 turn.1
  84.8 7.0 %all-to-all-start.1 = ((f32[8,32,128]{2,1,0:T(8,128)}), f32[8,32,128]{2,1,0:T(8,128)S(1)}, u32[]{:S(2)}, u32[]{:S(2)}) async-start(f32[8,32,128]{2,1,0:T(8,128)} %turn.1), calls=%async_computation.1 | async-start | bytes 262144 | tf_op jit(solution)/shard_map/all_to_all | solution.py:666
  91.8 1.1 %copy-done.6 = f32[50,24,128]{2,1,0:T(8,128)S(1)} copy-done((f32[50,24,128]{2,1,0:T(8,128)S(1)}, f32[50,24,128]{2,1,0:T(8,128)}, u32[]{:S(2)}) %copy-start.6) | copy-done | bytes 614424
  92.9 1.0 copy-done.8
  93.9 1.7 %inner.1 = (f32[50,24,128]{2,1,0:T(8,128)}, f32[50,48,128]{2,1,0:T(8,128)}) custom-call(s32[1]{0:T(128)S(6)} %copy.17.o_row, s32[1]{0:T(128)S(6)} %copy.18.o_col, f32[50,24,128]{2,1,0:T(8,128)S(1)} %copy-done.6, f32[50,24,128]{2,1,0:T(8,128)S(1)} %copy-done, s32[24,128]{1,0:T(8,128)S(1)} %copy-done.11, ...), custom_call_target="tpu_custom_call", output_to_operand_aliasing={{1}: (12, {})} | custom-call | tf_op jit(solution)/shard_map/inner/pallas_call | solution.py:668
  95.6 4.3 %all-to-all-done.1.sides = f32[8,32,128]{2,1,0:T(8,128)S(1)} async-done(((f32[8,32,128]{2,1,0:T(8,128)}), f32[8,32,128]{2,1,0:T(8,128)S(1)}, u32[]{:S(2)}, u32[]{:S(2)}) %all-to-all-start.1) | async-done | bytes 131104 | tf_op jit(solution)/shard_map/all_to_all | solution.py:666
  99.9 0.7 copy-done.13
  100.6 1.1 %outer.1 = (f32[50,48,128]{2,1,0:T(8,128)}, f32[2,50,2,64]{3,2,1,0:T(2,128)}, f32[2,50,2,64]{3,2,1,0:T(2,128)}) custom-call(s32[1]{0:T(128)S(6)} %copy.17.o_row, s32[1]{0:T(128)S(6)} %copy.18.o_col, f32[8,32,128]{2,1,0:T(8,128)S(1)} %all-to-all-done.1.sides, f32[48,128]{1,0:T(8,128)S(1)} %get-tuple-element.43.rest_7_.col_c, ...), custom_call_target="tpu_custom_call", output_to_operand_aliasing={{0}: (5, {})} | custom-call | tf_op jit(solution)/shard_map/outer/pallas_call | solution.py:681
  (38 shorter events, 1.0 us)
Async XLA Ops:
  1.9 28.1 %copy-start.4 = (f32[50,48,128]{2,1,0:T(8,128)S(1)}, f32[50,48,128]{2,1,0:T(8,128)}, u32[]{:S(2)}) copy-start(f32[50,48,128]{2,1,0:T(8,128)} %q.1) | copy-start | bytes 3686404
  4.4 14.8 %collective-permute-start.4 = (f32[168,128]{1,0:T(8,128)}, f32[168,128]{1,0:T(8,128)S(1)}, u32[]{:S(2)}, u32[]{:S(2)}) collective-permute-start(f32[168,128]{1,0:T(8,128)} %get-tuple-element.35.pay), channel_id=1, source_target_pairs={{208,176},{209,177},{210,178},{211,179},{212,180},{213,181},{214,1... | collective-permute-start | bytes 258056 | tf_op jit(solution)/shard_map/ppermute | solution.py:567
  5.1 14.1 %collective-permute-start = (f32[120,128]{1,0:T(8,128)}, f32[120,128]{1,0:T(8,128)S(1)}, u32[]{:S(2)}, u32[]{:S(2)}) collective-permute-start(f32[120,128]{1,0:T(8,128)} %get-tuple-element.31), channel_id=1, source_target_pairs={{0,32},{32,64},{64,96},{96,128},{128,160},{160,192},{192,224},{1,3... | collective-permute-start | bytes 184328 | tf_op jit(solution)/shard_map/ppermute | solution.py:572
  11.4 4.4 %collective-permute-start.2 = (f32[24,128]{1,0:T(8,128)}, f32[24,128]{1,0:T(8,128)S(1)}, u32[]{:S(2)}, u32[]{:S(2)}) collective-permute-start(f32[24,128]{1,0:T(8,128)} %get-tuple-element.33), channel_id=1, source_target_pairs={{0,1},{1,2},{2,3},{3,4},{4,5},{5,6},{6,7},{7,8},{8,9},{9,10},{10,1... | collective-permute-start | bytes 36872 | tf_op jit(solution)/shard_map/ppermute | solution.py:572
  14.5 4.6 %collective-permute-start.3 = (f32[24,128]{1,0:T(8,128)}, f32[24,128]{1,0:T(8,128)S(1)}, u32[]{:S(2)}, u32[]{:S(2)}) collective-permute-start(f32[24,128]{1,0:T(8,128)} %get-tuple-element.34), channel_id=1, source_target_pairs={{1,0},{2,1},{3,2},{4,3},{5,4},{6,5},{7,6},{8,7},{9,8},{10,9},{11,1... | collective-permute-start | bytes 36872 | tf_op jit(solution)/shard_map/ppermute | solution.py:572
  19.1 0.9 copy-start.9
  20.2 8.3 %collective-permute-start.5 = (f32[64,128]{1,0:T(8,128)S(1)}, f32[64,128]{1,0:T(8,128)S(1)}, u32[]{:S(2)}, u32[]{:S(2)}) collective-permute-start(f32[64,128]{1,0:T(8,128)S(1)} %get-tuple-element.36), channel_id=1, source_target_pairs={{144,0},{176,224},{145,3},{177,227},{146,6},{178,230},{147,9},{179... | collective-permute-start | bytes 98312 | tf_op jit(solution)/shard_map/ppermute | solution.py:567
  20.9 8.3 %collective-permute-start.6 = (f32[64,128]{1,0:T(8,128)S(1)}, f32[64,128]{1,0:T(8,128)S(1)}, u32[]{:S(2)}, u32[]{:S(2)}) collective-permute-start(f32[64,128]{1,0:T(8,128)S(1)} %get-tuple-element.37), channel_id=1, source_target_pairs={{144,1},{176,225},{145,4},{177,228},{146,7},{178,231},{147,10},{17... | collective-permute-start | bytes 98312 | tf_op jit(solution)/shard_map/ppermute | solution.py:567
  21.6 6.3 %collective-permute-start.1 = (f32[56,128]{1,0:T(8,128)}, f32[56,128]{1,0:T(8,128)S(1)}, u32[]{:S(2)}, u32[]{:S(2)}) collective-permute-start(f32[56,128]{1,0:T(8,128)} %get-tuple-element.32), channel_id=1, source_target_pairs={{32,0},{64,32},{96,64},{128,96},{160,128},{192,160},{224,192},{33,... | collective-permute-start | bytes 86024 | tf_op jit(solution)/shard_map/ppermute | solution.py:572
  23.5 19.1 %collective-permute-start.7 = (f32[64,128]{1,0:T(8,128)S(1)}, f32[64,128]{1,0:T(8,128)S(1)}, u32[]{:S(2)}, u32[]{:S(2)}) collective-permute-start(f32[64,128]{1,0:T(8,128)S(1)} %get-tuple-element.38), channel_id=1, source_target_pairs={{144,2},{176,226},{145,5},{177,229},{146,8},{178,232},{147,11},{17... | collective-permute-start | bytes 98312 | tf_op jit(solution)/shard_map/ppermute | solution.py:567
  24.8 17.8 %collective-permute-start.8 = (f32[64,128]{1,0:T(8,128)S(1)}, f32[64,128]{1,0:T(8,128)S(1)}, u32[]{:S(2)}, u32[]{:S(2)}) collective-permute-start(f32[64,128]{1,0:T(8,128)S(1)} %get-tuple-element.39), channel_id=1, source_target_pairs={{145,0},{177,224},{146,3},{178,227},{147,6},{179,230},{148,9},{180... | collective-permute-start | bytes 98312 | tf_op jit(solution)/shard_map/ppermute | solution.py:567
  27.9 14.7 %collective-permute-start.9 = (f32[64,128]{1,0:T(8,128)S(1)}, f32[64,128]{1,0:T(8,128)S(1)}, u32[]{:S(2)}, u32[]{:S(2)}) collective-permute-start(f32[64,128]{1,0:T(8,128)S(1)} %get-tuple-element.40), channel_id=1, source_target_pairs={{145,1},{177,225},{146,4},{178,228},{147,7},{179,231},{148,10},{18... | collective-permute-start | bytes 98312 | tf_op jit(solution)/shard_map/ppermute | solution.py:567
  28.5 14.1 %collective-permute-start.10 = (f32[64,128]{1,0:T(8,128)S(1)}, f32[64,128]{1,0:T(8,128)S(1)}, u32[]{:S(2)}, u32[]{:S(2)}) collective-permute-start(f32[64,128]{1,0:T(8,128)S(1)} %get-tuple-element.41), channel_id=1, source_target_pairs={{145,2},{177,226},{146,5},{178,229},{147,8},{179,232},{148,11},{18... | collective-permute-start | bytes 98312 | tf_op jit(solution)/shard_map/ppermute | solution.py:567
  29.2 13.4 %copy-start = (f32[50,24,128]{2,1,0:T(8,128)S(1)}, f32[50,24,128]{2,1,0:T(8,128)}, u32[]{:S(2)}) copy-start(f32[50,24,128]{2,1,0:T(8,128)} %nu.5) | copy-start | bytes 1843204
  29.2 13.4 %copy-start.1 = (f32[2,50,24,128]{3,2,1,0:T(8,128)S(1)}, f32[2,50,24,128]{3,2,1,0:T(8,128)}, u32[]{:S(2)}) copy-start(f32[2,50,24,128]{3,2,1,0:T(8,128)} %kappa.3) | copy-start | bytes 3686404
  29.2 13.4 %copy-start.2 = (f32[50,24,128]{2,1,0:T(8,128)S(1)}, f32[50,24,128]{2,1,0:T(8,128)}, u32[]{:S(2)}) copy-start(f32[50,24,128]{2,1,0:T(8,128)} %a.3) | copy-start | bytes 1843204
  29.2 13.3 %collective-permute-start.11 = (f32[64,128]{1,0:T(8,128)S(1)}, f32[64,128]{1,0:T(8,128)S(1)}, u32[]{:S(2)}, u32[]{:S(2)}) collective-permute-start(f32[64,128]{1,0:T(8,128)S(1)} %get-tuple-element.42.after), channel_id=1, source_target_pairs={{146,2},{178,226},{147,5},{179,229},{148,8},{180,232},{149,11},{18... | collective-permute-start | bytes 98312 | tf_op jit(solution)/shard_map/ppermute | solution.py:567
  30.1 1.7 %copy-start.3 = (f32[2,50,48,128]{3,2,1,0:T(8,128)S(1)}, f32[2,50,48,128]{3,2,1,0:T(8,128)}, u32[]{:S(2)}) copy-start(f32[2,50,48,128]{3,2,1,0:T(8,128)} %pkappa.1) | copy-start | bytes 7372804
  31.7 10.9 %copy-start.11 = (s32[24,128]{1,0:T(8,128)S(1)}, s32[24,128]{1,0:T(8,128)}, u32[]{:S(2)}) copy-start(s32[24,128]{1,0:T(8,128)} %mask.5) | copy-start | bytes 36868
  33.9 11.2 %copy-start.7 = (f32[2,50,8,128]{3,2,1,0:T(8,128)}, f32[2,50,8,128]{3,2,1,0:T(8,128)S(1)}, u32[]{:S(2)}) copy-start(f32[2,50,8,128]{3,2,1,0:T(8,128)S(1)} %get-tuple-element.50.row_k) | copy-start | bytes 1228804
  33.9 11.2 %copy-start.12 = (f32[48,128]{1,0:T(8,128)}, f32[48,128]{1,0:T(8,128)S(1)}, u32[]{:S(2)}) copy-start(f32[48,128]{1,0:T(8,128)S(1)} %get-tuple-element.53.col_r) | copy-start | bytes 73732
  45.1 39.0 %copy-start.5 = (f32[50,24,128]{2,1,0:T(8,128)}, f32[50,24,128]{2,1,0:T(8,128)S(1)}, u32[]{:S(2)}) copy-start(f32[50,24,128]{2,1,0:T(8,128)S(1)} %get-tuple-element.44.a) | copy-start | bytes 1843204
  45.1 14.0 %collective-permute-start.13 = (f32[112,128]{1,0:T(8,128)S(1)}, f32[112,128]{1,0:T(8,128)S(1)}, u32[]{:S(2)}, u32[]{:S(2)}) collective-permute-start(f32[112,128]{1,0:T(8,128)S(1)} %get-tuple-element.49), channel_id=1, source_target_pairs={{32,0},{64,32},{96,64},{128,96},{160,128},{192,160},{224,192},{33,... | collective-permute-start | bytes 172040 | tf_op jit(solution)/shard_map/ppermute | solution.py:572
  47.6 11.5 %collective-permute-start.12 = (f32[112,128]{1,0:T(8,128)S(1)}, f32[112,128]{1,0:T(8,128)S(1)}, u32[]{:S(2)}, u32[]{:S(2)}) collective-permute-start(f32[112,128]{1,0:T(8,128)S(1)} %get-tuple-element.48), channel_id=1, source_target_pairs={{0,128},{1,129},{2,130},{3,131},{4,132},{5,133},{6,134},{7,135},{8... | collective-permute-start | bytes 172040 | tf_op jit(solution)/shard_map/ppermute | solution.py:567
  52.7 6.3 %collective-permute-start.14 = (f32[50,128]{1,0:T(8,128)S(1)}, f32[50,128]{1,0:T(8,128)S(1)}, u32[]{:S(2)}, u32[]{:S(2)}) collective-permute-start(f32[50,128]{1,0:T(8,128)S(1)} %slice.3), channel_id=1, source_target_pairs={{0,32},{1,33},{2,34},{3,35},{4,36},{5,37},{6,38},{7,39},{8,40},{9,... | collective-permute-start | bytes 76808 | tf_op jit(solution)/shard_map/ppermute | solution.py:567
  84.1 7.7 %copy-start.10 = (f32[168,128]{1,0:T(8,128)S(1)}, f32[168,128]{1,0:T(8,128)}, u32[]{:S(2)}) copy-start(f32[168,128]{1,0:T(8,128)} %get-tuple-element.35.pay) | copy-start | bytes 258052
  84.8 15.1 %all-to-all-start.1 = ((f32[8,32,128]{2,1,0:T(8,128)}), f32[8,32,128]{2,1,0:T(8,128)S(1)}, u32[]{:S(2)}, u32[]{:S(2)}) async-start(f32[8,32,128]{2,1,0:T(8,128)} %turn.1), calls=%async_computation.1 | async-start | bytes 262144 | tf_op jit(solution)/shard_map/all_to_all | solution.py:666
  91.8 1.1 %copy-start.6 = (f32[50,24,128]{2,1,0:T(8,128)S(1)}, f32[50,24,128]{2,1,0:T(8,128)}, u32[]{:S(2)}) copy-start(f32[50,24,128]{2,1,0:T(8,128)} %copy-done.5) | copy-start | bytes 1843204
  92.9 1.0 copy-start.8
  99.9 0.7 copy-start.13

commit v4 on v3

--- a/solution.py
+++ b/solution.py
@@ -159,7 +159,7 @@
     to_down[56:120, :] = pay[104:168, :]
 
 
-def mix_kernel(o_col, pay, down, skip, after_left, after_right, *outs):
+def mix_kernel(o_col, pay, down, skip, after_left, after_right, after_up, after_base, *outs):
     g, x = lax.axis_index("gy"), lax.axis_index("gx")
     sig = o_col[0] - COL0
     own = pay[0:104, :] + jnp.where(g == 5, skip[0:104, :], 0.0)
@@ -611,15 +611,6 @@
     )
     h_left = shifted(v_right, "gx", GX, 1)
     h_right = shifted(v_left, "gx", GX, -1)
-    mixed = pl.pallas_call(
-        mix_kernel,
-        out_shape=(shape(SR, L),) * 7,
-        in_specs=[SM] + [VM] * 3 + [ANY] * 2,
-        out_specs=(VM,) * 7,
-        compiler_params=grant(4),
-        name="mix",
-    )(offset_col, pay, down, skip, h_left, h_right)
-    parts = [moved(message, pairs) for message, pairs in zip(mixed, panel_routes())]
     nest, parent = shape(K, NR, L), shape(K, PR, L)
     base, row_k, col_c, col_r = pl.pallas_call(
         base_kernel,
@@ -630,8 +621,16 @@
         compiler_params=grant(16),
         cost_estimate=pl.CostEstimate(flops=10000000, bytes_accessed=12000000, transcendentals=0),
         name="base",
-    )(*here, parent_adjoint, parent_kappa, mixed[6])
-
+    )(*here, parent_adjoint, parent_kappa, v_left)
+    mixed = pl.pallas_call(
+        mix_kernel,
+        out_shape=(shape(SR, L),) * 7,
+        in_specs=[SM] + [VM] * 3 + [ANY] * 4,
+        out_specs=(VM,) * 7,
+        compiler_params=grant(4),
+        name="mix",
+    )(offset_col, pay, down, skip, h_left, h_right, up, col_c)
+    parts = [moved(message, pairs) for message, pairs in zip(mixed, panel_routes())]
     state, to_up, to_down, v_left, v_right, side = pl.pallas_call(
         nest_kernel,
         out_shape=(nest, shape(112, L), shape(112, L), shape(NR, L), shape(NR, L), shape(16, L)),

time: 102 us -> 106 us (1.039)
  waiting for transfers between devices: 23.8 us -> 28.3 us
  starting transfers between devices: 34.6 us -> 33.1 us
    ppermute x10, waiting for transfers between devices: 13.7 us -> 23.9 us  [moved(): return lax.ppermute(value, ('gy', 'gx'), pairs)]
    ppermute x5, waiting for transfers between devices: 5.75 us -> 0.01 us  [shifted(): return lax.ppermute(value, axis, pairs)]
    ppermute x5, starting transfers between devices: 15.1 us -> 16.9 us  [shifted(): return lax.ppermute(value, axis, pairs)]
    ppermute x10, starting transfers between devices: 12.5 us -> 10.8 us  [moved(): return lax.ppermute(value, ('gy', 'gx'), pairs)]
    all_to_all x1, starting transfers between devices: 7.02 us -> 5.37 us  [on_device(): sides = lax.all_to_all(sides, 'gy', 0, 0)]
  transfers between devices with their start and end apart: 16 -> 16, of which waited for: 5 -> 3; matrix products, arithmetic and copies ran while one was open for 0% -> 0% of each run, Pallas kernels for 4% -> 4%
where the time goes in v4:
time: 106 us
  starting transfers between devices  33.1 us (31%)
  waiting for transfers between devices  28.3 us (27%)
  blocking collectives  25.8 us (24%)
  Pallas kernels  10.8 us (10%)
  local copies, waits for them, and re-layouts  5.25 us (5%)
  between operations  2.26 us (2%)
    all_to_all x1, blocking collectives, on_device(): across = lax.all_to_all(across, 'gx', 0, 0)  25.8 us
    ppermute x10, waiting for transfers between devices, moved(): return lax.ppermute(value, ('gy', 'gx'), pairs)  23.9 us
    ppermute x5, starting transfers between devices, shifted(): return lax.ppermute(value, axis, pairs)  16.9 us
    ppermute x10, starting transfers between devices, moved(): return lax.ppermute(value, ('gy', 'gx'), pairs)  10.8 us
    all_to_all x1, starting transfers between devices, on_device(): sides = lax.all_to_all(sides, 'gy', 0, 0)  5.37 us
    unnamed x28, local copies, waits for them, and re-layouts  5.25 us
    all_to_all x1, waiting for transfers between devices, on_device(): sides = lax.all_to_all(sides, 'gy', 0, 0)  4.35 us
    pallas_call x1, Pallas kernels, on_device(): pl.pallas_call(edge_kernel, out_shape=(shape(56, L), shape(120, L), shape...  2.45 us
  transfers between devices with their start and end apart: 16, of which 3 were waited for; matrix products, arithmetic and copies ran while one was open for 0% of the time, Pallas kernels for 4%

profile of v4, /device:TPU:1, one launch (start us, length us, event | category | flops | bytes accessed | tf_op | source)
XLA Modules:
  0.0 105.5 jit_solution(14765205973573600748)
XLA Ops:
  1.9 2.4 %edge.1 = (f32[56,128]{1,0:T(8,128)}, f32[120,128]{1,0:T(8,128)}, f32[24,128]{1,0:T(8,128)}, f32[24,128]{1,0:T(8,128)}, f32[168,128]{1,0:T(8,128)}) custom-call(s32[1]{0:T(128)S(6)} %copy.17.o_row, s32[1]{0:T(128)S(6)} %copy.18.o_col, f32[50,24,128]{2,1,0:T(8,128)} %a.3, f32[50,24,128]{2,1,0:T(8,128)} %nu.5, s32[24,128]{1,0:T(8,128)} %mask.5, ...), custom_call_target="tpu_custom_call" | custom-call | tf_op jit(solution)/shard_map/edge/pallas_call | solution.py:594
  4.4 0.7 collective-permute-start.4
  5.1 6.3 %collective-permute-start = (f32[120,128]{1,0:T(8,128)}, f32[120,128]{1,0:T(8,128)S(1)}, u32[]{:S(2)}, u32[]{:S(2)}) collective-permute-start(f32[120,128]{1,0:T(8,128)} %get-tuple-element.31), channel_id=1, source_target_pairs={{0,32},{32,64},{64,96},{96,128},{128,160},{160,192},{192,224},{1,3... | collective-permute-start | bytes 184328 | tf_op jit(solution)/shard_map/ppermute | solution.py:572
  11.4 1.9 %collective-permute-start.1 = (f32[56,128]{1,0:T(8,128)}, f32[56,128]{1,0:T(8,128)S(1)}, u32[]{:S(2)}, u32[]{:S(2)}) collective-permute-start(f32[56,128]{1,0:T(8,128)} %get-tuple-element.32), channel_id=1, source_target_pairs={{32,0},{64,32},{96,64},{128,96},{160,128},{192,160},{224,192},{33,... | collective-permute-start | bytes 86024 | tf_op jit(solution)/shard_map/ppermute | solution.py:572
  13.3 3.1 %collective-permute-start.2 = (f32[24,128]{1,0:T(8,128)}, f32[24,128]{1,0:T(8,128)S(1)}, u32[]{:S(2)}, u32[]{:S(2)}) collective-permute-start(f32[24,128]{1,0:T(8,128)} %get-tuple-element.33), channel_id=1, source_target_pairs={{0,1},{1,2},{2,3},{3,4},{4,5},{5,6},{6,7},{7,8},{8,9},{9,10},{10,1... | collective-permute-start | bytes 36872 | tf_op jit(solution)/shard_map/ppermute | solution.py:572
  16.4 1.4 %collective-permute-start.3 = (f32[24,128]{1,0:T(8,128)}, f32[24,128]{1,0:T(8,128)S(1)}, u32[]{:S(2)}, u32[]{:S(2)}) collective-permute-start(f32[24,128]{1,0:T(8,128)} %get-tuple-element.34.after), channel_id=1, source_target_pairs={{1,0},{2,1},{3,2},{4,3},{5,4},{6,5},{7,6},{8,7},{9,8},{10,9},{11,1... | collective-permute-start | bytes 36872 | tf_op jit(solution)/shard_map/ppermute | solution.py:572
  17.9 1.7 %copy-done.3 = f32[2,50,48,128]{3,2,1,0:T(8,128)S(1)} copy-done((f32[2,50,48,128]{3,2,1,0:T(8,128)S(1)}, f32[2,50,48,128]{3,2,1,0:T(8,128)}, u32[]{:S(2)}) %copy-start.3) | copy-done | bytes 2457624
  19.6 0.7 copy-done.13
  20.3 2.2 %base.1 = (f32[50,48,128]{2,1,0:T(8,128)}, f32[2,50,8,128]{3,2,1,0:T(8,128)S(1)}, f32[48,128]{1,0:T(8,128)S(1)}, f32[48,128]{1,0:T(8,128)S(1)}) custom-call(s32[1]{0:T(128)S(6)} %copy.17.o_row, s32[1]{0:T(128)S(6)} %copy.18.o_col, f32[50,48,128]{2,1,0:T(8,128)S(1)} %copy-done.4, f32[2,50,48,128]{3,2,1,0:T(8,128)S(1)} %copy-done.3, f32[24,128]{1,0:T(8,128)S(1)} %copy-done.13), custom_call_target="tpu_custom_call" | custom-call | flops 10000000 | bytes 12000000 | tf_op jit(solution)/shard_map/base/pallas_call | solution.py:615
  22.6 0.2 mix.1
  22.8 0.7 collective-permute-start.5
  23.4 0.7 collective-permute-start.6
  24.1 1.3 %collective-permute-start.7 = (f32[64,128]{1,0:T(8,128)S(1)}, f32[64,128]{1,0:T(8,128)S(1)}, u32[]{:S(2)}, u32[]{:S(2)}) collective-permute-start(f32[64,128]{1,0:T(8,128)S(1)} %get-tuple-element.39), channel_id=1, source_target_pairs={{144,2},{176,226},{145,5},{177,229},{146,8},{178,232},{147,11},{17... | collective-permute-start | bytes 98312 | tf_op jit(solution)/shard_map/ppermute | solution.py:567
  25.4 0.7 collective-permute-start.8
  26.1 0.7 collective-permute-start.9
  26.8 0.7 collective-permute-start.10
  27.4 0.7 collective-permute-start.11
  28.1 19.3 %collective-permute-done.7.rest_2_ = f32[64,128]{1,0:T(8,128)S(1)} collective-permute-done((f32[64,128]{1,0:T(8,128)S(1)}, f32[64,128]{1,0:T(8,128)S(1)}, u32[]{:S(2)}, u32[]{:S(2)}) %collective-permute-start.7) | collective-permute-done | bytes 32800 | tf_op jit(solution)/shard_map/ppermute | solution.py:567
  47.5 2.4 %nest.1 = (f32[50,24,128]{2,1,0:T(8,128)S(1)}, f32[112,128]{1,0:T(8,128)S(1)}, f32[112,128]{1,0:T(8,128)S(1)}, f32[24,128]{1,0:T(8,128)S(1)}, f32[24,128]{1,0:T(8,128)S(1)}, /*index=5*/f32[16,128]{1,0:T(8,128)S(1)}) custom-call(s32[1]{0:T(128)S(6)} %copy.17.o_row, s32[1]{0:T(128)S(6)} %copy.18.o_col, f32[50,24,128]{2,1,0:T(8,128)S(1)} %copy-done.2, ...), custom_call_target="tpu_custom_call" | custom-call | tf_op jit(solution)/shard_map/nest/pallas_call | solution.py:634
  49.9 4.2 %collective-permute-start.13 = (f32[112,128]{1,0:T(8,128)S(1)}, f32[112,128]{1,0:T(8,128)S(1)}, u32[]{:S(2)}, u32[]{:S(2)}) collective-permute-start(f32[112,128]{1,0:T(8,128)S(1)} %get-tuple-element.49), channel_id=1, source_target_pairs={{32,0},{64,32},{96,64},{128,96},{160,128},{192,160},{224,192},{33,... | collective-permute-start | bytes 172040 | tf_op jit(solution)/shard_map/ppermute | solution.py:572
  54.1 3.6 %collective-permute-start.12 = (f32[112,128]{1,0:T(8,128)S(1)}, f32[112,128]{1,0:T(8,128)S(1)}, u32[]{:S(2)}, u32[]{:S(2)}) collective-permute-start(f32[112,128]{1,0:T(8,128)S(1)} %get-tuple-element.48), channel_id=1, source_target_pairs={{0,128},{1,129},{2,130},{3,131},{4,132},{5,133},{6,134},{7,135},{8... | collective-permute-start | bytes 172040 | tf_op jit(solution)/shard_map/ppermute | solution.py:567
  57.7 1.3 %collective-permute-start.14 = (f32[50,128]{1,0:T(8,128)S(1)}, f32[50,128]{1,0:T(8,128)S(1)}, u32[]{:S(2)}, u32[]{:S(2)}) collective-permute-start(f32[50,128]{1,0:T(8,128)S(1)} %slice.3), channel_id=1, source_target_pairs={{0,32},{1,33},{2,34},{3,35},{4,36},{5,37},{6,38},{7,39},{8,40},{9,... | collective-permute-start | bytes 76808 | tf_op jit(solution)/shard_map/ppermute | solution.py:567
  59.0 4.6 %collective-permute-done.14.after.third = f32[50,128]{1,0:T(8,128)S(1)} collective-permute-done((f32[50,128]{1,0:T(8,128)S(1)}, f32[50,128]{1,0:T(8,128)S(1)}, u32[]{:S(2)}, u32[]{:S(2)}) %collective-permute-start.14) | collective-permute-done | bytes 25632 | tf_op jit(solution)/shard_map/ppermute | solution.py:567
  63.7 25.8 %all_to_all.10.across = f32[32,80,128]{2,1,0:T(8,128)S(1)} all-to-all(f32[32,80,128]{2,1,0:T(8,128)S(1)} %spread.1), channel_id=1, replica_groups=mesh['gy'=8,'gx'=32] {'gx'}, dimensions={0} | all-to-all | bytes 2621440 | tf_op jit(solution)/shard_map/all_to_all | solution.py:661
  89.5 0.7 turn.1
  90.2 5.4 %all-to-all-start.1 = ((f32[8,32,128]{2,1,0:T(8,128)}), f32[8,32,128]{2,1,0:T(8,128)S(1)}, u32[]{:S(2)}, u32[]{:S(2)}) async-start(f32[8,32,128]{2,1,0:T(8,128)} %turn.1), calls=%async_computation.1 | async-start | bytes 262144 | tf_op jit(solution)/shard_map/all_to_all | solution.py:665
  95.5 1.1 %copy-done.6 = f32[50,24,128]{2,1,0:T(8,128)S(1)} copy-done((f32[50,24,128]{2,1,0:T(8,128)S(1)}, f32[50,24,128]{2,1,0:T(8,128)}, u32[]{:S(2)}) %copy-start.6) | copy-done | bytes 614424
  96.6 1.0 copy-done.8
  97.6 1.7 %inner.1 = (f32[50,24,128]{2,1,0:T(8,128)}, f32[50,48,128]{2,1,0:T(8,128)}) custom-call(s32[1]{0:T(128)S(6)} %copy.17.o_row, s32[1]{0:T(128)S(6)} %copy.18.o_col, f32[50,24,128]{2,1,0:T(8,128)S(1)} %copy-done.6, f32[50,24,128]{2,1,0:T(8,128)S(1)} %copy-done, s32[24,128]{1,0:T(8,128)S(1)} %copy-done.10, ...), custom_call_target="tpu_custom_call", output_to_operand_aliasing={{1}: (12, {})} | custom-call | tf_op jit(solution)/shard_map/inner/pallas_call | solution.py:667
  99.3 4.4 %all-to-all-done.1.sides = f32[8,32,128]{2,1,0:T(8,128)S(1)} async-done(((f32[8,32,128]{2,1,0:T(8,128)}), f32[8,32,128]{2,1,0:T(8,128)S(1)}, u32[]{:S(2)}, u32[]{:S(2)}) %all-to-all-start.1) | async-done | bytes 131104 | tf_op jit(solution)/shard_map/all_to_all | solution.py:665
  103.7 0.7 copy-done.12
  104.4 1.1 %outer.1 = (f32[50,48,128]{2,1,0:T(8,128)}, f32[2,50,2,64]{3,2,1,0:T(2,128)}, f32[2,50,2,64]{3,2,1,0:T(2,128)}) custom-call(s32[1]{0:T(128)S(6)} %copy.17.o_row, s32[1]{0:T(128)S(6)} %copy.18.o_col, f32[8,32,128]{2,1,0:T(8,128)S(1)} %all-to-all-done.1.sides, ...), custom_call_target="tpu_custom_call", output_to_operand_aliasing={{0}: (5, {})} | custom-call | tf_op jit(solution)/shard_map/outer/pallas_call | solution.py:680
  (38 shorter events, 0.2 us)
Async XLA Ops:
  1.9 16.0 %copy-start.4 = (f32[50,48,128]{2,1,0:T(8,128)S(1)}, f32[50,48,128]{2,1,0:T(8,128)}, u32[]{:S(2)}) copy-start(f32[50,48,128]{2,1,0:T(8,128)} %q.1) | copy-start | bytes 3686404
  4.4 18.2 %collective-permute-start.4 = (f32[168,128]{1,0:T(8,128)}, f32[168,128]{1,0:T(8,128)S(1)}, u32[]{:S(2)}, u32[]{:S(2)}) collective-permute-start(f32[168,128]{1,0:T(8,128)} %get-tuple-element.35.pay), channel_id=1, source_target_pairs={{208,176},{209,177},{210,178},{211,179},{212,180},{213,181},{214,1... | collective-permute-start | bytes 258056 | tf_op jit(solution)/shard_map/ppermute | solution.py:567
  5.1 17.5 %collective-permute-start = (f32[120,128]{1,0:T(8,128)}, f32[120,128]{1,0:T(8,128)S(1)}, u32[]{:S(2)}, u32[]{:S(2)}) collective-permute-start(f32[120,128]{1,0:T(8,128)} %get-tuple-element.31), channel_id=1, source_target_pairs={{0,32},{32,64},{64,96},{96,128},{128,160},{160,192},{192,224},{1,3... | collective-permute-start | bytes 184328 | tf_op jit(solution)/shard_map/ppermute | solution.py:572
  11.4 11.2 %collective-permute-start.1 = (f32[56,128]{1,0:T(8,128)}, f32[56,128]{1,0:T(8,128)S(1)}, u32[]{:S(2)}, u32[]{:S(2)}) collective-permute-start(f32[56,128]{1,0:T(8,128)} %get-tuple-element.32), channel_id=1, source_target_pairs={{32,0},{64,32},{96,64},{128,96},{160,128},{192,160},{224,192},{33,... | collective-permute-start | bytes 86024 | tf_op jit(solution)/shard_map/ppermute | solution.py:572
  13.3 9.2 %collective-permute-start.2 = (f32[24,128]{1,0:T(8,128)}, f32[24,128]{1,0:T(8,128)S(1)}, u32[]{:S(2)}, u32[]{:S(2)}) collective-permute-start(f32[24,128]{1,0:T(8,128)} %get-tuple-element.33), channel_id=1, source_target_pairs={{0,1},{1,2},{2,3},{3,4},{4,5},{5,6},{6,7},{7,8},{8,9},{9,10},{10,1... | collective-permute-start | bytes 36872 | tf_op jit(solution)/shard_map/ppermute | solution.py:572
  16.4 31.0 %copy-start = (f32[50,24,128]{2,1,0:T(8,128)S(1)}, f32[50,24,128]{2,1,0:T(8,128)}, u32[]{:S(2)}) copy-start(f32[50,24,128]{2,1,0:T(8,128)} %nu.5) | copy-start | bytes 1843204
  16.4 31.0 %copy-start.1 = (f32[2,50,24,128]{3,2,1,0:T(8,128)S(1)}, f32[2,50,24,128]{3,2,1,0:T(8,128)}, u32[]{:S(2)}) copy-start(f32[2,50,24,128]{3,2,1,0:T(8,128)} %kappa.3) | copy-start | bytes 3686404
  16.4 31.0 %copy-start.2 = (f32[50,24,128]{2,1,0:T(8,128)S(1)}, f32[50,24,128]{2,1,0:T(8,128)}, u32[]{:S(2)}) copy-start(f32[50,24,128]{2,1,0:T(8,128)} %a.3) | copy-start | bytes 1843204
  16.4 6.1 %collective-permute-start.3 = (f32[24,128]{1,0:T(8,128)}, f32[24,128]{1,0:T(8,128)S(1)}, u32[]{:S(2)}, u32[]{:S(2)}) collective-permute-start(f32[24,128]{1,0:T(8,128)} %get-tuple-element.34.after), channel_id=1, source_target_pairs={{1,0},{2,1},{3,2},{4,3},{5,4},{6,5},{7,6},{8,7},{9,8},{10,9},{11,1... | collective-permute-start | bytes 36872 | tf_op jit(solution)/shard_map/ppermute | solution.py:572
  17.9 1.7 %copy-start.3 = (f32[2,50,48,128]{3,2,1,0:T(8,128)S(1)}, f32[2,50,48,128]{3,2,1,0:T(8,128)}, u32[]{:S(2)}) copy-start(f32[2,50,48,128]{3,2,1,0:T(8,128)} %pkappa.1) | copy-start | bytes 7372804
  19.6 0.7 copy-start.13
  20.3 2.3 %copy-start.9 = (f32[168,128]{1,0:T(8,128)S(1)}, f32[168,128]{1,0:T(8,128)}, u32[]{:S(2)}) copy-start(f32[168,128]{1,0:T(8,128)} %get-tuple-element.35.pay) | copy-start | bytes 258052
  20.3 27.2 %copy-start.10 = (s32[24,128]{1,0:T(8,128)S(1)}, s32[24,128]{1,0:T(8,128)}, u32[]{:S(2)}) copy-start(s32[24,128]{1,0:T(8,128)} %mask.5) | copy-start | bytes 36868
  22.5 27.3 %copy-start.7 = (f32[2,50,8,128]{3,2,1,0:T(8,128)}, f32[2,50,8,128]{3,2,1,0:T(8,128)S(1)}, u32[]{:S(2)}) copy-start(f32[2,50,8,128]{3,2,1,0:T(8,128)S(1)} %get-tuple-element.50.row_k) | copy-start | bytes 1228804
  22.5 27.3 %copy-start.11 = (f32[48,128]{1,0:T(8,128)}, f32[48,128]{1,0:T(8,128)S(1)}, u32[]{:S(2)}) copy-start(f32[48,128]{1,0:T(8,128)S(1)} %get-tuple-element.53.col_r) | copy-start | bytes 73732
  22.8 4.0 %collective-permute-start.5 = (f32[64,128]{1,0:T(8,128)S(1)}, f32[64,128]{1,0:T(8,128)S(1)}, u32[]{:S(2)}, u32[]{:S(2)}) collective-permute-start(f32[64,128]{1,0:T(8,128)S(1)} %get-tuple-element.37), channel_id=1, source_target_pairs={{144,0},{176,224},{145,3},{177,227},{146,6},{178,230},{147,9},{179... | collective-permute-start | bytes 98312 | tf_op jit(solution)/shard_map/ppermute | solution.py:567
  23.4 4.0 %collective-permute-start.6 = (f32[64,128]{1,0:T(8,128)S(1)}, f32[64,128]{1,0:T(8,128)S(1)}, u32[]{:S(2)}, u32[]{:S(2)}) collective-permute-start(f32[64,128]{1,0:T(8,128)S(1)} %get-tuple-element.38), channel_id=1, source_target_pairs={{144,1},{176,225},{145,4},{177,228},{146,7},{178,231},{147,10},{17... | collective-permute-start | bytes 98312 | tf_op jit(solution)/shard_map/ppermute | solution.py:567
  24.1 23.3 %collective-permute-start.7 = (f32[64,128]{1,0:T(8,128)S(1)}, f32[64,128]{1,0:T(8,128)S(1)}, u32[]{:S(2)}, u32[]{:S(2)}) collective-permute-start(f32[64,128]{1,0:T(8,128)S(1)} %get-tuple-element.39), channel_id=1, source_target_pairs={{144,2},{176,226},{145,5},{177,229},{146,8},{178,232},{147,11},{17... | collective-permute-start | bytes 98312 | tf_op jit(solution)/shard_map/ppermute | solution.py:567
  25.4 22.0 %collective-permute-start.8 = (f32[64,128]{1,0:T(8,128)S(1)}, f32[64,128]{1,0:T(8,128)S(1)}, u32[]{:S(2)}, u32[]{:S(2)}) collective-permute-start(f32[64,128]{1,0:T(8,128)S(1)} %get-tuple-element.40), channel_id=1, source_target_pairs={{145,0},{177,224},{146,3},{178,227},{147,6},{179,230},{148,9},{180... | collective-permute-start | bytes 98312 | tf_op jit(solution)/shard_map/ppermute | solution.py:567
  26.1 21.3 %collective-permute-start.9 = (f32[64,128]{1,0:T(8,128)S(1)}, f32[64,128]{1,0:T(8,128)S(1)}, u32[]{:S(2)}, u32[]{:S(2)}) collective-permute-start(f32[64,128]{1,0:T(8,128)S(1)} %get-tuple-element.41), channel_id=1, source_target_pairs={{145,1},{177,225},{146,4},{178,228},{147,7},{179,231},{148,10},{18... | collective-permute-start | bytes 98312 | tf_op jit(solution)/shard_map/ppermute | solution.py:567
  26.8 20.6 %collective-permute-start.10 = (f32[64,128]{1,0:T(8,128)S(1)}, f32[64,128]{1,0:T(8,128)S(1)}, u32[]{:S(2)}, u32[]{:S(2)}) collective-permute-start(f32[64,128]{1,0:T(8,128)S(1)} %get-tuple-element.42), channel_id=1, source_target_pairs={{145,2},{177,226},{146,5},{178,229},{147,8},{179,232},{148,11},{18... | collective-permute-start | bytes 98312 | tf_op jit(solution)/shard_map/ppermute | solution.py:567
  27.4 20.0 %collective-permute-start.11 = (f32[64,128]{1,0:T(8,128)S(1)}, f32[64,128]{1,0:T(8,128)S(1)}, u32[]{:S(2)}, u32[]{:S(2)}) collective-permute-start(f32[64,128]{1,0:T(8,128)S(1)} %get-tuple-element.43), channel_id=1, source_target_pairs={{146,2},{178,226},{147,5},{179,229},{148,8},{180,232},{149,11},{18... | collective-permute-start | bytes 98312 | tf_op jit(solution)/shard_map/ppermute | solution.py:567
  49.9 39.6 %copy-start.5 = (f32[50,24,128]{2,1,0:T(8,128)}, f32[50,24,128]{2,1,0:T(8,128)S(1)}, u32[]{:S(2)}) copy-start(f32[50,24,128]{2,1,0:T(8,128)S(1)} %get-tuple-element.44.a) | copy-start | bytes 1843204
  49.9 13.7 %collective-permute-start.13 = (f32[112,128]{1,0:T(8,128)S(1)}, f32[112,128]{1,0:T(8,128)S(1)}, u32[]{:S(2)}, u32[]{:S(2)}) collective-permute-start(f32[112,128]{1,0:T(8,128)S(1)} %get-tuple-element.49), channel_id=1, source_target_pairs={{32,0},{64,32},{96,64},{128,96},{160,128},{192,160},{224,192},{33,... | collective-permute-start | bytes 172040 | tf_op jit(solution)/shard_map/ppermute | solution.py:572
  54.1 9.5 %collective-permute-start.12 = (f32[112,128]{1,0:T(8,128)S(1)}, f32[112,128]{1,0:T(8,128)S(1)}, u32[]{:S(2)}, u32[]{:S(2)}) collective-permute-start(f32[112,128]{1,0:T(8,128)S(1)} %get-tuple-element.48), channel_id=1, source_target_pairs={{0,128},{1,129},{2,130},{3,131},{4,132},{5,133},{6,134},{7,135},{8... | collective-permute-start | bytes 172040 | tf_op jit(solution)/shard_map/ppermute | solution.py:567
  57.7 5.9 %collective-permute-start.14 = (f32[50,128]{1,0:T(8,128)S(1)}, f32[50,128]{1,0:T(8,128)S(1)}, u32[]{:S(2)}, u32[]{:S(2)}) collective-permute-start(f32[50,128]{1,0:T(8,128)S(1)} %slice.3), channel_id=1, source_target_pairs={{0,32},{1,33},{2,34},{3,35},{4,36},{5,37},{6,38},{7,39},{8,40},{9,... | collective-permute-start | bytes 76808 | tf_op jit(solution)/shard_map/ppermute | solution.py:567
  90.2 13.5 %all-to-all-start.1 = ((f32[8,32,128]{2,1,0:T(8,128)}), f32[8,32,128]{2,1,0:T(8,128)S(1)}, u32[]{:S(2)}, u32[]{:S(2)}) async-start(f32[8,32,128]{2,1,0:T(8,128)} %turn.1), calls=%async_computation.1 | async-start | bytes 262144 | tf_op jit(solution)/shard_map/all_to_all | solution.py:665
  95.5 1.1 %copy-start.6 = (f32[50,24,128]{2,1,0:T(8,128)S(1)}, f32[50,24,128]{2,1,0:T(8,128)}, u32[]{:S(2)}) copy-start(f32[50,24,128]{2,1,0:T(8,128)} %copy-done.5) | copy-start | bytes 1843204
  96.6 1.0 copy-start.8
  103.7 0.7 copy-start.12

commit v5 on v3

--- a/solution.py
+++ b/solution.py
@@ -486,7 +486,7 @@
         back.wait()
 
 
-def outer_kernel(o_row, o_col, sides, col_c, col_r, q, q_out, s_w, s_g, panel_s, local_s, d_s, q_s, sems):
+def outer_kernel(o_row, o_col, sides, col_c, col_r, q, q_out, s_w, s_g, panel_s, local_s, d_s, q_s, turned_s, y_s, sems):
     g, x, oy, ox = place(o_row, o_col)
     is_west, is_east, spot = side_lane(x, ox)
     side_ok = (is_west | is_east) & (g >= SOUTH) & (g < GY - 1)
@@ -523,30 +523,29 @@
         above = jnp.where((lane == 0) | (lane == 64), 0.0, pltpu.roll(cs, 1, 1)) * rs
         below = cs * rs
         own = own * rs
-        own, above, below, rs = (pltpu.roll(v, spot, 1) for v in (own, above, below, rs))
-
-        def column(values, i):
-            return to_first(values, i)
-
-        zero = jnp.zeros((PR, L), F32)
-        for step, first in ((1, 0), (0, 64)):
-            y = zero
-            for k in range(K):
-                term = column(own, first + k)
-                if step == 0:
-                    term = term + d_s[k] * column(rs, first + k)
-                y = term + column(above, first + k) * y
-                d_s[k] = y
-            if step == 1:
-                for k in range(K - 2, -1, -1):
-                    y = d_s[k] + column(below, first + k) * y
-                    d_s[k] = y
+        for i, values in enumerate((own, above, below, rs)):
+            turned_s[i] = jnp.concatenate([values, jnp.zeros((L - PR, L), F32)], 0).T
+        y_s[...] = jnp.zeros(y_s.shape, F32)
+
+        def level(i, k):
+            return turned_s[i, pl.ds(k, 1), :]
+
+        for first in (0, 64):
+            y = jnp.zeros((1, L), F32)
+            for k in range(first, first + K):
+                term = level(0, k)
+                if first:
+                    term = term + y_s[pl.ds(k - first, 1), :] * level(3, k)
+                y = term + level(1, k) * y
+                y_s[pl.ds(k, 1), :] = y
+            for k in range(first + K - 2, first - 1, -1):
+                y = y_s[pl.ds(k, 1), :] + level(2, k) * y
+                y_s[pl.ds(k, 1), :] = y
+        share = pltpu.roll(y_s[...].T[0:PR], spot, 1)
         whole_copy().wait()
-        d_s[K - 1] = jnp.where(here, y, 0.0) + q_s[K - 1]
         copies = []
-        for k in range(K - 2, -1, -1):
-            y = d_s[k] + column(below, 64 + k) * y
-            d_s[k] = jnp.where(here, y, 0.0) + q_s[k]
+        for k in range(K - 1, -1, -1):
+            d_s[k] = jnp.where(here, to_first(share, 64 + k), 0.0) + q_s[k]
             if k % 10 == 0:
                 part = pl.ds(k, 10)
                 copies.append(pltpu.make_async_copy(d_s.at[part], q_out.at[part], sems.at[1 + k // 10]))
@@ -685,7 +684,7 @@
         out_specs=(HB, VM, VM),
         scratch_shapes=[
             pltpu.VMEM((256, L), F32), pltpu.VMEM((PR, L), F32), pltpu.VMEM((K, PR, L), F32), pltpu.VMEM((K, PR, L), F32),
-            pltpu.SemaphoreType.DMA((6,)),
+            pltpu.VMEM((4, L, L), F32), pltpu.VMEM((L, L), F32), pltpu.SemaphoreType.DMA((6,)),
         ],
         input_output_aliases={5: 0},
         compiler_params=grant(12),

time: 102 us -> 102 us (level)
    ppermute x10, starting transfers between devices: 12.5 us -> 10.9 us  [moved(): return lax.ppermute(value, ('gy', 'gx'), pairs)]
    ppermute x5, starting transfers between devices: 15.1 us -> 16.5 us  [shifted(): return lax.ppermute(value, axis, pairs)]
where the time goes in v5:
time: 102 us; the launch traced here: 101 us
  starting transfers between devices  33.6 us (33%)
  blocking collectives  25.6 us (25%)
  waiting for transfers between devices  23.5 us (23%)
  Pallas kernels  10.7 us (10%)
  local copies, waits for them, and re-layouts  5.44 us (5%)
  between operations  2.23 us (2%)
    all_to_all x1, blocking collectives, on_device(): across = lax.all_to_all(across, 'gx', 0, 0)  25.6 us
    ppermute x5, starting transfers between devices, shifted(): return lax.ppermute(value, axis, pairs)  16.5 us
    ppermute x10, waiting for transfers between devices, moved(): return lax.ppermute(value, ('gy', 'gx'), pairs)  13.5 us
    ppermute x10, starting transfers between devices, moved(): return lax.ppermute(value, ('gy', 'gx'), pairs)  10.9 us
    all_to_all x1, starting transfers between devices, on_device(): sides = lax.all_to_all(sides, 'gy', 0, 0)  6.27 us
    ppermute x5, waiting for transfers between devices, shifted(): return lax.ppermute(value, axis, pairs)  5.75 us
    unnamed x28, local copies, waits for them, and re-layouts  5.43 us
    all_to_all x1, waiting for transfers between devices, on_device(): sides = lax.all_to_all(sides, 'gy', 0, 0)  4.3 us
  transfers between devices with their start and end apart: 16, of which 5 were waited for; matrix products, arithmetic and copies ran while one was open for 0% of the time, Pallas kernels for 4%

profile of v5, /device:TPU:1, one launch (start us, length us, event | category | flops | bytes accessed | tf_op | source)
XLA Modules:
  0.0 101.2 jit_solution(16821437927866609649)
XLA Ops:
  1.9 2.4 %edge.1 = (f32[56,128]{1,0:T(8,128)}, f32[120,128]{1,0:T(8,128)}, f32[24,128]{1,0:T(8,128)}, f32[24,128]{1,0:T(8,128)}, f32[168,128]{1,0:T(8,128)}) custom-call(s32[1]{0:T(128)S(6)} %copy.17.o_row, s32[1]{0:T(128)S(6)} %copy.18.o_col, f32[50,24,128]{2,1,0:T(8,128)} %a.3, f32[50,24,128]{2,1,0:T(8,128)} %nu.5, s32[24,128]{1,0:T(8,128)} %mask.5, ...), custom_call_target="tpu_custom_call" | custom-call | tf_op jit(solution)/shard_map/edge/pallas_call | solution.py:593
  4.4 0.7 collective-permute-start.4
  5.1 6.3 %collective-permute-start = (f32[120,128]{1,0:T(8,128)}, f32[120,128]{1,0:T(8,128)S(1)}, u32[]{:S(2)}, u32[]{:S(2)}) collective-permute-start(f32[120,128]{1,0:T(8,128)} %get-tuple-element.31), channel_id=1, source_target_pairs={{0,32},{32,64},{64,96},{96,128},{128,160},{160,192},{192,224},{1,3... | collective-permute-start | bytes 184328 | tf_op jit(solution)/shard_map/ppermute | solution.py:571
  11.4 3.1 %collective-permute-start.2 = (f32[24,128]{1,0:T(8,128)}, f32[24,128]{1,0:T(8,128)S(1)}, u32[]{:S(2)}, u32[]{:S(2)}) collective-permute-start(f32[24,128]{1,0:T(8,128)} %get-tuple-element.33), channel_id=1, source_target_pairs={{0,1},{1,2},{2,3},{3,4},{4,5},{5,6},{6,7},{7,8},{8,9},{9,10},{10,1... | collective-permute-start | bytes 36872 | tf_op jit(solution)/shard_map/ppermute | solution.py:571
  14.5 1.3 %collective-permute-start.3 = (f32[24,128]{1,0:T(8,128)}, f32[24,128]{1,0:T(8,128)S(1)}, u32[]{:S(2)}, u32[]{:S(2)}) collective-permute-start(f32[24,128]{1,0:T(8,128)} %get-tuple-element.34), channel_id=1, source_target_pairs={{1,0},{2,1},{3,2},{4,3},{5,4},{6,5},{7,6},{8,7},{9,8},{10,9},{11,1... | collective-permute-start | bytes 36872 | tf_op jit(solution)/shard_map/ppermute | solution.py:571
  15.8 3.3 %collective-permute-done.3.after_right.h_right = f32[24,128]{1,0:T(8,128)S(1)} collective-permute-done((f32[24,128]{1,0:T(8,128)}, f32[24,128]{1,0:T(8,128)S(1)}, u32[]{:S(2)}, u32[]{:S(2)}) %collective-permute-start.3) | collective-permute-done | bytes 12320 | tf_op jit(solution)/shard_map/ppermute | solution.py:571
  19.1 0.9 copy-done.9
  20.2 0.7 collective-permute-start.5
  20.9 0.7 collective-permute-start.6
  21.6 1.9 %collective-permute-start.1 = (f32[56,128]{1,0:T(8,128)}, f32[56,128]{1,0:T(8,128)S(1)}, u32[]{:S(2)}, u32[]{:S(2)}) collective-permute-start(f32[56,128]{1,0:T(8,128)} %get-tuple-element.32), channel_id=1, source_target_pairs={{32,0},{64,32},{96,64},{128,96},{160,128},{192,160},{224,192},{33,... | collective-permute-start | bytes 86024 | tf_op jit(solution)/shard_map/ppermute | solution.py:571
  23.5 1.3 %collective-permute-start.7 = (f32[64,128]{1,0:T(8,128)S(1)}, f32[64,128]{1,0:T(8,128)S(1)}, u32[]{:S(2)}, u32[]{:S(2)}) collective-permute-start(f32[64,128]{1,0:T(8,128)S(1)} %get-tuple-element.38), channel_id=1, source_target_pairs={{144,2},{176,226},{145,5},{177,229},{146,8},{178,232},{147,11},{17... | collective-permute-start | bytes 98312 | tf_op jit(solution)/shard_map/ppermute | solution.py:566
  24.8 0.7 collective-permute-start.8
  25.5 2.4 %collective-permute-done.1.h_down = f32[56,128]{1,0:T(8,128)S(1)} collective-permute-done((f32[56,128]{1,0:T(8,128)}, f32[56,128]{1,0:T(8,128)S(1)}, u32[]{:S(2)}, u32[]{:S(2)}) %collective-permute-start.1) | collective-permute-done | bytes 28704 | tf_op jit(solution)/shard_map/ppermute | solution.py:571
  28.5 0.7 collective-permute-start.10
  29.2 0.8 collective-permute-start.11
  30.1 1.7 %copy-done.3 = f32[2,50,48,128]{3,2,1,0:T(8,128)S(1)} copy-done((f32[2,50,48,128]{3,2,1,0:T(8,128)S(1)}, f32[2,50,48,128]{3,2,1,0:T(8,128)}, u32[]{:S(2)}) %copy-start.3) | copy-done | bytes 2457624
  31.8 2.1 %base.1 = (f32[50,48,128]{2,1,0:T(8,128)}, f32[2,50,8,128]{3,2,1,0:T(8,128)S(1)}, f32[48,128]{1,0:T(8,128)S(1)}, f32[48,128]{1,0:T(8,128)S(1)}) custom-call(s32[1]{0:T(128)S(6)} %copy.17.o_row, s32[1]{0:T(128)S(6)} %copy.18.o_col, f32[50,48,128]{2,1,0:T(8,128)S(1)} %copy-done.4, f32[2,50,48,128]{3,2,1,0:T(8,128)S(1)} %copy-done.3, ...), custom_call_target="tpu_custom_call" | custom-call | flops 10000000 | bytes 12000000 | tf_op jit(solution)/shard_map/base/pallas_call | solution.py:623
  33.9 8.1 %collective-permute-done.7.rest_2_ = f32[64,128]{1,0:T(8,128)S(1)} collective-permute-done((f32[64,128]{1,0:T(8,128)S(1)}, f32[64,128]{1,0:T(8,128)S(1)}, u32[]{:S(2)}, u32[]{:S(2)}) %collective-permute-start.7) | collective-permute-done | bytes 32800 | tf_op jit(solution)/shard_map/ppermute | solution.py:566
  42.1 2.4 %nest.1 = (f32[50,24,128]{2,1,0:T(8,128)S(1)}, f32[112,128]{1,0:T(8,128)S(1)}, f32[112,128]{1,0:T(8,128)S(1)}, f32[24,128]{1,0:T(8,128)S(1)}, f32[24,128]{1,0:T(8,128)S(1)}, /*index=5*/f32[16,128]{1,0:T(8,128)S(1)}) custom-call(s32[1]{0:T(128)S(6)} %copy.17.o_row, s32[1]{0:T(128)S(6)} %copy.18.o_col, f32[50,24,128]{2,1,0:T(8,128)S(1)} %copy-done.2, ...), custom_call_target="tpu_custom_call" | custom-call | tf_op jit(solution)/shard_map/nest/pallas_call | solution.py:634
  44.5 3.9 %collective-permute-start.13 = (f32[112,128]{1,0:T(8,128)S(1)}, f32[112,128]{1,0:T(8,128)S(1)}, u32[]{:S(2)}, u32[]{:S(2)}) collective-permute-start(f32[112,128]{1,0:T(8,128)S(1)} %get-tuple-element.49), channel_id=1, source_target_pairs={{32,0},{64,32},{96,64},{128,96},{160,128},{192,160},{224,192},{33,... | collective-permute-start | bytes 172040 | tf_op jit(solution)/shard_map/ppermute | solution.py:571
  48.4 3.5 %collective-permute-start.12 = (f32[112,128]{1,0:T(8,128)S(1)}, f32[112,128]{1,0:T(8,128)S(1)}, u32[]{:S(2)}, u32[]{:S(2)}) collective-permute-start(f32[112,128]{1,0:T(8,128)S(1)} %get-tuple-element.48), channel_id=1, source_target_pairs={{0,128},{1,129},{2,130},{3,131},{4,132},{5,133},{6,134},{7,135},{8... | collective-permute-start | bytes 172040 | tf_op jit(solution)/shard_map/ppermute | solution.py:566
  51.9 1.3 %collective-permute-start.14 = (f32[50,128]{1,0:T(8,128)S(1)}, f32[50,128]{1,0:T(8,128)S(1)}, u32[]{:S(2)}, u32[]{:S(2)}) collective-permute-start(f32[50,128]{1,0:T(8,128)S(1)} %slice.3), channel_id=1, source_target_pairs={{0,32},{1,33},{2,34},{3,35},{4,36},{5,37},{6,38},{7,39},{8,40},{9,... | collective-permute-start | bytes 76808 | tf_op jit(solution)/shard_map/ppermute | solution.py:566
  53.2 5.4 %collective-permute-done.14.after.third = f32[50,128]{1,0:T(8,128)S(1)} collective-permute-done((f32[50,128]{1,0:T(8,128)S(1)}, f32[50,128]{1,0:T(8,128)S(1)}, u32[]{:S(2)}, u32[]{:S(2)}) %collective-permute-start.14) | collective-permute-done | bytes 25632 | tf_op jit(solution)/shard_map/ppermute | solution.py:566
  58.7 25.6 %all_to_all.10.across = f32[32,80,128]{2,1,0:T(8,128)S(1)} all-to-all(f32[32,80,128]{2,1,0:T(8,128)S(1)} %spread.1), channel_id=1, replica_groups=mesh['gy'=8,'gx'=32] {'gx'}, dimensions={0} | all-to-all | bytes 2621440 | tf_op jit(solution)/shard_map/all_to_all | solution.py:661
  84.3 0.7 turn.1
  85.0 6.3 %all-to-all-start.1 = ((f32[8,32,128]{2,1,0:T(8,128)}), f32[8,32,128]{2,1,0:T(8,128)S(1)}, u32[]{:S(2)}, u32[]{:S(2)}) async-start(f32[8,32,128]{2,1,0:T(8,128)} %turn.1), calls=%async_computation.1 | async-start | bytes 262144 | tf_op jit(solution)/shard_map/all_to_all | solution.py:665
  91.3 1.1 %copy-done.6 = f32[50,24,128]{2,1,0:T(8,128)S(1)} copy-done((f32[50,24,128]{2,1,0:T(8,128)S(1)}, f32[50,24,128]{2,1,0:T(8,128)}, u32[]{:S(2)}) %copy-start.6) | copy-done | bytes 614424
  92.3 1.0 copy-done.8
  93.3 1.7 %inner.1 = (f32[50,24,128]{2,1,0:T(8,128)}, f32[50,48,128]{2,1,0:T(8,128)}) custom-call(s32[1]{0:T(128)S(6)} %copy.17.o_row, s32[1]{0:T(128)S(6)} %copy.18.o_col, f32[50,24,128]{2,1,0:T(8,128)S(1)} %copy-done.6, f32[50,24,128]{2,1,0:T(8,128)S(1)} %copy-done, s32[24,128]{1,0:T(8,128)S(1)} %copy-done.11, ...), custom_call_target="tpu_custom_call", output_to_operand_aliasing={{1}: (12, {})} | custom-call | tf_op jit(solution)/shard_map/inner/pallas_call | solution.py:667
  95.1 4.3 %all-to-all-done.1.sides = f32[8,32,128]{2,1,0:T(8,128)S(1)} async-done(((f32[8,32,128]{2,1,0:T(8,128)}), f32[8,32,128]{2,1,0:T(8,128)S(1)}, u32[]{:S(2)}, u32[]{:S(2)}) %all-to-all-start.1) | async-done | bytes 131104 | tf_op jit(solution)/shard_map/all_to_all | solution.py:665
  99.4 0.7 copy-done.13
  100.1 1.1 %outer.1 = (f32[50,48,128]{2,1,0:T(8,128)}, f32[2,50,2,64]{3,2,1,0:T(2,128)}, f32[2,50,2,64]{3,2,1,0:T(2,128)}) custom-call(s32[1]{0:T(128)S(6)} %copy.17.o_row, s32[1]{0:T(128)S(6)} %copy.18.o_col, f32[8,32,128]{2,1,0:T(8,128)S(1)} %all-to-all-done.1.sides, f32[48,128]{1,0:T(8,128)S(1)} %get-tuple-element.43.rest_7_.col_c, ...), custom_call_target="tpu_custom_call", output_to_operand_aliasing={{0}: (5, {})} | custom-call | tf_op jit(solution)/shard_map/outer/pallas_call | solution.py:680
  (38 shorter events, 1.0 us)
Async XLA Ops:
  1.9 28.1 %copy-start.4 = (f32[50,48,128]{2,1,0:T(8,128)S(1)}, f32[50,48,128]{2,1,0:T(8,128)}, u32[]{:S(2)}) copy-start(f32[50,48,128]{2,1,0:T(8,128)} %q.1) | copy-start | bytes 3686404
  4.4 14.8 %collective-permute-start.4 = (f32[168,128]{1,0:T(8,128)}, f32[168,128]{1,0:T(8,128)S(1)}, u32[]{:S(2)}, u32[]{:S(2)}) collective-permute-start(f32[168,128]{1,0:T(8,128)} %get-tuple-element.35.pay), channel_id=1, source_target_pairs={{208,176},{209,177},{210,178},{211,179},{212,180},{213,181},{214,1... | collective-permute-start | bytes 258056 | tf_op jit(solution)/shard_map/ppermute | solution.py:566
  5.1 14.1 %collective-permute-start = (f32[120,128]{1,0:T(8,128)}, f32[120,128]{1,0:T(8,128)S(1)}, u32[]{:S(2)}, u32[]{:S(2)}) collective-permute-start(f32[120,128]{1,0:T(8,128)} %get-tuple-element.31), channel_id=1, source_target_pairs={{0,32},{32,64},{64,96},{96,128},{128,160},{160,192},{192,224},{1,3... | collective-permute-start | bytes 184328 | tf_op jit(solution)/shard_map/ppermute | solution.py:571
  11.4 4.4 %collective-permute-start.2 = (f32[24,128]{1,0:T(8,128)}, f32[24,128]{1,0:T(8,128)S(1)}, u32[]{:S(2)}, u32[]{:S(2)}) collective-permute-start(f32[24,128]{1,0:T(8,128)} %get-tuple-element.33), channel_id=1, source_target_pairs={{0,1},{1,2},{2,3},{3,4},{4,5},{5,6},{6,7},{7,8},{8,9},{9,10},{10,1... | collective-permute-start | bytes 36872 | tf_op jit(solution)/shard_map/ppermute | solution.py:571
  14.5 4.6 %collective-permute-start.3 = (f32[24,128]{1,0:T(8,128)}, f32[24,128]{1,0:T(8,128)S(1)}, u32[]{:S(2)}, u32[]{:S(2)}) collective-permute-start(f32[24,128]{1,0:T(8,128)} %get-tuple-element.34), channel_id=1, source_target_pairs={{1,0},{2,1},{3,2},{4,3},{5,4},{6,5},{7,6},{8,7},{9,8},{10,9},{11,1... | collective-permute-start | bytes 36872 | tf_op jit(solution)/shard_map/ppermute | solution.py:571
  19.1 0.9 copy-start.9
  20.2 8.3 %collective-permute-start.5 = (f32[64,128]{1,0:T(8,128)S(1)}, f32[64,128]{1,0:T(8,128)S(1)}, u32[]{:S(2)}, u32[]{:S(2)}) collective-permute-start(f32[64,128]{1,0:T(8,128)S(1)} %get-tuple-element.36), channel_id=1, source_target_pairs={{144,0},{176,224},{145,3},{177,227},{146,6},{178,230},{147,9},{179... | collective-permute-start | bytes 98312 | tf_op jit(solution)/shard_map/ppermute | solution.py:566
  20.9 8.3 %collective-permute-start.6 = (f32[64,128]{1,0:T(8,128)S(1)}, f32[64,128]{1,0:T(8,128)S(1)}, u32[]{:S(2)}, u32[]{:S(2)}) collective-permute-start(f32[64,128]{1,0:T(8,128)S(1)} %get-tuple-element.37), channel_id=1, source_target_pairs={{144,1},{176,225},{145,4},{177,228},{146,7},{178,231},{147,10},{17... | collective-permute-start | bytes 98312 | tf_op jit(solution)/shard_map/ppermute | solution.py:566
  21.6 6.3 %collective-permute-start.1 = (f32[56,128]{1,0:T(8,128)}, f32[56,128]{1,0:T(8,128)S(1)}, u32[]{:S(2)}, u32[]{:S(2)}) collective-permute-start(f32[56,128]{1,0:T(8,128)} %get-tuple-element.32), channel_id=1, source_target_pairs={{32,0},{64,32},{96,64},{128,96},{160,128},{192,160},{224,192},{33,... | collective-permute-start | bytes 86024 | tf_op jit(solution)/shard_map/ppermute | solution.py:571
  23.5 18.5 %collective-permute-start.7 = (f32[64,128]{1,0:T(8,128)S(1)}, f32[64,128]{1,0:T(8,128)S(1)}, u32[]{:S(2)}, u32[]{:S(2)}) collective-permute-start(f32[64,128]{1,0:T(8,128)S(1)} %get-tuple-element.38), channel_id=1, source_target_pairs={{144,2},{176,226},{145,5},{177,229},{146,8},{178,232},{147,11},{17... | collective-permute-start | bytes 98312 | tf_op jit(solution)/shard_map/ppermute | solution.py:566
  24.8 17.2 %collective-permute-start.8 = (f32[64,128]{1,0:T(8,128)S(1)}, f32[64,128]{1,0:T(8,128)S(1)}, u32[]{:S(2)}, u32[]{:S(2)}) collective-permute-start(f32[64,128]{1,0:T(8,128)S(1)} %get-tuple-element.39), channel_id=1, source_target_pairs={{145,0},{177,224},{146,3},{178,227},{147,6},{179,230},{148,9},{180... | collective-permute-start | bytes 98312 | tf_op jit(solution)/shard_map/ppermute | solution.py:566
  27.9 14.2 %collective-permute-start.9 = (f32[64,128]{1,0:T(8,128)S(1)}, f32[64,128]{1,0:T(8,128)S(1)}, u32[]{:S(2)}, u32[]{:S(2)}) collective-permute-start(f32[64,128]{1,0:T(8,128)S(1)} %get-tuple-element.40), channel_id=1, source_target_pairs={{145,1},{177,225},{146,4},{178,228},{147,7},{179,231},{148,10},{18... | collective-permute-start | bytes 98312 | tf_op jit(solution)/shard_map/ppermute | solution.py:566
  28.5 13.5 %collective-permute-start.10 = (f32[64,128]{1,0:T(8,128)S(1)}, f32[64,128]{1,0:T(8,128)S(1)}, u32[]{:S(2)}, u32[]{:S(2)}) collective-permute-start(f32[64,128]{1,0:T(8,128)S(1)} %get-tuple-element.41), channel_id=1, source_target_pairs={{145,2},{177,226},{146,5},{178,229},{147,8},{179,232},{148,11},{18... | collective-permute-start | bytes 98312 | tf_op jit(solution)/shard_map/ppermute | solution.py:566
  29.2 12.8 %copy-start = (f32[50,24,128]{2,1,0:T(8,128)S(1)}, f32[50,24,128]{2,1,0:T(8,128)}, u32[]{:S(2)}) copy-start(f32[50,24,128]{2,1,0:T(8,128)} %nu.5) | copy-start | bytes 1843204
  29.2 12.8 %copy-start.1 = (f32[2,50,24,128]{3,2,1,0:T(8,128)S(1)}, f32[2,50,24,128]{3,2,1,0:T(8,128)}, u32[]{:S(2)}) copy-start(f32[2,50,24,128]{3,2,1,0:T(8,128)} %kappa.3) | copy-start | bytes 3686404
  29.2 12.8 %copy-start.2 = (f32[50,24,128]{2,1,0:T(8,128)S(1)}, f32[50,24,128]{2,1,0:T(8,128)}, u32[]{:S(2)}) copy-start(f32[50,24,128]{2,1,0:T(8,128)} %a.3) | copy-start | bytes 1843204
  29.2 12.8 %collective-permute-start.11 = (f32[64,128]{1,0:T(8,128)S(1)}, f32[64,128]{1,0:T(8,128)S(1)}, u32[]{:S(2)}, u32[]{:S(2)}) collective-permute-start(f32[64,128]{1,0:T(8,128)S(1)} %get-tuple-element.42.after), channel_id=1, source_target_pairs={{146,2},{178,226},{147,5},{179,229},{148,8},{180,232},{149,11},{18... | collective-permute-start | bytes 98312 | tf_op jit(solution)/shard_map/ppermute | solution.py:566
  30.1 1.7 %copy-start.3 = (f32[2,50,48,128]{3,2,1,0:T(8,128)S(1)}, f32[2,50,48,128]{3,2,1,0:T(8,128)}, u32[]{:S(2)}) copy-start(f32[2,50,48,128]{3,2,1,0:T(8,128)} %pkappa.1) | copy-start | bytes 7372804
  31.7 10.3 %copy-start.11 = (s32[24,128]{1,0:T(8,128)S(1)}, s32[24,128]{1,0:T(8,128)}, u32[]{:S(2)}) copy-start(s32[24,128]{1,0:T(8,128)} %mask.5) | copy-start | bytes 36868
  33.9 10.6 %copy-start.7 = (f32[2,50,8,128]{3,2,1,0:T(8,128)}, f32[2,50,8,128]{3,2,1,0:T(8,128)S(1)}, u32[]{:S(2)}) copy-start(f32[2,50,8,128]{3,2,1,0:T(8,128)S(1)} %get-tuple-element.50.row_k) | copy-start | bytes 1228804
  33.9 10.6 %copy-start.12 = (f32[48,128]{1,0:T(8,128)}, f32[48,128]{1,0:T(8,128)S(1)}, u32[]{:S(2)}) copy-start(f32[48,128]{1,0:T(8,128)S(1)} %get-tuple-element.53.col_r) | copy-start | bytes 73732
  44.5 39.8 %copy-start.5 = (f32[50,24,128]{2,1,0:T(8,128)}, f32[50,24,128]{2,1,0:T(8,128)S(1)}, u32[]{:S(2)}) copy-start(f32[50,24,128]{2,1,0:T(8,128)S(1)} %get-tuple-element.44.a) | copy-start | bytes 1843204
  44.5 14.1 %collective-permute-start.13 = (f32[112,128]{1,0:T(8,128)S(1)}, f32[112,128]{1,0:T(8,128)S(1)}, u32[]{:S(2)}, u32[]{:S(2)}) collective-permute-start(f32[112,128]{1,0:T(8,128)S(1)} %get-tuple-element.49), channel_id=1, source_target_pairs={{32,0},{64,32},{96,64},{128,96},{160,128},{192,160},{224,192},{33,... | collective-permute-start | bytes 172040 | tf_op jit(solution)/shard_map/ppermute | solution.py:571
  48.4 10.2 %collective-permute-start.12 = (f32[112,128]{1,0:T(8,128)S(1)}, f32[112,128]{1,0:T(8,128)S(1)}, u32[]{:S(2)}, u32[]{:S(2)}) collective-permute-start(f32[112,128]{1,0:T(8,128)S(1)} %get-tuple-element.48), channel_id=1, source_target_pairs={{0,128},{1,129},{2,130},{3,131},{4,132},{5,133},{6,134},{7,135},{8... | collective-permute-start | bytes 172040 | tf_op jit(solution)/shard_map/ppermute | solution.py:566
  51.9 6.7 %collective-permute-start.14 = (f32[50,128]{1,0:T(8,128)S(1)}, f32[50,128]{1,0:T(8,128)S(1)}, u32[]{:S(2)}, u32[]{:S(2)}) collective-permute-start(f32[50,128]{1,0:T(8,128)S(1)} %slice.3), channel_id=1, source_target_pairs={{0,32},{1,33},{2,34},{3,35},{4,36},{5,37},{6,38},{7,39},{8,40},{9,... | collective-permute-start | bytes 76808 | tf_op jit(solution)/shard_map/ppermute | solution.py:566
  84.3 6.9 %copy-start.10 = (f32[168,128]{1,0:T(8,128)S(1)}, f32[168,128]{1,0:T(8,128)}, u32[]{:S(2)}) copy-start(f32[168,128]{1,0:T(8,128)} %get-tuple-element.35.pay) | copy-start | bytes 258052
  85.0 14.4 %all-to-all-start.1 = ((f32[8,32,128]{2,1,0:T(8,128)}), f32[8,32,128]{2,1,0:T(8,128)S(1)}, u32[]{:S(2)}, u32[]{:S(2)}) async-start(f32[8,32,128]{2,1,0:T(8,128)} %turn.1), calls=%async_computation.1 | async-start | bytes 262144 | tf_op jit(solution)/shard_map/all_to_all | solution.py:665
  91.3 1.1 %copy-start.6 = (f32[50,24,128]{2,1,0:T(8,128)S(1)}, f32[50,24,128]{2,1,0:T(8,128)}, u32[]{:S(2)}) copy-start(f32[50,24,128]{2,1,0:T(8,128)} %copy-done.5) | copy-start | bytes 1843204
  92.3 1.0 copy-start.8
  99.4 0.7 copy-start.13
